TPU v7x, 256 devices: a whole 4x4x8 slice. The times are simulated.
256 devices in a mesh: dp: 4 (over y), table: 64 (over z, x, core).
Axes of the slice: x: 4, y: 4, z: 8, core: 2. Of those that a mesh axis runs over, the one named last changes fastest.
Arguments:
- table_rows: float32 [24576, 1280], P('table'), may hold values from -1.2 to 1.2
- first_moment: float32 [24576, 1280], P('table'), may hold values from -2 to 2
- second_moment: float32 [24576, 1280], P('table'), may hold values from 0.05 to 5
- grad_rows: bfloat16 [262144, 1280], P(('dp', 'table')), may hold values from -6 to 6
- row_ids: int32 [262144], P(('dp', 'table')), may hold values from 0 to 384, as said below
- next_ids: int32 [262144], P(('dp', 'table')), may hold values from 0 to 384, as said below
Outputs:
- new_table: float32 [24576, 1280], P('table')
- new_first: float32 [24576, 1280], P('table')
- new_second: float32 [24576, 1280], P('table')
- fetched: bfloat16 [262144, 1280], P(('dp', 'table'))
Inputs may be any that keep to these rules, and one draw needn't show every extreme that they name: `row_ids`: each block of 16 slots from one device to one owner holds its live rows first and then empty slots marked 384; every draw has blocks with all 16 slots live; rows may repeat. `next_ids`: same layout as row_ids.
All inputs are finite; a program needn't handle non-finite values.
Results may differ from a plain program's by a relative error of at most 0.001.
Values may be sent and summed in bfloat16 or wider, within the bound.
No kernel may reach another device: no remote copies, remote signals or barrier semaphores. Data moves between devices by JAX's collectives and lax.ppermute only.
A program may use at most 64 MiB of HBM per device.

v0:
```python
import jax
import jax.numpy as jnp
from jax import lax
from jax.sharding import PartitionSpec as P

STEP = 20


def adamw(weights, first, second, grads):
    first_new = 0.9 * first + 0.1 * grads
    second_new = 0.95 * second + 0.05 * grads * grads
    corr_one = 1.0 - 0.9**STEP
    corr_two = 1.0 - 0.95**STEP
    update = first_new / corr_one / (jnp.sqrt(second_new / corr_two) + 1e-08) + 0.01 * weights
    return (weights - 0.1 * update, first_new, second_new)


def local(table_rows, first_moment, second_moment, grad_rows, row_ids, next_ids):
    groups = lax.axis_size("table")
    slots = row_ids.shape[0]
    block = slots // groups
    width = grad_rows.shape[1]
    rows_dev = table_rows.shape[0]
    sent_grads = grad_rows.reshape(groups, block, width)
    sent_ids = row_ids.reshape(groups, block)
    got_grads, got_ids = (
        lax.all_to_all(sent_grads, "table", split_axis=0, concat_axis=0, tiled=True),
        lax.all_to_all(sent_ids, "table", split_axis=0, concat_axis=0, tiled=True),
    )
    flat_ids = got_ids.reshape(slots)
    flat_grads = got_grads.reshape(slots, width)
    selector = (lax.broadcasted_iota(jnp.int32, (rows_dev, slots), 0) == flat_ids[None, :]).astype(
        jnp.bfloat16
    )
    local_sum = jnp.dot(selector, flat_grads, preferred_element_type=jnp.float32)
    summed = lax.psum(local_sum, "dp")
    new_table, new_first, new_second = adamw(table_rows, first_moment, second_moment, summed)
    padded = jnp.concatenate(
        [new_table.astype(jnp.bfloat16), jnp.zeros((1, width), jnp.bfloat16)], 0
    )
    found = jnp.take(
        padded,
        lax.all_to_all(
            next_ids.reshape(groups, block), "table", split_axis=0, concat_axis=0, tiled=True
        ),
        axis=0,
    )
    fetched = lax.all_to_all(found, "table", split_axis=0, concat_axis=0, tiled=True)
    return (new_table, new_first, new_second, fetched.reshape(slots, width))


def solution(mesh):
    return jax.shard_map(
        local,
        mesh=mesh,
        in_specs=(
            P("table", None),
            P("table", None),
            P("table", None),
            P(("dp", "table"), None),
            P(("dp", "table")),
            P(("dp", "table")),
        ),
        out_specs=(P("table", None), P("table", None), P("table", None), P(("dp", "table"), None)),
        check_vma=False,
    )
```

profile of v0, /device:TPU:1, one launch (start us, length us, event | category | flops | bytes accessed | tf_op | source)
XLA Modules:
  0.0 253.5 jit_solution(11222661443661590317)
XLA Ops:
  7.2 0.8 all_to_all.22
  7.9 22.2 %all_to_all.34 = s32[64,1,16]{2,1,0:T(1,128)S(1)} all-to-all(s32[64,1,16]{2,1,0:T(1,128)S(1)} %bitcast.17), channel_id=1, replica_groups=mesh['dp'=4,'table'=64] {'table'}, dimensions={0} | all-to-all | bytes 8192 | tf_op jit(solution)/shard_map/all_to_all | solution.py:28
  30.1 4.8 %all-to-all-start.1 = ((bf16[64,16,1280]{2,1,0:T(8,128)(2,1)}), bf16[64,16,1280]{2,1,0:T(8,128)(2,1)S(1)}, u32[]{:S(2)}, u32[]{:S(2)}) async-start(bf16[64,16,1280]{2,1,0:T(8,128)(2,1)} %bitcast.13), calls=%async_computation.1 | async-start | bytes 5242880 | tf_op jit(solution)/shard_map/all_to_all | solution.py:27
  34.9 0.0 all-reduce.3.cloned.1.call-start
  35.0 0.5 broadcast.41
  35.5 0.7 reduce.3
  36.2 0.1 eq.10
  36.3 60.1 %all-to-all-done.1 = bf16[64,16,1280]{2,1,0:T(8,128)(2,1)S(1)} async-done(((bf16[64,16,1280]{2,1,0:T(8,128)(2,1)}), bf16[64,16,1280]{2,1,0:T(8,128)(2,1)S(1)}, u32[]{:S(2)}, u32[]{:S(2)}) %all-to-all-start.1) | async-done | bytes 2621472 | tf_op jit(solution)/shard_map/all_to_all | solution.py:27
  96.4 0.0 copy-start.1
  96.4 2.5 fusion.1
  98.9 0.0 copy-start
  98.9 0.0 all-reduce.3.cloned.1.call-update
  98.9 0.0 copy-done.1
  98.9 0.1 all_to_all.25
  99.0 15.9 %all_to_all.35 = s32[64,1,16]{2,1,0:T(1,128)S(1)} all-to-all(s32[64,1,16]{2,1,0:T(1,128)S(1)} %bitcast.18), channel_id=1, replica_groups=mesh['dp'=4,'table'=64] {'table'}, dimensions={0} | all-to-all | bytes 8192 | tf_op jit(solution)/shard_map/all_to_all | solution.py:43
  114.9 0.1 reshape.66
  115.0 43.2 %all-reduce.3.cloned.1.call-done = f32[384,1280]{1,0:T(8,128)} async-done(((f32[384,1280]{1,0:T(8,128)}), f32[384,1280]{1,0:T(8,128)}) %all-reduce.3.cloned.1.call-update) | async-done | bytes 1966096 | tf_op jit(solution)/shard_map/psum | solution.py:36
  158.2 0.0 copy-done
  158.2 6.2 %fusion.3 = (bf16[384,1280]{1,0:T(8,128)(2,1)S(1)}, f32[384,1280]{1,0:T(8,128)}, f32[384,1280]{1,0:T(8,128)}, f32[384,1280]{1,0:T(8,128)}) fusion(f32[384,1280]{1,0:T(8,128)S(1)} %copy-done, f32[384,1280]{1,0:T(8,128)} %all-reduce.3.cloned.1.call-done, f32[384,1280]{1,0:T(8,128)} %param.7, f32[384,1280]{1,0:T(8,128)} %param.8), kind=kLoop, calls=%fused_computation.13 | loop fusion | flops 7864320 | bytes 14745600 | tf_op jit(solution)/shard_map/convert_element_type | solution.py:39
  164.4 0.1 concatenate.3
  164.5 5.5 %gather_fusion = bf16[1024,1280]{1,0:T(8,128)(2,1)} fusion(bf16[385,1280]{1,0:T(8,128)(2,1)S(1)} %concatenate.3, s32[1024]{0:T(1024)S(1)} %broadcast_clamp_fusion), kind=kCustom, calls=%fused_computation | custom fusion | bytes 5246976 | tf_op jit(solution)/shard_map/jit(_take)/gather | solution.py:41
  169.9 2.0 broadcast_select_fusion
  172.0 73.2 %all_to_all.36 = bf16[64,16,1280]{2,1,0:T(8,128)(2,1)S(1)} all-to-all(bf16[64,16,1280]{2,1,0:T(8,128)(2,1)S(1)} %broadcast_select_fusion), channel_id=1, replica_groups=mesh['dp'=4,'table'=64] {'table'}, dimensions={0} | all-to-all | bytes 5242880 | tf_op jit(solution)/shard_map/all_to_all | solution.py:48
  245.2 1.5 copy.14
  (3 shorter events, 0.0 us)
Async XLA Ops:
  30.1 66.3 %all-to-all-start.1 = ((bf16[64,16,1280]{2,1,0:T(8,128)(2,1)}), bf16[64,16,1280]{2,1,0:T(8,128)(2,1)S(1)}, u32[]{:S(2)}, u32[]{:S(2)}) async-start(bf16[64,16,1280]{2,1,0:T(8,128)(2,1)} %bitcast.13), calls=%async_computation.1 | async-start | bytes 5242880 | tf_op jit(solution)/shard_map/all_to_all | solution.py:27
  34.9 123.3 %all-reduce.3.cloned.1.call-start = ((), (), s32[]{:S(2)}) async-start(), calls=%async_computation.4 | async-start | bytes 3932160 | tf_op jit(solution)/shard_map/psum | solution.py:36
  96.4 2.5 copy-start.1
  98.9 59.3 %copy-start = (f32[384,1280]{1,0:T(8,128)S(1)}, f32[384,1280]{1,0:T(8,128)}, u32[]{:S(2)}) copy-start(f32[384,1280]{1,0:T(8,128)} %param.6) | copy-start | bytes 5898244
Sparse Core Ops, SparseCore 0:
  99.1 59.0 all-reduce.2
where the time goes:
time: 254 us
  blocking collectives  111 us (44%)
  waiting for transfers between devices  103 us (41%)
  between operations  14.1 us (6%)
  other arithmetic  9.03 us (4%)
  local copies, waits for them, and re-layouts  8.52 us (3%)
  starting transfers between devices  4.87 us (2%)
    all_to_all x1, blocking collectives, local(): lax.all_to_all(found, 'table', split_axis=0, concat_axis=0, tiled=True)  73.2 us
    all_to_all x1, waiting for transfers between devices, local(): lax.all_to_all(sent_grads, 'table', split_axis=0, concat_axis=0, tiled=True)  60.1 us
    psum x1, waiting for transfers between devices, local(): summed = lax.psum(local_sum, 'dp')  43.2 us
    all_to_all x1, blocking collectives, local(): lax.all_to_all(sent_ids, 'table', split_axis=0, concat_axis=0, tiled=True)  22.2 us
    all_to_all x1, blocking collectives, local(): lax.all_to_all(next_ids.reshape(groups, block), 'table', split_axis=0, co...  15.9 us
    convert_element_type x1, other arithmetic, local(): new_table.astype(jnp.bfloat16)  6.23 us
    gather x1, local copies, waits for them, and re-layouts, local(): jnp.take(padded, lax.all_to_all(next_ids.reshape(groups, block), 'table',...  5.46 us
  transfers between devices with their start and end apart: 2, of which 2 were waited for; matrix products, arithmetic and copies ran while one was open for 1% of the time, Pallas kernels for 0%

commit v1 on v0

v1 whole, which is shorter than its diff:
```python
import jax
import jax.numpy as jnp
from jax import lax
from jax.experimental import pallas as pl
from jax.experimental.pallas import tpu as pltpu
from jax.sharding import Mesh, PartitionSpec as P

STEP = 20
LANES = 128
CAP = 16
BF = jnp.bfloat16
F32 = jnp.float32
F16 = jnp.float16
SLAB = ("y", "x", "c")
GROUP = 32
NZ = 8
NY = 4
XC = 8
ROWS = 384
HALF = 192
QROWS = 960
SENT = 336
BACK = 320


def adamw(weights, first, second, grads):
    first_new = 0.9 * first + 0.1 * grads
    second_new = 0.95 * second + 0.05 * grads * grads
    corr_one = 1.0 - 0.9**STEP
    corr_two = 1.0 - 0.95**STEP
    update = first_new / corr_one / (jnp.sqrt(second_new / corr_two) + 1e-08) + 0.01 * weights
    return (weights - 0.1 * update, first_new, second_new)


def low_lanes(shape):
    return lax.broadcasted_iota(jnp.int32, shape, len(shape) - 1) < 64


def pair(a, b, upper):
    low = low_lanes(a.shape)
    axis = a.ndim - 1
    if isinstance(upper, bool):
        return jnp.where(low, pltpu.roll(a, 64, axis), b) if upper else jnp.where(low, a, pltpu.roll(b, 64, axis))
    return jnp.where(
        upper,
        jnp.where(low, pltpu.roll(a, 64, axis), b),
        jnp.where(low, a, pltpu.roll(b, 64, axis)),
    )


def params(mib):
    return pltpu.CompilerParams(vmem_limit_bytes=mib * 1024 * 1024)


def hbm(x):
    return pltpu.with_memory_space_constraint(x, pltpu.HBM)


def tile_iota(axis):
    return lax.broadcasted_iota(jnp.int32, (8, LANES), axis)


def diagonal(rolled, shift):
    moved = pltpu.roll(rolled, (NZ * LANES - CAP * shift) % LANES, 1)
    kept = jnp.where(tile_iota(1) // CAP == tile_iota(0), moved, 0.0)
    return jnp.sum(kept, axis=0, keepdims=True)


def row_roll(x):
    return pltpu.roll(x, 0, 1, stride=CAP, stride_axis=0)


PACK_STEP = 2


def pack_kernel(g_ref, row_ref, next_ref, o_ref):
    ids = [row_roll(r[...].astype(F32)) for r in (row_ref, next_ref)]
    sub = lax.broadcasted_iota(jnp.int32, (CAP, LANES), 0)
    for u in range(PACK_STEP):
        for y in range(NY):
            for z in range(NZ):
                o_ref[y, u, pl.ds(z * CAP, CAP), :] = g_ref[z, u, :, pl.ds(y * LANES, LANES)]
                o_ref[y, u, pl.ds(128 + z * CAP, CAP), :] = g_ref[z, u, :, pl.ds(512 + y * LANES, LANES)]
            for k in range(NZ // 2):
                cols = pl.ds(1024 + (y // 2) * LANES, LANES)
                a = g_ref[2 * k, u, :, cols].astype(F32)
                b = g_ref[2 * k + 1, u, :, cols].astype(F32)
                o_ref[y, u, pl.ds(256 + k * CAP, CAP), :] = pair(a, b, y % 2 == 1).astype(BF)
        head = jnp.zeros((CAP, LANES), F32)
        for t in range(2):
            mine = diagonal(ids[t], pl.program_id(0) * PACK_STEP + u)
            upper = jnp.floor(mine * (1.0 / 16.0))
            head = jnp.where(sub == 2 * t, upper, head)
            head = jnp.where(sub == 2 * t + 1, mine - 16.0 * upper, head)
        for y in range(NY):
            o_ref[y, u, pl.ds(BACK, CAP), :] = head.astype(BF)


def pack(grad_rows, row_ids, next_ids):
    whole = pl.BlockSpec((8, LANES), lambda i: (0, 0))
    return pl.pallas_call(
        pack_kernel,
        grid=(XC // PACK_STEP,),
        in_specs=[pl.BlockSpec((NZ, PACK_STEP, CAP, 1280), lambda i: (0, i, 0, 0)), whole, whole],
        out_specs=pl.BlockSpec((NY, PACK_STEP, SENT, LANES), lambda i: (0, i, 0, 0)),
        out_shape=pltpu.HBM((NY, XC, SENT, LANES), BF),
        compiler_params=params(12),
        name="pack",
    )(
        hbm(grad_rows.reshape(NZ, XC, CAP, 1280)),
        hbm(row_ids.reshape(8, LANES)),
        hbm(next_ids.reshape(8, LANES)),
    )


def reduce_kernel(z_ref, got_ref, o_ref, next_ref, ids_ref):
    sub = tile_iota(0)
    for q in range(GROUP // 8):
        tiles = [jnp.zeros((8, LANES), F32)] * 2
        for j in range(8):
            head = got_ref[8 * q + j, pl.ds(BACK, CAP), :].astype(F32)
            for t in range(2):
                mine = head[2 * t : 2 * t + 1] * 16.0 + head[2 * t + 1 : 2 * t + 2]
                tiles[t] = jnp.where(sub == j, mine, tiles[t])
        for t, ref in ((0, ids_ref), (1, next_ref)):
            rolled = row_roll(tiles[t])
            for k in range(NZ):
                ref[pl.ds(k, 1), pl.ds(q * LANES, LANES)] = diagonal(rolled, z_ref[0] + k).astype(jnp.int32)
    rows = lax.broadcasted_iota(jnp.int32, (ROWS, GROUP * CAP), 0)
    for k in range(NZ):
        z = (z_ref[0] + k) % NZ
        pick = jnp.where(rows == ids_ref[pl.ds(k, 1), :], 1.0, 0.0).astype(BF)
        starts = (z * CAP, 128 + z * CAP, 256 + (z // 2) * CAP)
        slots = jnp.concatenate(
            [got_ref[:, pl.ds(pl.multiple_of(at, CAP), CAP), :].reshape(GROUP * CAP, LANES) for at in starts], axis=1
        )
        total = jnp.dot(pick, slots, preferred_element_type=F32)
        o_ref[k, pl.ds(0, ROWS), :] = total[:, :128]
        o_ref[k, pl.ds(ROWS, ROWS), :] = total[:, 128:256]
        last = total[:, 256:]
        o_ref[k, pl.ds(2 * ROWS, HALF), :] = pair(last[:HALF], last[HALF:], z % 2 == 1)


def partial_sums(z, got):
    vmem = pl.BlockSpec(memory_space=pltpu.VMEM)
    smem = pl.BlockSpec(memory_space=pltpu.SMEM)
    return pl.pallas_call(
        reduce_kernel,
        in_specs=[smem, vmem],
        out_specs=[vmem, vmem],
        out_shape=[
            jax.ShapeDtypeStruct((NZ, QROWS, LANES), F32),
            jax.ShapeDtypeStruct((NZ, GROUP * CAP), jnp.int32),
        ],
        scratch_shapes=[pltpu.VMEM((NZ, GROUP * CAP), jnp.int32)],
        compiler_params=params(16),
        name="partial_sums",
    )(z, got)


def quarter_kernel(y_ref, *refs):
    odd = y_ref[0] % 2 == 1
    for i in range(3):
        a, b, c = (r[...] for r in refs[3 * i : 3 * i + 3])
        o_ref = refs[9 + i]
        o_ref[pl.ds(0, ROWS), :] = a
        o_ref[pl.ds(ROWS, ROWS), :] = b
        o_ref[pl.ds(2 * ROWS, HALF), :] = pair(c[:HALF], c[HALF:], odd)


def quarters(y, *arrays):
    spec = [
        pl.BlockSpec((ROWS, LANES), lambda i, s: (0, s[0])),
        pl.BlockSpec((ROWS, LANES), lambda i, s: (0, NY + s[0])),
        pl.BlockSpec((ROWS, LANES), lambda i, s: (0, 2 * NY + s[0] // 2)),
    ]
    return pl.pallas_call(
        quarter_kernel,
        grid_spec=pltpu.PrefetchScalarGridSpec(
            num_scalar_prefetch=1,
            grid=(1,),
            in_specs=spec * 3,
            out_specs=[pl.BlockSpec((QROWS, LANES), lambda i, s: (0, 0))] * 3,
        ),
        out_shape=[jax.ShapeDtypeStruct((QROWS, LANES), F32)] * 3,
        compiler_params=params(12),
        cost_estimate=pl.CostEstimate(flops=1_000_000, bytes_accessed=3_000_000, transcendentals=0),
        name="quarters",
    )(y, *[hbm(t) for t in arrays for _ in range(3)])


def fetch_kernel(z_ref, ids_ref, *refs):
    tables, o_ref = refs[:NZ], refs[NZ]
    low = low_lanes((GROUP, CAP, LANES))
    rows = lax.broadcasted_iota(jnp.int32, (GROUP * CAP, ROWS), 1).astype(F32)
    columns = jnp.transpose(ids_ref[...].astype(F32))
    for k in range(NZ):
        z = (z_ref[0] + k) % NZ
        pick = jnp.where(rows == columns[:, k : k + 1], 1.0, 0.0).astype(BF)
        table = tables[k]
        last = table[pl.ds(2 * ROWS, HALF), :].astype(F32)
        moved = pltpu.roll(last, 64, 1)
        odd = z % 2 == 1
        lower = jnp.where(odd, moved, last).astype(BF)
        higher = jnp.where(odd, last, moved).astype(BF)
        wide = jnp.concatenate(
            [table[pl.ds(0, ROWS), :], table[pl.ds(ROWS, ROWS), :], jnp.concatenate([lower, higher], axis=0)],
            axis=1,
        )
        found = jnp.dot(pick, wide, preferred_element_type=F32)
        found = found.astype(BF).reshape(GROUP, CAP, 3 * LANES)
        at = pl.multiple_of(z * CAP, CAP)
        o_ref[:, pl.ds(at, CAP), :] = found[:, :, :128]
        o_ref[:, pl.ds(at + 128, CAP), :] = found[:, :, 128:256]
        both = pl.ds(pl.multiple_of(256 + (z // 2) * CAP, CAP), CAP)
        old = o_ref[:, both, :]
        o_ref[:, both, :] = jnp.where(low == odd, old, found[:, :, 256:])


def fetch(z, ids, tables):
    vmem = pl.BlockSpec(memory_space=pltpu.VMEM)
    return pl.pallas_call(
        fetch_kernel,
        in_specs=[pl.BlockSpec(memory_space=pltpu.SMEM)] + [vmem] * 9,
        out_specs=vmem,
        out_shape=jax.ShapeDtypeStruct((GROUP, BACK, LANES), BF),
        compiler_params=params(16),
        name="fetch",
    )(z, ids, *tables)


UNPACK_STEP = 2


def unpack_kernel(g_ref, o_ref):
    for u in range(UNPACK_STEP):
        for y in range(NY):
            for z in range(NZ):
                o_ref[z, u, :, pl.ds(y * LANES, LANES)] = g_ref[y, u, pl.ds(z * CAP, CAP), :]
                o_ref[z, u, :, pl.ds(512 + y * LANES, LANES)] = g_ref[y, u, pl.ds(128 + z * CAP, CAP), :]
        for t in range(2):
            for k in range(NZ // 2):
                a = g_ref[2 * t, u, pl.ds(256 + k * CAP, CAP), :].astype(F32)
                b = g_ref[2 * t + 1, u, pl.ds(256 + k * CAP, CAP), :].astype(F32)
                cols = pl.ds(1024 + t * LANES, LANES)
                o_ref[2 * k, u, :, cols] = pair(a, b, False).astype(BF)
                o_ref[2 * k + 1, u, :, cols] = pair(a, b, True).astype(BF)


def unpack(back):
    out = pl.pallas_call(
        unpack_kernel,
        grid=(XC // UNPACK_STEP,),
        in_specs=[pl.BlockSpec((NY, UNPACK_STEP, BACK, LANES), lambda i: (0, i, 0, 0))],
        out_specs=pl.BlockSpec((NZ, UNPACK_STEP, CAP, 1280), lambda i: (0, i, 0, 0)),
        out_shape=pltpu.HBM((NZ, XC, CAP, 1280), BF),
        compiler_params=params(12),
        name="unpack",
    )(back.reshape(NY, XC, BACK, LANES))
    return out.reshape(NZ * XC * CAP, 1280)


FULL_STEP = 48


def full_kernel(y_ref, *refs):
    g_refs, (w_ref, m_ref, v_ref, ow_ref, om_ref, ov_ref, all_ref) = refs[:NY], refs[NY:]
    for d in range(NY):
        all_ref[(y_ref[0] + d) % NY] = g_refs[d][...]
    for half in range(2):
        for t in range(10):
            if t < 8:
                grads = all_ref[t % NY, 2 * (t // NY) + half]
            else:
                grads = pair(all_ref[2 * (t - 8), 4], all_ref[2 * (t - 8) + 1, 4], half == 1)
            cols = pl.ds(t * LANES, LANES)
            w, m, v = adamw(w_ref[half, :, cols], m_ref[half, :, cols], v_ref[half, :, cols], grads)
            ow_ref[half, :, cols] = w
            om_ref[half, :, cols] = m
            ov_ref[half, :, cols] = v


def full_rows(y, grads, table_rows, first_moment, second_moment):
    wide = pl.BlockSpec((2, FULL_STEP, 1280), lambda i, s: (0, i, 0))
    part = pl.BlockSpec((5, FULL_STEP, LANES), lambda i, s: (0, i, 0))
    outs = pl.pallas_call(
        full_kernel,
        grid_spec=pltpu.PrefetchScalarGridSpec(
            num_scalar_prefetch=1,
            grid=(HALF // FULL_STEP,),
            in_specs=[part] * NY + [wide] * 3,
            out_specs=[wide] * 3,
            scratch_shapes=[pltpu.VMEM((NY, 5, FULL_STEP, LANES), F32)],
        ),
        out_shape=[pltpu.HBM((2, HALF, 1280), F32)] * 3,
        compiler_params=params(12),
        cost_estimate=pl.CostEstimate(flops=10_000_000, bytes_accessed=14_000_000, transcendentals=0),
        name="full_rows",
    )(
        y,
        *[g.reshape(5, HALF, LANES) for g in grads],
        *[hbm(t.reshape(2, HALF, 1280)) for t in (table_rows, first_moment, second_moment)],
    )
    return tuple(t.reshape(ROWS, 1280) for t in outs)


def along(value, axis, size, step):
    return lax.ppermute(value, axis, [(i, (i + step) % size) for i in range(size)])


def send_root(x, step):
    root = jnp.sqrt(jnp.abs(x)) * 256.0
    got = along(jnp.where(x < 0.0, -root, root).astype(F16), "z", NZ, step).astype(F32)
    return got * jnp.abs(got) * (1.0 / 65536.0)


def reduce_z(part):
    up = send_root(part[4], 1)
    down = send_root(part[5], -1)
    for k in (3, 2):
        up = send_root(part[k] + up, 1)
        down = send_root(part[9 - k] + down, -1)
    return part[0] + down + send_root(part[1] + up, 1)


def gather_z(own):
    got = {0: own}
    up = down = own
    for k in (1, 2, 3):
        up, down = along(up, "z", NZ, 1), along(down, "z", NZ, -1)
        got[NZ - k], got[k] = up, down
    got[4] = along(up, "z", NZ, 1)
    return [got[k] for k in range(NZ)]


def gather_y(own):
    return [own] + [along(own, "y", NY, -d) for d in range(1, NY)]


def local(table_rows, first_moment, second_moment, grad_rows, row_ids, next_ids):
    z = lax.axis_index("z").astype(jnp.int32)[None]
    y = lax.axis_index("y").astype(jnp.int32)[None]
    sent = pack(grad_rows, row_ids, next_ids)
    got = lax.all_to_all(sent.reshape(GROUP, SENT, LANES), SLAB, split_axis=0, concat_axis=0, tiled=True)
    mine = quarters(y, table_rows, first_moment, second_moment)
    part, wanted = partial_sums(z, got)
    summed = reduce_z(part)
    own = adamw(*mine, summed)[0].astype(BF)
    tables, grads = lax.optimization_barrier((gather_z(own), gather_y(summed)))
    found = fetch(z, wanted, tables)
    back = lax.all_to_all(found, SLAB, split_axis=0, concat_axis=0, tiled=True)
    outs = full_rows(y, grads, table_rows, first_moment, second_moment)
    return (*outs, unpack(back))


def solution(mesh):
    fine = Mesh(mesh.devices.reshape(NY, NZ, 4, 2), ("y", "z", "x", "c"))
    owner = ("z", "x", "c")
    every = ("y", "z", "x", "c")
    return jax.shard_map(
        local,
        mesh=fine,
        in_specs=(P(owner, None), P(owner, None), P(owner, None), P(every, None), P(every), P(every)),
        out_specs=(P(owner, None), P(owner, None), P(owner, None), P(every, None)),
        check_vma=False,
    )
```

time: 254 us -> 188 us (0.74)
  blocking collectives: 111 us -> 0 us
  starting transfers between devices: 4.87 us -> 48 us
  Pallas kernels: 0 us -> 21.3 us
  between operations: 14.1 us -> 0.79 us
  other arithmetic: 9.03 us -> 3.61 us
  waiting for transfers between devices: 103 us -> 108 us
  local copies, waits for them, and re-layouts: 8.52 us -> 5.42 us
    all_to_all x3 -> x0, blocking collectives: 111 us -> none  [the longest x1 73.2 us: local(): lax.all_to_all(found, 'table', split_axis=0, concat_axis=0, tiled=True)]
    ppermute x0 -> x17, waiting for transfers between devices: none -> 48.9 us  [along(): lax.ppermute(value, axis, [(i, (i + step) % size) for i in range(size)])]
    psum x1 -> x0, waiting for transfers between devices: 43.2 us -> none  [local(): summed = lax.psum(local_sum, 'dp')]
    ppermute x0 -> x17, starting transfers between devices: none -> 22.1 us  [along(): lax.ppermute(value, axis, [(i, (i + step) % size) for i in range(size)])]
    pallas_call x0 -> x6, Pallas kernels: none -> 21.3 us  [the longest x1 6.3 us: full_rows(): pl.pallas_call(full_kernel, grid_spec=pltpu.PrefetchScalarGridSpec(num_sc...]
    all_to_all x1 -> x2, starting transfers between devices: 4.83 us -> 25.9 us  [the longest x1 17.3 us: local(): back = lax.all_to_all(found, SLAB, split_axis=0, concat_axis=0, tiled=True)]
    gather x1 -> x0, local copies, waits for them, and re-layouts: 5.46 us -> none  [local(): jnp.take(padded, lax.all_to_all(next_ids.reshape(groups, block), 'table',...]
    unnamed x5 -> x14, local copies, waits for them, and re-layouts: 1.5 us -> 5.42 us
  transfers between devices with their start and end apart: 2 -> 19, of which waited for: 2 -> 14; matrix products, arithmetic and copies ran while one was open for 1% -> 0% of each run, Pallas kernels for 0% -> 4%
where the time goes in v1:
time: 188 us; the launch traced here: 187 us
  waiting for transfers between devices  108 us (57%)
  starting transfers between devices  48 us (26%)
  Pallas kernels  21.3 us (11%)
  local copies, waits for them, and re-layouts  5.42 us (3%)
  other arithmetic  3.61 us (2%)
    ppermute x17, waiting for transfers between devices, along(): lax.ppermute(value, axis, [(i, (i + step) % size) for i in range(size)])  48.9 us
    all_to_all x1, waiting for transfers between devices, local(): lax.all_to_all(sent.reshape(GROUP, SENT, LANES), SLAB, split_axis=0, conc...  35 us
    all_to_all x1, waiting for transfers between devices, local(): back = lax.all_to_all(found, SLAB, split_axis=0, concat_axis=0, tiled=True)  24.2 us
    ppermute x17, starting transfers between devices, along(): lax.ppermute(value, axis, [(i, (i + step) % size) for i in range(size)])  22.1 us
    all_to_all x1, starting transfers between devices, local(): back = lax.all_to_all(found, SLAB, split_axis=0, concat_axis=0, tiled=True)  17.3 us
    all_to_all x1, starting transfers between devices, local(): lax.all_to_all(sent.reshape(GROUP, SENT, LANES), SLAB, split_axis=0, conc...  8.59 us
    pallas_call x1, Pallas kernels, full_rows(): pl.pallas_call(full_kernel, grid_spec=pltpu.PrefetchScalarGridSpec(num_sc...  6.3 us
    unnamed x14, local copies, waits for them, and re-layouts  5.42 us
  transfers between devices with their start and end apart: 19, of which 14 were waited for; matrix products, arithmetic and copies ran while one was open for 0% of the time, Pallas kernels for 4%

profile of v1, /device:TPU:1, one launch (start us, length us, event | category | flops | bytes accessed | tf_op | source)
XLA Modules:
  0.0 187.1 jit_solution(5998836675022991709)
XLA Ops:
  0.6 4.5 %pack.1 = bf16[4,8,336,128]{3,2,1,0:T(8,128)(2,1)} custom-call(bf16[8,8,16,1280]{3,2,1,0:T(8,128)(2,1)} %bitcast.58, s32[8,128]{1,0:T(8,128)} %bitcast.60, s32[8,128]{1,0:T(8,128)} %bitcast.61), custom_call_target="tpu_custom_call" | custom-call | tf_op jit(solution)/shard_map/pack/pallas_call | solution.py:101
  5.1 8.6 %all-to-all-start = ((bf16[32,336,128]{2,1,0:T(8,128)(2,1)}), bf16[32,336,128]{2,1,0:T(8,128)(2,1)S(1)}, u32[]{:S(2)}, u32[]{:S(2)}) async-start(bf16[32,336,128]{2,1,0:T(8,128)(2,1)} %bitcast.57), calls=%async_computation | async-start | bytes 5505024 | tf_op jit(solution)/shard_map/all_to_all | solution.py:344
  13.7 35.0 %all-to-all-done.got_ref = bf16[32,336,128]{2,1,0:T(8,128)(2,1)S(1)} async-done(((bf16[32,336,128]{2,1,0:T(8,128)(2,1)}), bf16[32,336,128]{2,1,0:T(8,128)(2,1)S(1)}, u32[]{:S(2)}, u32[]{:S(2)}) %all-to-all-start) | async-done | bytes 2752544 | tf_op jit(solution)/shard_map/all_to_all | solution.py:344
  48.7 2.0 %partial_sums.1 = (f32[8,960,128]{2,1,0:T(8,128)S(1)}, s32[8,512]{1,0:T(8,128)S(1)}) custom-call(s32[1]{0:T(128)} %bitcast.1.z_ref, bf16[32,336,128]{2,1,0:T(8,128)(2,1)S(1)} %all-to-all-done.got_ref), custom_call_target="tpu_custom_call" | custom-call | tf_op jit(solution)/shard_map/partial_sums/pallas_call | solution.py:147
  50.7 0.2 fusion
  51.0 5.7 %collective-permute-start = (f16[960,128]{1,0:T(8,128)(2,1)S(1)}, f16[960,128]{1,0:T(8,128)(2,1)S(1)}, u32[]{:S(2)}, u32[]{:S(2)}) collective-permute-start(f16[960,128]{1,0:T(8,128)(2,1)S(1)} %fusion), channel_id=1, source_target_pairs={{0,56},{8,0},{16,8},{24,16},{32,24},{40,32},{48,40},{56,48},{1,57}... | collective-permute-start | bytes 737288 | tf_op jit(solution)/shard_map/ppermute | solution.py:308
  56.6 3.1 %collective-permute-done = f16[960,128]{1,0:T(8,128)(2,1)S(1)} collective-permute-done((f16[960,128]{1,0:T(8,128)(2,1)S(1)}, f16[960,128]{1,0:T(8,128)(2,1)S(1)}, u32[]{:S(2)}, u32[]{:S(2)}) %collective-permute-start) | collective-permute-done | bytes 245792 | tf_op jit(solution)/shard_map/ppermute | solution.py:308
  59.8 0.3 fusion.3
  60.1 3.2 %collective-permute-start.1 = (f16[960,128]{1,0:T(8,128)(2,1)S(1)}, f16[960,128]{1,0:T(8,128)(2,1)S(1)}, u32[]{:S(2)}, u32[]{:S(2)}) collective-permute-start(f16[960,128]{1,0:T(8,128)(2,1)S(1)} %fusion.3), channel_id=1, source_target_pairs={{0,56},{8,0},{16,8},{24,16},{32,24},{40,32},{48,40},{56,48},{1,57}... | collective-permute-start | bytes 737288 | tf_op jit(solution)/shard_map/ppermute | solution.py:308
  63.3 3.1 %collective-permute-done.1 = f16[960,128]{1,0:T(8,128)(2,1)S(1)} collective-permute-done((f16[960,128]{1,0:T(8,128)(2,1)S(1)}, f16[960,128]{1,0:T(8,128)(2,1)S(1)}, u32[]{:S(2)}, u32[]{:S(2)}) %collective-permute-start.1) | collective-permute-done | bytes 245792 | tf_op jit(solution)/shard_map/ppermute | solution.py:308
  66.4 0.5 fusion.6
  67.0 0.1 collective-permute-start.3
  67.0 6.7 %collective-permute-done.3 = f16[960,128]{1,0:T(8,128)(2,1)S(1)} collective-permute-done((f16[960,128]{1,0:T(8,128)(2,1)S(1)}, f16[960,128]{1,0:T(8,128)(2,1)S(1)}, u32[]{:S(2)}, u32[]{:S(2)}) %collective-permute-start.3) | collective-permute-done | bytes 245792 | tf_op jit(solution)/shard_map/ppermute | solution.py:308
  73.7 0.3 fusion.13
  74.0 0.1 collective-permute-start.4
  74.1 7.4 %collective-permute-done.4 = f16[960,128]{1,0:T(8,128)(2,1)S(1)} collective-permute-done((f16[960,128]{1,0:T(8,128)(2,1)S(1)}, f16[960,128]{1,0:T(8,128)(2,1)S(1)}, u32[]{:S(2)}, u32[]{:S(2)}) %collective-permute-start.4) | collective-permute-done | bytes 245792 | tf_op jit(solution)/shard_map/ppermute | solution.py:308
  81.6 0.3 fusion.16
  81.9 0.1 collective-permute-start.5
  82.0 2.7 %collective-permute-start.2 = (f16[960,128]{1,0:T(8,128)(2,1)S(1)}, f16[960,128]{1,0:T(8,128)(2,1)S(1)}, u32[]{:S(2)}, u32[]{:S(2)}) collective-permute-start(f16[960,128]{1,0:T(8,128)(2,1)S(1)} %get-tuple-element.46), channel_id=1, source_target_pairs={{0,56},{8,0},{16,8},{24,16},{32,24},{40,32},{48,40},{56,48},{1,57}... | collective-permute-start | bytes 737288 | tf_op jit(solution)/shard_map/ppermute | solution.py:308
  84.6 6.3 %collective-permute-done.5 = f16[960,128]{1,0:T(8,128)(2,1)S(1)} collective-permute-done((f16[960,128]{1,0:T(8,128)(2,1)S(1)}, f16[960,128]{1,0:T(8,128)(2,1)S(1)}, u32[]{:S(2)}, u32[]{:S(2)}) %collective-permute-start.5) | collective-permute-done | bytes 245792 | tf_op jit(solution)/shard_map/ppermute | solution.py:308
  90.9 0.3 fusion.19
  91.2 0.1 collective-permute-start.6
  91.3 1.8 quarters.1
  93.2 6.5 %collective-permute-done.6 = f16[960,128]{1,0:T(8,128)(2,1)S(1)} collective-permute-done((f16[960,128]{1,0:T(8,128)(2,1)S(1)}, f16[960,128]{1,0:T(8,128)(2,1)S(1)}, u32[]{:S(2)}, u32[]{:S(2)}) %collective-permute-start.6) | collective-permute-done | bytes 245792 | tf_op jit(solution)/shard_map/ppermute | solution.py:308
  99.7 1.6 subtract_convert_fusion
  101.3 0.1 collective-permute-start.10
  101.4 2.7 %collective-permute-start.7 = (bf16[960,128]{1,0:T(8,128)(2,1)S(1)}, bf16[960,128]{1,0:T(8,128)(2,1)S(1)}, u32[]{:S(2)}, u32[]{:S(2)}) collective-permute-start(bf16[960,128]{1,0:T(8,128)(2,1)S(1)} %get-tuple-element.36.refs_0_), channel_id=1, source_target_pairs={{0,56},{8,0},{16,8},{24,16},{32,24},{40,32},{48,40},{56,48},{1,57}... | collective-permute-start | bytes 737288 | tf_op jit(solution)/shard_map/ppermute | solution.py:308
  104.0 6.2 %collective-permute-done.10.refs_7_ = bf16[960,128]{1,0:T(8,128)(2,1)S(1)} collective-permute-done((bf16[960,128]{1,0:T(8,128)(2,1)S(1)}, bf16[960,128]{1,0:T(8,128)(2,1)S(1)}, u32[]{:S(2)}, u32[]{:S(2)}) %collective-permute-start.10) | collective-permute-done | bytes 245792 | tf_op jit(solution)/shard_map/ppermute | solution.py:308
  110.3 1.5 collective-permute-start.16
  111.7 2.7 %collective-permute-start.8 = (bf16[960,128]{1,0:T(8,128)(2,1)S(1)}, bf16[960,128]{1,0:T(8,128)(2,1)S(1)}, u32[]{:S(2)}, u32[]{:S(2)}) collective-permute-start(bf16[960,128]{1,0:T(8,128)(2,1)S(1)} %collective-permute-done.7.refs_1_), channel_id=1, source_target_pairs={{0,56},{8,0},{16,8},{24,16},{32,24},{40,32},{48,40},{56,48},{1,57}... | collective-permute-start | bytes 737288 | tf_op jit(solution)/shard_map/ppermute | solution.py:308
  114.4 2.1 %collective-permute-done.11.refs_6_ = bf16[960,128]{1,0:T(8,128)(2,1)S(1)} collective-permute-done((bf16[960,128]{1,0:T(8,128)(2,1)S(1)}, bf16[960,128]{1,0:T(8,128)(2,1)S(1)}, u32[]{:S(2)}, u32[]{:S(2)}) %collective-permute-start.11) | collective-permute-done | bytes 245792 | tf_op jit(solution)/shard_map/ppermute | solution.py:308
  116.5 1.9 %collective-permute-done.8.refs_2_ = bf16[960,128]{1,0:T(8,128)(2,1)S(1)} collective-permute-done((bf16[960,128]{1,0:T(8,128)(2,1)S(1)}, bf16[960,128]{1,0:T(8,128)(2,1)S(1)}, u32[]{:S(2)}, u32[]{:S(2)}) %collective-permute-start.8) | collective-permute-done | bytes 245792 | tf_op jit(solution)/shard_map/ppermute | solution.py:308
  118.4 3.4 %collective-permute-start.9 = (bf16[960,128]{1,0:T(8,128)(2,1)S(1)}, bf16[960,128]{1,0:T(8,128)(2,1)S(1)}, u32[]{:S(2)}, u32[]{:S(2)}) collective-permute-start(bf16[960,128]{1,0:T(8,128)(2,1)S(1)} %collective-permute-done.8.refs_2_), channel_id=1, source_target_pairs={{0,56},{8,0},{16,8},{24,16},{32,24},{40,32},{48,40},{56,48},{1,57}... | collective-permute-start | bytes 737288 | tf_op jit(solution)/shard_map/ppermute | solution.py:308
  121.8 0.9 collective-permute-done.12.refs_5_
  122.8 0.8 copy-done.1
  123.5 0.8 copy-done.3
  124.3 0.9 collective-permute-done.16
  125.2 0.8 copy-done.5
  126.0 3.7 %collective-permute-done.13.refs_4_ = bf16[960,128]{1,0:T(8,128)(2,1)S(1)} collective-permute-done((bf16[960,128]{1,0:T(8,128)(2,1)S(1)}, bf16[960,128]{1,0:T(8,128)(2,1)S(1)}, u32[]{:S(2)}, u32[]{:S(2)}) %collective-permute-start.13) | collective-permute-done | bytes 245792 | tf_op jit(solution)/shard_map/ppermute | solution.py:308
  129.7 4.3 %fetch.1 = bf16[32,320,128]{2,1,0:T(8,128)(2,1)} custom-call(s32[1]{0:T(128)} %bitcast.1.z_ref, s32[8,512]{1,0:T(8,128)S(1)} %get-tuple-element.35.ids_ref, bf16[960,128]{1,0:T(8,128)(2,1)S(1)} %get-tuple-element.36.refs_0_, bf16[960,128]{1,0:T(8,128)(2,1)S(1)} %collective-permute-done.7.refs_1_, bf16[960,128]{1,0:T(8,128)(2,1)S(1)} %collective-permute-done.8.refs_2_, ...), custom_call_target="tpu_custom_call" | custom-call | tf_op jit(solution)/shard_map/fetch/pallas_call | solution.py:222
  134.0 17.3 %all-to-all-start.1 = ((bf16[32,320,128]{2,1,0:T(8,128)(2,1)}), bf16[32,320,128]{2,1,0:T(8,128)(2,1)S(1)}, u32[]{:S(2)}, u32[]{:S(2)}) async-start(bf16[32,320,128]{2,1,0:T(8,128)(2,1)} %fetch.1), calls=%async_computation.1 | async-start | bytes 5242880 | tf_op jit(solution)/shard_map/all_to_all | solution.py:351
  151.3 0.0 copy-start.2
  151.3 1.0 copy-done.2
  152.3 1.0 copy-done.4
  153.3 1.0 copy-done.6
  154.4 6.3 %full_rows.1 = (f32[2,192,1280]{2,1,0:T(8,128)}, f32[2,192,1280]{2,1,0:T(8,128)}, f32[2,192,1280]{2,1,0:T(8,128)}) custom-call(s32[1]{0:T(128)} %bitcast.y_ref, f32[5,192,128]{2,1,0:T(8,128)S(1)} %bitcast.50, f32[5,192,128]{2,1,0:T(8,128)S(1)} %bitcast.51, f32[5,192,128]{2,1,0:T(8,128)S(1)} %bitcast.52, f32[5,192,128]{2,1,0:T(8,128)S(1)} %bitcast.53, ...), custom_call_target="tpu_custom_call" | custom-call | flops 10000000 | bytes 14000000 | tf_op jit(solution)/shard_map/full_rows/pallas_call | solution.py:286
  160.7 24.2 %all-to-all-done.1 = bf16[32,320,128]{2,1,0:T(8,128)(2,1)S(1)} async-done(((bf16[32,320,128]{2,1,0:T(8,128)(2,1)}), bf16[32,320,128]{2,1,0:T(8,128)(2,1)S(1)}, u32[]{:S(2)}, u32[]{:S(2)}) %all-to-all-start.1) | async-done | bytes 2621472 | tf_op jit(solution)/shard_map/all_to_all | solution.py:351
  184.8 2.3 %unpack.1 = bf16[8,8,16,1280]{3,2,1,0:T(8,128)(2,1)} custom-call(bf16[4,8,320,128]{3,2,1,0:T(8,128)(2,1)S(1)} %bitcast.49), custom_call_target="tpu_custom_call" | custom-call | tf_op jit(solution)/shard_map/unpack/pallas_call | solution.py:251
  (17 shorter events, 0.0 us)
Async XLA Ops:
  5.1 43.6 %all-to-all-start = ((bf16[32,336,128]{2,1,0:T(8,128)(2,1)}), bf16[32,336,128]{2,1,0:T(8,128)(2,1)S(1)}, u32[]{:S(2)}, u32[]{:S(2)}) async-start(bf16[32,336,128]{2,1,0:T(8,128)(2,1)} %bitcast.57), calls=%async_computation | async-start | bytes 5505024 | tf_op jit(solution)/shard_map/all_to_all | solution.py:344
  50.7 40.5 %copy-start = (f32[8,960,128]{2,1,0:T(8,128)}, f32[8,960,128]{2,1,0:T(8,128)S(1)}, u32[]{:S(2)}) copy-start(f32[8,960,128]{2,1,0:T(8,128)S(1)} %get-tuple-element.26) | copy-start | bytes 11796484
  51.0 8.8 %collective-permute-start = (f16[960,128]{1,0:T(8,128)(2,1)S(1)}, f16[960,128]{1,0:T(8,128)(2,1)S(1)}, u32[]{:S(2)}, u32[]{:S(2)}) collective-permute-start(f16[960,128]{1,0:T(8,128)(2,1)S(1)} %fusion), channel_id=1, source_target_pairs={{0,56},{8,0},{16,8},{24,16},{32,24},{40,32},{48,40},{56,48},{1,57}... | collective-permute-start | bytes 737288 | tf_op jit(solution)/shard_map/ppermute | solution.py:308
  60.1 6.3 %collective-permute-start.1 = (f16[960,128]{1,0:T(8,128)(2,1)S(1)}, f16[960,128]{1,0:T(8,128)(2,1)S(1)}, u32[]{:S(2)}, u32[]{:S(2)}) collective-permute-start(f16[960,128]{1,0:T(8,128)(2,1)S(1)} %fusion.3), channel_id=1, source_target_pairs={{0,56},{8,0},{16,8},{24,16},{32,24},{40,32},{48,40},{56,48},{1,57}... | collective-permute-start | bytes 737288 | tf_op jit(solution)/shard_map/ppermute | solution.py:308
  67.0 6.8 %collective-permute-start.3 = (f16[960,128]{1,0:T(8,128)(2,1)S(1)}, f16[960,128]{1,0:T(8,128)(2,1)S(1)}, u32[]{:S(2)}, u32[]{:S(2)}) collective-permute-start(f16[960,128]{1,0:T(8,128)(2,1)S(1)} %get-tuple-element.47), channel_id=1, source_target_pairs={{0,8},{8,16},{16,24},{24,32},{32,40},{40,48},{48,56},{56,0},{1,9},... | collective-permute-start | bytes 737288 | tf_op jit(solution)/shard_map/ppermute | solution.py:308
  74.0 7.5 %collective-permute-start.4 = (f16[960,128]{1,0:T(8,128)(2,1)S(1)}, f16[960,128]{1,0:T(8,128)(2,1)S(1)}, u32[]{:S(2)}, u32[]{:S(2)}) collective-permute-start(f16[960,128]{1,0:T(8,128)(2,1)S(1)} %fusion.13), channel_id=1, source_target_pairs={{0,8},{8,16},{16,24},{24,32},{32,40},{40,48},{48,56},{56,0},{1,9},... | collective-permute-start | bytes 737288 | tf_op jit(solution)/shard_map/ppermute | solution.py:308
  81.9 9.0 %collective-permute-start.5 = (f16[960,128]{1,0:T(8,128)(2,1)S(1)}, f16[960,128]{1,0:T(8,128)(2,1)S(1)}, u32[]{:S(2)}, u32[]{:S(2)}) collective-permute-start(f16[960,128]{1,0:T(8,128)(2,1)S(1)} %fusion.16), channel_id=1, source_target_pairs={{0,8},{8,16},{16,24},{24,32},{32,40},{40,48},{48,56},{56,0},{1,9},... | collective-permute-start | bytes 737288 | tf_op jit(solution)/shard_map/ppermute | solution.py:308
  82.0 11.2 %collective-permute-start.2 = (f16[960,128]{1,0:T(8,128)(2,1)S(1)}, f16[960,128]{1,0:T(8,128)(2,1)S(1)}, u32[]{:S(2)}, u32[]{:S(2)}) collective-permute-start(f16[960,128]{1,0:T(8,128)(2,1)S(1)} %get-tuple-element.46), channel_id=1, source_target_pairs={{0,56},{8,0},{16,8},{24,16},{32,24},{40,32},{48,40},{56,48},{1,57}... | collective-permute-start | bytes 737288 | tf_op jit(solution)/shard_map/ppermute | solution.py:308
  91.2 8.4 %collective-permute-start.6 = (f16[960,128]{1,0:T(8,128)(2,1)S(1)}, f16[960,128]{1,0:T(8,128)(2,1)S(1)}, u32[]{:S(2)}, u32[]{:S(2)}) collective-permute-start(f16[960,128]{1,0:T(8,128)(2,1)S(1)} %fusion.19), channel_id=1, source_target_pairs={{0,8},{8,16},{16,24},{24,32},{32,40},{40,48},{48,56},{56,0},{1,9},... | collective-permute-start | bytes 737288 | tf_op jit(solution)/shard_map/ppermute | solution.py:308
  101.3 8.9 %collective-permute-start.10 = (bf16[960,128]{1,0:T(8,128)(2,1)S(1)}, bf16[960,128]{1,0:T(8,128)(2,1)S(1)}, u32[]{:S(2)}, u32[]{:S(2)}) collective-permute-start(bf16[960,128]{1,0:T(8,128)(2,1)S(1)} %get-tuple-element.36.refs_0_), channel_id=1, source_target_pairs={{0,8},{8,16},{16,24},{24,32},{32,40},{40,48},{48,56},{56,0},{1,9},... | collective-permute-start | bytes 737288 | tf_op jit(solution)/shard_map/ppermute | solution.py:308
  101.4 10.3 %collective-permute-start.7 = (bf16[960,128]{1,0:T(8,128)(2,1)S(1)}, bf16[960,128]{1,0:T(8,128)(2,1)S(1)}, u32[]{:S(2)}, u32[]{:S(2)}) collective-permute-start(bf16[960,128]{1,0:T(8,128)(2,1)S(1)} %get-tuple-element.36.refs_0_), channel_id=1, source_target_pairs={{0,56},{8,0},{16,8},{24,16},{32,24},{40,32},{48,40},{56,48},{1,57}... | collective-permute-start | bytes 737288 | tf_op jit(solution)/shard_map/ppermute | solution.py:308
  110.2 6.3 %collective-permute-start.11 = (bf16[960,128]{1,0:T(8,128)(2,1)S(1)}, bf16[960,128]{1,0:T(8,128)(2,1)S(1)}, u32[]{:S(2)}, u32[]{:S(2)}) collective-permute-start(bf16[960,128]{1,0:T(8,128)(2,1)S(1)} %collective-permute-done.10.refs_7_), channel_id=1, source_target_pairs={{0,8},{8,16},{16,24},{24,32},{32,40},{40,48},{48,56},{56,0},{1,9},... | collective-permute-start | bytes 737288 | tf_op jit(solution)/shard_map/ppermute | solution.py:308
  110.2 12.5 %collective-permute-start.14 = (f32[960,128]{1,0:T(8,128)S(1)}, f32[960,128]{1,0:T(8,128)S(1)}, u32[]{:S(2)}, u32[]{:S(2)}) collective-permute-start(f32[960,128]{1,0:T(8,128)S(1)} %get-tuple-element.28), channel_id=1, source_target_pairs={{0,192},{64,0},{128,64},{192,128},{1,193},{65,1},{129,65},{193,129... | collective-permute-start | bytes 1474568 | tf_op jit(solution)/shard_map/ppermute | solution.py:308
  110.2 13.3 %collective-permute-start.15 = (f32[960,128]{1,0:T(8,128)S(1)}, f32[960,128]{1,0:T(8,128)S(1)}, u32[]{:S(2)}, u32[]{:S(2)}) collective-permute-start(f32[960,128]{1,0:T(8,128)S(1)} %get-tuple-element.28), channel_id=1, source_target_pairs={{0,128},{64,192},{128,0},{192,64},{1,129},{65,193},{129,1},{193,65... | collective-permute-start | bytes 1474568 | tf_op jit(solution)/shard_map/ppermute | solution.py:308
  110.3 14.9 %collective-permute-start.16 = (f32[960,128]{1,0:T(8,128)S(1)}, f32[960,128]{1,0:T(8,128)S(1)}, u32[]{:S(2)}, u32[]{:S(2)}) collective-permute-start(f32[960,128]{1,0:T(8,128)S(1)} %get-tuple-element.28), channel_id=1, source_target_pairs={{0,64},{64,128},{128,192},{192,0},{1,65},{65,129},{129,193},{193,1... | collective-permute-start | bytes 1474568 | tf_op jit(solution)/shard_map/ppermute | solution.py:308
  111.7 6.7 %collective-permute-start.8 = (bf16[960,128]{1,0:T(8,128)(2,1)S(1)}, bf16[960,128]{1,0:T(8,128)(2,1)S(1)}, u32[]{:S(2)}, u32[]{:S(2)}) collective-permute-start(bf16[960,128]{1,0:T(8,128)(2,1)S(1)} %collective-permute-done.7.refs_1_), channel_id=1, source_target_pairs={{0,56},{8,0},{16,8},{24,16},{32,24},{40,32},{48,40},{56,48},{1,57}... | collective-permute-start | bytes 737288 | tf_op jit(solution)/shard_map/ppermute | solution.py:308
  116.5 6.3 %collective-permute-start.12 = (bf16[960,128]{1,0:T(8,128)(2,1)S(1)}, bf16[960,128]{1,0:T(8,128)(2,1)S(1)}, u32[]{:S(2)}, u32[]{:S(2)}) collective-permute-start(bf16[960,128]{1,0:T(8,128)(2,1)S(1)} %collective-permute-done.11.refs_6_), channel_id=1, source_target_pairs={{0,8},{8,16},{16,24},{24,32},{32,40},{40,48},{48,56},{56,0},{1,9},... | collective-permute-start | bytes 737288 | tf_op jit(solution)/shard_map/ppermute | solution.py:308
  118.4 7.5 %collective-permute-start.9 = (bf16[960,128]{1,0:T(8,128)(2,1)S(1)}, bf16[960,128]{1,0:T(8,128)(2,1)S(1)}, u32[]{:S(2)}, u32[]{:S(2)}) collective-permute-start(bf16[960,128]{1,0:T(8,128)(2,1)S(1)} %collective-permute-done.8.refs_2_), channel_id=1, source_target_pairs={{0,56},{8,0},{16,8},{24,16},{32,24},{40,32},{48,40},{56,48},{1,57}... | collective-permute-start | bytes 737288 | tf_op jit(solution)/shard_map/ppermute | solution.py:308
  122.8 6.9 %collective-permute-start.13 = (bf16[960,128]{1,0:T(8,128)(2,1)S(1)}, bf16[960,128]{1,0:T(8,128)(2,1)S(1)}, u32[]{:S(2)}, u32[]{:S(2)}) collective-permute-start(bf16[960,128]{1,0:T(8,128)(2,1)S(1)} %collective-permute-done.12.refs_5_), channel_id=1, source_target_pairs={{0,8},{8,16},{16,24},{24,32},{32,40},{40,48},{48,56},{56,0},{1,9},... | collective-permute-start | bytes 737288 | tf_op jit(solution)/shard_map/ppermute | solution.py:308
  122.8 0.8 copy-start.1
  123.5 0.8 copy-start.3
  125.2 0.8 copy-start.5
  134.0 50.8 %all-to-all-start.1 = ((bf16[32,320,128]{2,1,0:T(8,128)(2,1)}), bf16[32,320,128]{2,1,0:T(8,128)(2,1)S(1)}, u32[]{:S(2)}, u32[]{:S(2)}) async-start(bf16[32,320,128]{2,1,0:T(8,128)(2,1)} %fetch.1), calls=%async_computation.1 | async-start | bytes 5242880 | tf_op jit(solution)/shard_map/all_to_all | solution.py:351
  151.3 1.0 copy-start.2
  152.3 1.0 copy-start.4
  153.3 1.0 copy-start.6

commit v2 on v1

v2 whole, which is shorter than its diff:
```python
import functools

import jax
import jax.numpy as jnp
from jax import lax
from jax.experimental import pallas as pl
from jax.experimental.pallas import tpu as pltpu
from jax.sharding import Mesh, PartitionSpec as P

STEP = 20
LANES = 128
CAP = 16
BF = jnp.bfloat16
F32 = jnp.float32
F16 = jnp.float16
SLAB = ("y", "x", "c")
GROUP = 32
NZ = 8
NY = 4
XC = 8
ROWS = 384
HALF = 192
QROWS = 960


def adamw(weights, first, second, grads):
    first_new = 0.9 * first + 0.1 * grads
    second_new = 0.95 * second + 0.05 * grads * grads
    corr_one = 1.0 - 0.9**STEP
    corr_two = 1.0 - 0.95**STEP
    update = first_new / corr_one / (jnp.sqrt(second_new / corr_two) + 1e-08) + 0.01 * weights
    return (weights - 0.1 * update, first_new, second_new)


def low_lanes(shape):
    return lax.broadcasted_iota(jnp.int32, shape, len(shape) - 1) < 64


def pair(a, b, upper):
    low = low_lanes(a.shape)
    axis = a.ndim - 1
    if isinstance(upper, bool):
        return jnp.where(low, pltpu.roll(a, 64, axis), b) if upper else jnp.where(low, a, pltpu.roll(b, 64, axis))
    return jnp.where(
        upper,
        jnp.where(low, pltpu.roll(a, 64, axis), b),
        jnp.where(low, a, pltpu.roll(b, 64, axis)),
    )


def params(mib):
    return pltpu.CompilerParams(vmem_limit_bytes=mib * 1024 * 1024)


def hbm(x):
    return pltpu.with_memory_space_constraint(x, pltpu.HBM)


def tile_iota(axis):
    return lax.broadcasted_iota(jnp.int32, (8, LANES), axis)


def diagonal(rolled, shift):
    moved = pltpu.roll(rolled, (NZ * LANES - CAP * shift) % LANES, 1)
    kept = jnp.where(tile_iota(1) // CAP == tile_iota(0), moved, 0.0)
    return jnp.sum(kept, axis=0, keepdims=True)


def row_roll(x):
    return pltpu.roll(x, 0, 1, stride=CAP, stride_axis=0)


def chunk_rows(n):
    return 2 * CAP * n + CAP * ((n + 1) // 2)


def pack_kernel(n, step, with_ids, z_ref, *refs):
    blocks, o_ref = refs[:n], refs[-1]
    sub = lax.broadcasted_iota(jnp.int32, (CAP, LANES), 0)
    if with_ids:
        ids = [row_roll(r[...].astype(F32)) for r in refs[n : n + 2]]
    for u in range(step):
        rest = jnp.zeros((CAP, LANES), F32)
        if with_ids:
            for t in range(2):
                mine = diagonal(ids[t], pl.program_id(0) * step + u)
                upper = jnp.floor(mine * (1.0 / 16.0))
                lower = mine - 16.0 * upper
                for r, row in enumerate((pltpu.roll(upper, 64, 1), upper, pltpu.roll(lower, 64, 1), lower)):
                    rest = jnp.where(sub == 4 * t + r, row, rest)
        for y in range(NY):
            for p in range(n):
                o_ref[y, u, pl.ds(p * CAP, CAP), :] = blocks[p][0, u, :, pl.ds(y * LANES, LANES)]
                o_ref[y, u, pl.ds((n + p) * CAP, CAP), :] = blocks[p][0, u, :, pl.ds(512 + y * LANES, LANES)]
            cols = pl.ds(1024 + (y // 2) * LANES, LANES)
            for t in range((n + 1) // 2):
                a = blocks[2 * t][0, u, :, cols].astype(F32)
                if 2 * t + 1 < n:
                    tile = pair(a, blocks[2 * t + 1][0, u, :, cols].astype(F32), y % 2 == 1)
                else:
                    tile = jnp.where(low_lanes(a.shape), pltpu.roll(a, 64, 1) if y % 2 else a, rest)
                o_ref[y, u, pl.ds((2 * n + t) * CAP, CAP), :] = tile.astype(BF)


def pack(z, ks, grad_rows, ids=()):
    n, step = len(ks), 4
    rows = chunk_rows(n)
    whole = pl.BlockSpec((8, LANES), lambda i, s: (0, 0))
    block = lambda k: pl.BlockSpec((1, step, CAP, 1280), lambda i, s: ((s[0] + k) % NZ, i, 0, 0))
    grads = hbm(grad_rows.reshape(NZ, XC, CAP, 1280))
    out = pl.pallas_call(
        functools.partial(pack_kernel, n, step, bool(ids)),
        grid_spec=pltpu.PrefetchScalarGridSpec(
            num_scalar_prefetch=1,
            grid=(XC // step,),
            in_specs=[block(k) for k in ks] + [whole for _ in ids],
            out_specs=pl.BlockSpec((NY, step, rows, LANES), lambda i, s: (0, i, 0, 0)),
        ),
        out_shape=pltpu.HBM((NY, XC, rows, LANES), BF),
        compiler_params=params(14),
        cost_estimate=pl.CostEstimate(flops=0, bytes_accessed=700_000 * n, transcendentals=0),
        name="pack",
    )(z, *[grads] * n, *[hbm(i.reshape(8, LANES)) for i in ids])
    return out.reshape(GROUP, rows, LANES)


def read_ids(z_ref, got_ref, at, outs):
    sub = tile_iota(0)
    low = low_lanes((8, LANES))
    for q in range(GROUP // 8):
        tiles = [jnp.zeros((8, LANES), F32)] * 4
        for j in range(8):
            head = got_ref[8 * q + j, pl.ds(at, CAP), :].astype(F32)
            for t in range(4):
                row = 4 * (t // 2) + t % 2
                mine = head[row : row + 1] * 16.0 + head[row + 2 : row + 3]
                tiles[t] = jnp.where(sub == j, mine, tiles[t])
        for t, ref in enumerate(outs):
            rolled = row_roll(jnp.where(low, pltpu.roll(tiles[2 * t], 64, 1), tiles[2 * t + 1]))
            for k in range(NZ):
                ref[pl.ds(k, 1), pl.ds(q * LANES, LANES)] = diagonal(rolled, z_ref[0] + k).astype(jnp.int32)


def sums_kernel(ks, first, z_ref, *refs):
    n = len(ks)
    if first:
        got_ref, outs, ids_ref = refs[0], refs[1 : 1 + n], refs[1 + n]
        read_ids(z_ref, got_ref, (2 * n + n // 2) * CAP, refs[1 + n :])
    else:
        got_ref, ids_ref, outs = refs[0], refs[1], refs[2:]
    rows = lax.broadcasted_iota(jnp.int32, (ROWS, GROUP * CAP), 0)
    for p, k in enumerate(ks):
        pick = jnp.where(rows == ids_ref[pl.ds(k, 1), :], 1.0, 0.0).astype(BF)
        slots = jnp.concatenate(
            [
                got_ref[:, pl.ds(at * CAP, CAP), :].reshape(GROUP * CAP, LANES)
                for at in (p, n + p, 2 * n + p // 2)
            ],
            axis=1,
        )
        total = jnp.dot(pick, slots, preferred_element_type=F32)
        outs[p][pl.ds(0, ROWS), :] = total[:, :128]
        outs[p][pl.ds(ROWS, ROWS), :] = total[:, 128:256]
        last = total[:, 256:]
        outs[p][pl.ds(2 * ROWS, HALF), :] = pair(last[:HALF], last[HALF:], p % 2 == 1)


def partial_sums(z, ks, got, ids=None):
    vmem = pl.BlockSpec(memory_space=pltpu.VMEM)
    first = ids is None
    ids_shape = jax.ShapeDtypeStruct((NZ, GROUP * CAP), jnp.int32)
    outs = [jax.ShapeDtypeStruct((QROWS, LANES), F32)] * len(ks) + [ids_shape] * (2 if first else 0)
    got = pl.pallas_call(
        functools.partial(sums_kernel, ks, first),
        in_specs=[pl.BlockSpec(memory_space=pltpu.SMEM)] + [vmem] * (1 if first else 2),
        out_specs=[vmem] * len(outs),
        out_shape=outs,
        compiler_params=params(12),
        name="partial_sums",
    )(z, got, *(() if first else (ids,)))
    return dict(zip(ks, got)), tuple(got[len(ks) :])


def quarter_kernel(y_ref, *refs):
    odd = y_ref[0] % 2 == 1
    for i in range(3):
        a, b, c = (r[...] for r in refs[3 * i : 3 * i + 3])
        o_ref = refs[9 + i]
        o_ref[pl.ds(0, ROWS), :] = a
        o_ref[pl.ds(ROWS, ROWS), :] = b
        o_ref[pl.ds(2 * ROWS, HALF), :] = pair(c[:HALF], c[HALF:], odd)


def quarters(y, *arrays):
    spec = [
        pl.BlockSpec((ROWS, LANES), lambda i, s: (0, s[0])),
        pl.BlockSpec((ROWS, LANES), lambda i, s: (0, NY + s[0])),
        pl.BlockSpec((ROWS, LANES), lambda i, s: (0, 2 * NY + s[0] // 2)),
    ]
    return pl.pallas_call(
        quarter_kernel,
        grid_spec=pltpu.PrefetchScalarGridSpec(
            num_scalar_prefetch=1,
            grid=(1,),
            in_specs=spec * 3,
            out_specs=[pl.BlockSpec((QROWS, LANES), lambda i, s: (0, 0))] * 3,
        ),
        out_shape=[jax.ShapeDtypeStruct((QROWS, LANES), F32)] * 3,
        compiler_params=params(12),
        cost_estimate=pl.CostEstimate(flops=1_000_000, bytes_accessed=3_000_000, transcendentals=0),
        name="quarters",
    )(y, *[hbm(t) for t in arrays for _ in range(3)])


def fetch_kernel(ks, ids_ref, *refs):
    n = len(ks)
    tables, o_ref = refs[:n], refs[n]
    rows = lax.broadcasted_iota(jnp.int32, (GROUP * CAP, ROWS), 1).astype(F32)
    columns = jnp.transpose(ids_ref[...].astype(F32))
    low = low_lanes((GROUP, CAP, LANES))
    even = None
    for p, k in enumerate(ks):
        pick = jnp.where(rows == columns[:, k : k + 1], 1.0, 0.0).astype(BF)
        table = tables[p]
        last = table[pl.ds(2 * ROWS, HALF), :]
        moved = pltpu.roll(last.astype(F32), 64, 1).astype(BF)
        halves = [moved, last] if p % 2 else [last, moved]
        wide = jnp.concatenate(
            [table[pl.ds(0, ROWS), :], table[pl.ds(ROWS, ROWS), :], jnp.concatenate(halves, axis=0)], axis=1
        )
        found = jnp.dot(pick, wide, preferred_element_type=F32)
        found = found.astype(BF).reshape(GROUP, CAP, 3 * LANES)
        o_ref[:, pl.ds(p * CAP, CAP), :] = found[:, :, :128]
        o_ref[:, pl.ds((n + p) * CAP, CAP), :] = found[:, :, 128:256]
        if p % 2:
            o_ref[:, pl.ds((2 * n + p // 2) * CAP, CAP), :] = jnp.where(low, even, found[:, :, 256:])
        else:
            even = found[:, :, 256:]
            if p == n - 1:
                o_ref[:, pl.ds((2 * n + p // 2) * CAP, CAP), :] = even


def fetch(ks, ids, tables):
    vmem = pl.BlockSpec(memory_space=pltpu.VMEM)
    return pl.pallas_call(
        functools.partial(fetch_kernel, ks),
        in_specs=[vmem] * (1 + len(ks)),
        out_specs=vmem,
        out_shape=jax.ShapeDtypeStruct((GROUP, chunk_rows(len(ks)), LANES), BF),
        compiler_params=params(12),
        name="fetch",
    )(ids, *[tables[k] for k in ks])


def unpack_kernel(chunks, step, z_ref, *refs):
    o_ref = refs[-1]
    for ks, g_ref in zip(chunks, refs):
        n = len(ks)
        for p, k in enumerate(ks):
            z = (z_ref[0] + k) % NZ
            for u in range(step):
                for y in range(NY):
                    o_ref[z, u, :, pl.ds(y * LANES, LANES)] = g_ref[y, u, pl.ds(p * CAP, CAP), :]
                    o_ref[z, u, :, pl.ds(512 + y * LANES, LANES)] = g_ref[y, u, pl.ds((n + p) * CAP, CAP), :]
                at = pl.ds((2 * n + p // 2) * CAP, CAP)
                for t in range(2):
                    a = g_ref[2 * t, u, at, :].astype(F32)
                    b = g_ref[2 * t + 1, u, at, :].astype(F32)
                    o_ref[z, u, :, pl.ds(1024 + t * LANES, LANES)] = pair(a, b, p % 2 == 1).astype(BF)


def unpack(z, chunks, backs):
    step = 2
    out = pl.pallas_call(
        functools.partial(unpack_kernel, chunks, step),
        grid_spec=pltpu.PrefetchScalarGridSpec(
            num_scalar_prefetch=1,
            grid=(XC // step,),
            in_specs=[
                pl.BlockSpec((NY, step, chunk_rows(len(ks)), LANES), lambda i, s: (0, i, 0, 0)) for ks in chunks
            ],
            out_specs=pl.BlockSpec((NZ, step, CAP, 1280), lambda i, s: (0, i, 0, 0)),
        ),
        out_shape=pltpu.HBM((NZ, XC, CAP, 1280), BF),
        compiler_params=params(12),
        name="unpack",
    )(z, *[b.reshape(NY, XC, -1, LANES) for b in backs])
    return out.reshape(NZ * XC * CAP, 1280)


FULL_STEP = 48


def full_kernel(y_ref, *refs):
    g_refs, (w_ref, m_ref, v_ref, ow_ref, om_ref, ov_ref, all_ref) = refs[:NY], refs[NY:]
    for d in range(NY):
        all_ref[(y_ref[0] + d) % NY] = g_refs[d][...]
    for half in range(2):
        for t in range(10):
            if t < 8:
                grads = all_ref[t % NY, 2 * (t // NY) + half]
            else:
                grads = pair(all_ref[2 * (t - 8), 4], all_ref[2 * (t - 8) + 1, 4], half == 1)
            cols = pl.ds(t * LANES, LANES)
            w, m, v = adamw(w_ref[half, :, cols], m_ref[half, :, cols], v_ref[half, :, cols], grads)
            ow_ref[half, :, cols] = w
            om_ref[half, :, cols] = m
            ov_ref[half, :, cols] = v


def full_rows(y, grads, table_rows, first_moment, second_moment):
    wide = pl.BlockSpec((2, FULL_STEP, 1280), lambda i, s: (0, i, 0))
    part = pl.BlockSpec((5, FULL_STEP, LANES), lambda i, s: (0, i, 0))
    outs = pl.pallas_call(
        full_kernel,
        grid_spec=pltpu.PrefetchScalarGridSpec(
            num_scalar_prefetch=1,
            grid=(HALF // FULL_STEP,),
            in_specs=[part] * NY + [wide] * 3,
            out_specs=[wide] * 3,
            scratch_shapes=[pltpu.VMEM((NY, 5, FULL_STEP, LANES), F32)],
        ),
        out_shape=[pltpu.HBM((2, HALF, 1280), F32)] * 3,
        compiler_params=params(12),
        cost_estimate=pl.CostEstimate(flops=10_000_000, bytes_accessed=14_000_000, transcendentals=0),
        name="full_rows",
    )(
        y,
        *[g.reshape(5, HALF, LANES) for g in grads],
        *[hbm(t.reshape(2, HALF, 1280)) for t in (table_rows, first_moment, second_moment)],
    )
    return tuple(t.reshape(ROWS, 1280) for t in outs)


def along(value, axis, size, step):
    return lax.ppermute(value, axis, [(i, (i + step) % size) for i in range(size)])


def coded(x):
    root = jnp.sqrt(jnp.abs(x)) * 256.0
    return jnp.where(x < 0.0, -root, root).astype(F16)


def decoded(h):
    wide = h.astype(F32)
    return wide * jnp.abs(wide) * (1.0 / 65536.0)


def both_ways(up, down):
    up, down = lax.optimization_barrier((up, down))
    return lax.optimization_barrier((along(up, "z", NZ, 1), along(down, "z", NZ, -1)))


def send_sums(up, down):
    up, down = both_ways(coded(up), coded(down))
    return decoded(up), decoded(down)


def swap(x):
    return lax.all_to_all(x, SLAB, split_axis=0, concat_axis=0, tiled=True)


FAR, NEAR = (4, 3, 5), (2, 6, 1, 7, 0)
FIRST, LATER = (0, 1, 7, 2, 6), (3, 5, 4)


def local(table_rows, first_moment, second_moment, grad_rows, row_ids, next_ids):
    z = lax.axis_index("z").astype(jnp.int32)[None]
    y = lax.axis_index("y").astype(jnp.int32)[None]
    far = swap(pack(z, FAR, grad_rows, (row_ids, next_ids)))
    near = swap(pack(z, NEAR, grad_rows))
    mine = quarters(y, table_rows, first_moment, second_moment)
    part, (ids, wanted) = partial_sums(z, FAR, far)
    up = decoded(along(coded(part[4]), "z", NZ, 1))
    up, down = send_sums(part[3] + up, part[5])
    near, up, down = lax.optimization_barrier((near, up, down))
    part, _ = partial_sums(z, NEAR, near, ids)
    up, down = send_sums(part[2] + up, part[6] + down)
    up, down = send_sums(part[1] + up, part[7] + down)
    shared = coded(part[0] + up + down)
    summed = decoded(shared)
    own = adamw(*mine, summed)[0].astype(BF)
    grads = [shared] + [along(shared, "y", NY, -d) for d in range(1, NY)]
    tables = {0: own}
    tables[7], tables[1] = both_ways(own, own)
    tables[6], tables[2], *grads[1:] = lax.optimization_barrier(
        (along(tables[7], "z", NZ, 1), along(tables[1], "z", NZ, -1), *grads[1:])
    )
    found, tables[6], tables[2] = lax.optimization_barrier((fetch(FIRST, wanted, tables), tables[6], tables[2]))
    back = swap(found)
    tables[5], tables[3] = both_ways(tables[6], tables[2])
    tables[4] = along(tables[5], "z", NZ, 1)
    back, found = lax.optimization_barrier((back, fetch(LATER, wanted, tables)))
    backs = [back, swap(found)]
    outs = full_rows(y, [decoded(g) for g in grads], table_rows, first_moment, second_moment)
    return (*outs, unpack(z, (FIRST, LATER), backs))


def solution(mesh):
    fine = Mesh(mesh.devices.reshape(NY, NZ, 4, 2), ("y", "z", "x", "c"))
    owner = ("z", "x", "c")
    every = ("y", "z", "x", "c")
    return jax.shard_map(
        local,
        mesh=fine,
        in_specs=(P(owner, None), P(owner, None), P(owner, None), P(every, None), P(every), P(every)),
        out_specs=(P(owner, None), P(owner, None), P(owner, None), P(every, None)),
        check_vma=False,
    )
```

time: 188 us -> 157 us (0.84)
  waiting for transfers between devices: 108 us -> 68.5 us
  starting transfers between devices: 48 us -> 58.6 us
  local copies, waits for them, and re-layouts: 5.42 us -> 0.01 us
    all_to_all x2 -> x4, waiting for transfers between devices: 59.1 us -> 30.6 us  [swap(): return lax.all_to_all(x, SLAB, split_axis=0, concat_axis=0, tiled=True)]
    ppermute x17, waiting for transfers between devices: 48.9 us -> 37.9 us  [along(): lax.ppermute(value, axis, [(i, (i + step) % size) for i in range(size)])]
    ppermute x17, starting transfers between devices: 22.1 us -> 30.6 us  [along(): lax.ppermute(value, axis, [(i, (i + step) % size) for i in range(size)])]
    unnamed x14 -> x6, local copies, waits for them, and re-layouts: 5.42 us -> 0.01 us
    mul x0 -> x5, other arithmetic: none -> 2.29 us  [decoded(): return wide * jnp.abs(wide) * (1.0 / 65536.0)]
    all_to_all x2 -> x4, starting transfers between devices: 25.9 us -> 28 us  [swap(): return lax.all_to_all(x, SLAB, split_axis=0, concat_axis=0, tiled=True)]
    pallas_call x4 -> x7, Pallas kernels: 13.1 us -> 14.9 us  [the longest x2 5.32 us: pack(): pl.pallas_call(functools.partial(pack_kernel, n, step, bool(ids)), grid_s...]
  transfers between devices with their start and end apart: 19 -> 21, of which waited for: 14 -> 11; matrix products, arithmetic and copies ran while one was open for 0% -> 2% of each run, Pallas kernels for 4% -> 9%
where the time goes in v2:
time: 157 us; the launch traced here: 156 us
  waiting for transfers between devices  68.5 us (44%)
  starting transfers between devices  58.6 us (37%)
  Pallas kernels  23.1 us (15%)
  other arithmetic  5.02 us (3%)
    ppermute x17, waiting for transfers between devices, along(): lax.ppermute(value, axis, [(i, (i + step) % size) for i in range(size)])  37.9 us
    ppermute x17, starting transfers between devices, along(): lax.ppermute(value, axis, [(i, (i + step) % size) for i in range(size)])  30.6 us
    all_to_all x4, waiting for transfers between devices, swap(): return lax.all_to_all(x, SLAB, split_axis=0, concat_axis=0, tiled=True)  30.6 us
    all_to_all x4, starting transfers between devices, swap(): return lax.all_to_all(x, SLAB, split_axis=0, concat_axis=0, tiled=True)  28 us
    pallas_call x1, Pallas kernels, full_rows(): pl.pallas_call(full_kernel, grid_spec=pltpu.PrefetchScalarGridSpec(num_sc...  6.33 us
    pallas_call x2, Pallas kernels, pack(): pl.pallas_call(functools.partial(pack_kernel, n, step, bool(ids)), grid_s...  5.32 us
    pallas_call x2, Pallas kernels, fetch(): pl.pallas_call(functools.partial(fetch_kernel, ks), in_specs=[vmem] * (1...  4.89 us
  transfers between devices with their start and end apart: 21, of which 11 were waited for; matrix products, arithmetic and copies ran while one was open for 2% of the time, Pallas kernels for 9%

profile of v2, /device:TPU:1, one launch (start us, length us, event | category | flops | bytes accessed | tf_op | source)
XLA Modules:
  0.0 156.0 jit_solution(14300874437713493683)
XLA Ops:
  0.6 2.6 %pack.3 = bf16[4,8,128,128]{3,2,1,0:T(8,128)(2,1)} custom-call(s32[1]{0:T(128)} %bitcast.1.z_ref, bf16[8,8,16,1280]{3,2,1,0:T(8,128)(2,1)} %bitcast.26, bf16[8,8,16,1280]{3,2,1,0:T(8,128)(2,1)} %bitcast.27, bf16[8,8,16,1280]{3,2,1,0:T(8,128)(2,1)} %bitcast.28, s32[8,128]{1,0:T(8,128)} %bitcast.40, s32[8,128]{1,0:T(8,128)} %bitcast.41), custom_call_target="tpu_custom_call" | custom-call | bytes 2100000 | tf_op jit(solution)/shard_map/pack/pallas_call | solution.py:111
  3.2 8.6 %all-to-all-start.1 = ((bf16[32,128,128]{2,1,0:T(8,128)(2,1)}), bf16[32,128,128]{2,1,0:T(8,128)(2,1)S(1)}, u32[]{:S(2)}, u32[]{:S(2)}) async-start(bf16[32,128,128]{2,1,0:T(8,128)(2,1)} %bitcast.38), calls=%async_computation.1 | async-start | bytes 2097152 | tf_op jit(solution)/shard_map/all_to_all | solution.py:360
  11.8 2.7 %pack.2 = bf16[4,8,208,128]{3,2,1,0:T(8,128)(2,1)} custom-call(s32[1]{0:T(128)} %bitcast.1.z_ref, bf16[8,8,16,1280]{3,2,1,0:T(8,128)(2,1)} %bitcast.29, bf16[8,8,16,1280]{3,2,1,0:T(8,128)(2,1)} %bitcast.30, bf16[8,8,16,1280]{3,2,1,0:T(8,128)(2,1)} %bitcast.31, bf16[8,8,16,1280]{3,2,1,0:T(8,128)(2,1)} %bitcast.32, bf16[8,8,16,1280]{3,2,1,0:T(8,128)(2,1)} %bitcast.33), custom_call_target="tpu_custom_call" | custom-call | bytes 3500000 | tf_op jit(solution)/shard_map/pack/pallas_call | solution.py:111
  14.6 14.4 %all-to-all-done.1.refs_0_ = bf16[32,128,128]{2,1,0:T(8,128)(2,1)S(1)} async-done(((bf16[32,128,128]{2,1,0:T(8,128)(2,1)}), bf16[32,128,128]{2,1,0:T(8,128)(2,1)S(1)}, u32[]{:S(2)}, u32[]{:S(2)}) %all-to-all-start.1) | async-done | bytes 1048608 | tf_op jit(solution)/shard_map/all_to_all | solution.py:360
  29.0 4.0 %all-to-all-start = ((bf16[32,208,128]{2,1,0:T(8,128)(2,1)}), bf16[32,208,128]{2,1,0:T(8,128)(2,1)S(1)}, u32[]{:S(2)}, u32[]{:S(2)}) async-start(bf16[32,208,128]{2,1,0:T(8,128)(2,1)} %bitcast.37), calls=%async_computation | async-start | bytes 3407872 | tf_op jit(solution)/shard_map/all_to_all | solution.py:360
  33.0 1.1 partial_sums.2
  34.1 0.2 fusion
  34.3 1.7 %collective-permute-start = (f16[960,128]{1,0:T(8,128)(2,1)S(1)}, f16[960,128]{1,0:T(8,128)(2,1)S(1)}, u32[]{:S(2)}, u32[]{:S(2)}) collective-permute-start(f16[960,128]{1,0:T(8,128)(2,1)S(1)} %fusion), channel_id=1, source_target_pairs={{0,8},{8,16},{16,24},{24,32},{32,40},{40,48},{48,56},{56,0},{1,9},... | collective-permute-start | bytes 737288 | tf_op jit(solution)/shard_map/ppermute | solution.py:336
  36.0 0.2 fusion.4
  36.3 9.8 %collective-permute-done = f16[960,128]{1,0:T(8,128)(2,1)S(1)} collective-permute-done((f16[960,128]{1,0:T(8,128)(2,1)S(1)}, f16[960,128]{1,0:T(8,128)(2,1)S(1)}, u32[]{:S(2)}, u32[]{:S(2)}) %collective-permute-start) | collective-permute-done | bytes 245792 | tf_op jit(solution)/shard_map/ppermute | solution.py:336
  46.0 0.3 fusion.3
  46.4 2.7 %collective-permute-start.2 = (f16[960,128]{1,0:T(8,128)(2,1)S(1)}, f16[960,128]{1,0:T(8,128)(2,1)S(1)}, u32[]{:S(2)}, u32[]{:S(2)}) collective-permute-start(f16[960,128]{1,0:T(8,128)(2,1)S(1)} %fusion.4), channel_id=1, source_target_pairs={{0,56},{8,0},{16,8},{24,16},{32,24},{40,32},{48,40},{56,48},{1,57}... | collective-permute-start | bytes 737288 | tf_op jit(solution)/shard_map/ppermute | solution.py:336
  49.1 5.1 %collective-permute-done.1 = f16[960,128]{1,0:T(8,128)(2,1)S(1)} collective-permute-done((f16[960,128]{1,0:T(8,128)(2,1)S(1)}, f16[960,128]{1,0:T(8,128)(2,1)S(1)}, u32[]{:S(2)}, u32[]{:S(2)}) %collective-permute-start.1) | collective-permute-done | bytes 245792 | tf_op jit(solution)/shard_map/ppermute | solution.py:336
  54.2 1.1 fusion.5
  55.3 1.3 all-to-all-done.refs_0_
  56.6 1.2 partial_sums.3
  57.8 0.2 fusion.8
  58.1 0.2 fusion.7
  58.4 1.7 %collective-permute-start.3 = (f16[960,128]{1,0:T(8,128)(2,1)S(1)}, f16[960,128]{1,0:T(8,128)(2,1)S(1)}, u32[]{:S(2)}, u32[]{:S(2)}) collective-permute-start(f16[960,128]{1,0:T(8,128)(2,1)S(1)} %fusion.7), channel_id=1, source_target_pairs={{0,8},{8,16},{16,24},{24,32},{32,40},{40,48},{48,56},{56,0},{1,9},... | collective-permute-start | bytes 737288 | tf_op jit(solution)/shard_map/ppermute | solution.py:336
  60.1 4.0 %collective-permute-start.4 = (f16[960,128]{1,0:T(8,128)(2,1)S(1)}, f16[960,128]{1,0:T(8,128)(2,1)S(1)}, u32[]{:S(2)}, u32[]{:S(2)}) collective-permute-start(f16[960,128]{1,0:T(8,128)(2,1)S(1)} %fusion.8), channel_id=1, source_target_pairs={{0,56},{8,0},{16,8},{24,16},{32,24},{40,32},{48,40},{56,48},{1,57}... | collective-permute-start | bytes 737288 | tf_op jit(solution)/shard_map/ppermute | solution.py:336
  64.1 4.0 %collective-permute-done.3 = f16[960,128]{1,0:T(8,128)(2,1)S(1)} collective-permute-done((f16[960,128]{1,0:T(8,128)(2,1)S(1)}, f16[960,128]{1,0:T(8,128)(2,1)S(1)}, u32[]{:S(2)}, u32[]{:S(2)}) %collective-permute-start.3) | collective-permute-done | bytes 245792 | tf_op jit(solution)/shard_map/ppermute | solution.py:336
  68.1 0.3 fusion.14
  68.4 0.3 fusion.11
  68.8 2.7 %collective-permute-start.6 = (f16[960,128]{1,0:T(8,128)(2,1)S(1)}, f16[960,128]{1,0:T(8,128)(2,1)S(1)}, u32[]{:S(2)}, u32[]{:S(2)}) collective-permute-start(f16[960,128]{1,0:T(8,128)(2,1)S(1)} %fusion.14), channel_id=1, source_target_pairs={{0,56},{8,0},{16,8},{24,16},{32,24},{40,32},{48,40},{56,48},{1,57}... | collective-permute-start | bytes 737288 | tf_op jit(solution)/shard_map/ppermute | solution.py:336
  71.5 1.8 %quarters.1 = (f32[960,128]{1,0:T(8,128)S(1)}, f32[960,128]{1,0:T(8,128)S(1)}, f32[960,128]{1,0:T(8,128)S(1)}) custom-call(s32[1]{0:T(128)} %bitcast.y_ref, f32[384,1280]{1,0:T(8,128)} %refs_2_.1, f32[384,1280]{1,0:T(8,128)} %refs_2_.1, f32[384,1280]{1,0:T(8,128)} %refs_2_.1, f32[384,1280]{1,0:T(8,128)} %refs_5_.1, f32[384,1280]{1,0:T(8,128)} %refs_5_.1, ...), custom_call_target="tpu_custom_call" | custom-call | flops 1000000 | bytes 3000000 | tf_op jit(solution)/shard_map/quarters/pallas_call | solution.py:200
  73.3 1.7 %collective-permute-done.5 = f16[960,128]{1,0:T(8,128)(2,1)S(1)} collective-permute-done((f16[960,128]{1,0:T(8,128)(2,1)S(1)}, f16[960,128]{1,0:T(8,128)(2,1)S(1)}, u32[]{:S(2)}, u32[]{:S(2)}) %collective-permute-start.5) | collective-permute-done | bytes 245792 | tf_op jit(solution)/shard_map/ppermute | solution.py:336
  75.1 0.8 subtract_convert_fusion
  75.9 2.2 %collective-permute-start.7 = (bf16[960,128]{1,0:T(8,128)(2,1)S(1)}, bf16[960,128]{1,0:T(8,128)(2,1)S(1)}, u32[]{:S(2)}, u32[]{:S(2)}) collective-permute-start(bf16[960,128]{1,0:T(8,128)(2,1)S(1)} %get-tuple-element.81.refs_0_), channel_id=1, source_target_pairs={{0,8},{8,16},{16,24},{24,32},{32,40},{40,48},{48,56},{56,0},{1,9},... | collective-permute-start | bytes 737288 | tf_op jit(solution)/shard_map/ppermute | solution.py:336
  78.1 0.8 collective-permute-start.8
  78.9 5.6 %collective-permute-start.13 = (f16[960,128]{1,0:T(8,128)(2,1)S(1)}, f16[960,128]{1,0:T(8,128)(2,1)S(1)}, u32[]{:S(2)}, u32[]{:S(2)}) collective-permute-start(f16[960,128]{1,0:T(8,128)(2,1)S(1)} %get-tuple-element.103), channel_id=1, source_target_pairs={{0,64},{64,128},{128,192},{192,0},{1,65},{65,129},{129,193},{193,1... | collective-permute-start | bytes 737288 | tf_op jit(solution)/shard_map/ppermute | solution.py:336
  84.6 0.7 collective-permute-start.12
  85.3 2.1 %collective-permute-start.11 = (f16[960,128]{1,0:T(8,128)(2,1)S(1)}, f16[960,128]{1,0:T(8,128)(2,1)S(1)}, u32[]{:S(2)}, u32[]{:S(2)}) collective-permute-start(f16[960,128]{1,0:T(8,128)(2,1)S(1)} %get-tuple-element.103), channel_id=1, source_target_pairs={{0,192},{64,0},{128,64},{192,128},{1,193},{65,1},{129,65},{193,129... | collective-permute-start | bytes 737288 | tf_op jit(solution)/shard_map/ppermute | solution.py:336
  87.3 2.7 %collective-permute-start.10 = (bf16[960,128]{1,0:T(8,128)(2,1)S(1)}, bf16[960,128]{1,0:T(8,128)(2,1)S(1)}, u32[]{:S(2)}, u32[]{:S(2)}) collective-permute-start(bf16[960,128]{1,0:T(8,128)(2,1)S(1)} %collective-permute-done.8.refs_1_), channel_id=1, source_target_pairs={{0,56},{8,0},{16,8},{24,16},{32,24},{40,32},{48,40},{56,48},{1,57}... | collective-permute-start | bytes 737288 | tf_op jit(solution)/shard_map/ppermute | solution.py:336
  90.0 4.7 %collective-permute-done.12 = f16[960,128]{1,0:T(8,128)(2,1)S(1)} collective-permute-done((f16[960,128]{1,0:T(8,128)(2,1)S(1)}, f16[960,128]{1,0:T(8,128)(2,1)S(1)}, u32[]{:S(2)}, u32[]{:S(2)}) %collective-permute-start.12) | collective-permute-done | bytes 245792 | tf_op jit(solution)/shard_map/ppermute | solution.py:336
  94.7 2.8 %fetch.2 = bf16[32,208,128]{2,1,0:T(8,128)(2,1)} custom-call(s32[8,512]{1,0:T(8,128)S(1)} %get-tuple-element.90.ids_ref, bf16[960,128]{1,0:T(8,128)(2,1)S(1)} %get-tuple-element.81.refs_0_, bf16[960,128]{1,0:T(8,128)(2,1)S(1)} %collective-permute-done.8.refs_1_, bf16[960,128]{1,0:T(8,128)(2,1)S(1)} %collective-permute-done.7.refs_2_, ...), custom_call_target="tpu_custom_call" | custom-call | tf_op jit(solution)/shard_map/fetch/pallas_call | solution.py:245
  97.5 9.6 %all-to-all-start.2 = ((bf16[32,208,128]{2,1,0:T(8,128)(2,1)}), bf16[32,208,128]{2,1,0:T(8,128)(2,1)S(1)}, u32[]{:S(2)}, u32[]{:S(2)}) async-start(bf16[32,208,128]{2,1,0:T(8,128)(2,1)} %fetch.2), calls=%async_computation.2 | async-start | bytes 3407872 | tf_op jit(solution)/shard_map/all_to_all | solution.py:360
  107.1 1.0 collective-permute-start.14
  108.1 1.8 %collective-permute-start.15 = (bf16[960,128]{1,0:T(8,128)(2,1)S(1)}, bf16[960,128]{1,0:T(8,128)(2,1)S(1)}, u32[]{:S(2)}, u32[]{:S(2)}) collective-permute-start(bf16[960,128]{1,0:T(8,128)(2,1)S(1)} %collective-permute-done.10.refs_3_), channel_id=1, source_target_pairs={{0,56},{8,0},{16,8},{24,16},{32,24},{40,32},{48,40},{56,48},{1,57}... | collective-permute-start | bytes 737288 | tf_op jit(solution)/shard_map/ppermute | solution.py:336
  109.9 5.9 %collective-permute-done.14.refs_1_ = bf16[960,128]{1,0:T(8,128)(2,1)S(1)} collective-permute-done((bf16[960,128]{1,0:T(8,128)(2,1)S(1)}, bf16[960,128]{1,0:T(8,128)(2,1)S(1)}, u32[]{:S(2)}, u32[]{:S(2)}) %collective-permute-start.14) | collective-permute-done | bytes 245792 | tf_op jit(solution)/shard_map/ppermute | solution.py:336
  115.7 0.9 collective-permute-start.16
  116.6 6.8 %collective-permute-done.16.refs_2_ = bf16[960,128]{1,0:T(8,128)(2,1)S(1)} collective-permute-done((bf16[960,128]{1,0:T(8,128)(2,1)S(1)}, bf16[960,128]{1,0:T(8,128)(2,1)S(1)}, u32[]{:S(2)}, u32[]{:S(2)}) %collective-permute-start.16) | collective-permute-done | bytes 245792 | tf_op jit(solution)/shard_map/ppermute | solution.py:336
  123.3 2.1 %fetch.3 = bf16[32,128,128]{2,1,0:T(8,128)(2,1)} custom-call(s32[8,512]{1,0:T(8,128)S(1)} %get-tuple-element.90.ids_ref, bf16[960,128]{1,0:T(8,128)(2,1)S(1)} %collective-permute-done.15.refs_0_, bf16[960,128]{1,0:T(8,128)(2,1)S(1)} %collective-permute-done.14.refs_1_, bf16[960,128]{1,0:T(8,128)(2,1)S(1)} %collective-permute-done.16.refs_2_), custom_call_target="tpu_custom_call" | custom-call | tf_op jit(solution)/shard_map/fetch/pallas_call | solution.py:245
  125.4 5.2 %all-to-all-done.2 = bf16[32,208,128]{2,1,0:T(8,128)(2,1)S(1)} async-done(((bf16[32,208,128]{2,1,0:T(8,128)(2,1)}), bf16[32,208,128]{2,1,0:T(8,128)(2,1)S(1)}, u32[]{:S(2)}, u32[]{:S(2)}) %all-to-all-start.2) | async-done | bytes 1703968 | tf_op jit(solution)/shard_map/all_to_all | solution.py:360
  130.6 5.7 %all-to-all-start.3 = ((bf16[32,128,128]{2,1,0:T(8,128)(2,1)}), bf16[32,128,128]{2,1,0:T(8,128)(2,1)S(1)}, u32[]{:S(2)}, u32[]{:S(2)}) async-start(bf16[32,128,128]{2,1,0:T(8,128)(2,1)} %fetch.3), calls=%async_computation.3 | async-start | bytes 2097152 | tf_op jit(solution)/shard_map/all_to_all | solution.py:360
  136.4 1.0 fusion.20
  137.6 6.3 %full_rows.1 = (f32[2,192,1280]{2,1,0:T(8,128)}, f32[2,192,1280]{2,1,0:T(8,128)}, f32[2,192,1280]{2,1,0:T(8,128)}) custom-call(s32[1]{0:T(128)} %bitcast.y_ref, f32[5,192,128]{2,1,0:T(8,128)S(1)} %bitcast.22, f32[5,192,128]{2,1,0:T(8,128)S(1)} %bitcast.23, f32[5,192,128]{2,1,0:T(8,128)S(1)} %bitcast.24, f32[5,192,128]{2,1,0:T(8,128)S(1)} %bitcast.25, ...), custom_call_target="tpu_custom_call" | custom-call | flops 10000000 | bytes 14000000 | tf_op jit(solution)/shard_map/full_rows/pallas_call | solution.py:314
  143.9 9.7 %all-to-all-done.3 = bf16[32,128,128]{2,1,0:T(8,128)(2,1)S(1)} async-done(((bf16[32,128,128]{2,1,0:T(8,128)(2,1)}), bf16[32,128,128]{2,1,0:T(8,128)(2,1)S(1)}, u32[]{:S(2)}, u32[]{:S(2)}) %all-to-all-start.3) | async-done | bytes 1048608 | tf_op jit(solution)/shard_map/all_to_all | solution.py:360
  153.6 2.4 %unpack.1 = bf16[8,8,16,1280]{3,2,1,0:T(8,128)(2,1)} custom-call(s32[1]{0:T(128)} %bitcast.1.z_ref, bf16[4,8,208,128]{3,2,1,0:T(8,128)(2,1)S(1)} %bitcast.20, bf16[4,8,128,128]{3,2,1,0:T(8,128)(2,1)S(1)} %bitcast.21), custom_call_target="tpu_custom_call" | custom-call | tf_op jit(solution)/shard_map/unpack/pallas_call | solution.py:274
  (22 shorter events, 0.4 us)
Async XLA Ops:
  3.2 25.8 %all-to-all-start.1 = ((bf16[32,128,128]{2,1,0:T(8,128)(2,1)}), bf16[32,128,128]{2,1,0:T(8,128)(2,1)S(1)}, u32[]{:S(2)}, u32[]{:S(2)}) async-start(bf16[32,128,128]{2,1,0:T(8,128)(2,1)} %bitcast.38), calls=%async_computation.1 | async-start | bytes 2097152 | tf_op jit(solution)/shard_map/all_to_all | solution.py:360
  29.0 27.6 %all-to-all-start = ((bf16[32,208,128]{2,1,0:T(8,128)(2,1)}), bf16[32,208,128]{2,1,0:T(8,128)(2,1)S(1)}, u32[]{:S(2)}, u32[]{:S(2)}) async-start(bf16[32,208,128]{2,1,0:T(8,128)(2,1)} %bitcast.37), calls=%async_computation | async-start | bytes 3407872 | tf_op jit(solution)/shard_map/all_to_all | solution.py:360
  34.3 11.7 %collective-permute-start = (f16[960,128]{1,0:T(8,128)(2,1)S(1)}, f16[960,128]{1,0:T(8,128)(2,1)S(1)}, u32[]{:S(2)}, u32[]{:S(2)}) collective-permute-start(f16[960,128]{1,0:T(8,128)(2,1)S(1)} %fusion), channel_id=1, source_target_pairs={{0,8},{8,16},{16,24},{24,32},{32,40},{40,48},{48,56},{56,0},{1,9},... | collective-permute-start | bytes 737288 | tf_op jit(solution)/shard_map/ppermute | solution.py:336
  46.3 7.9 %collective-permute-start.1 = (f16[960,128]{1,0:T(8,128)(2,1)S(1)}, f16[960,128]{1,0:T(8,128)(2,1)S(1)}, u32[]{:S(2)}, u32[]{:S(2)}) collective-permute-start(f16[960,128]{1,0:T(8,128)(2,1)S(1)} %fusion.3), channel_id=1, source_target_pairs={{0,8},{8,16},{16,24},{24,32},{32,40},{40,48},{48,56},{56,0},{1,9},... | collective-permute-start | bytes 737288 | tf_op jit(solution)/shard_map/ppermute | solution.py:336
  46.4 7.8 %collective-permute-start.2 = (f16[960,128]{1,0:T(8,128)(2,1)S(1)}, f16[960,128]{1,0:T(8,128)(2,1)S(1)}, u32[]{:S(2)}, u32[]{:S(2)}) collective-permute-start(f16[960,128]{1,0:T(8,128)(2,1)S(1)} %fusion.4), channel_id=1, source_target_pairs={{0,56},{8,0},{16,8},{24,16},{32,24},{40,32},{48,40},{56,48},{1,57}... | collective-permute-start | bytes 737288 | tf_op jit(solution)/shard_map/ppermute | solution.py:336
  56.6 1.3 copy-start.1
  56.6 1.5 copy-start
  58.4 9.7 %collective-permute-start.3 = (f16[960,128]{1,0:T(8,128)(2,1)S(1)}, f16[960,128]{1,0:T(8,128)(2,1)S(1)}, u32[]{:S(2)}, u32[]{:S(2)}) collective-permute-start(f16[960,128]{1,0:T(8,128)(2,1)S(1)} %fusion.7), channel_id=1, source_target_pairs={{0,8},{8,16},{16,24},{24,32},{32,40},{40,48},{48,56},{56,0},{1,9},... | collective-permute-start | bytes 737288 | tf_op jit(solution)/shard_map/ppermute | solution.py:336
  60.1 8.0 %collective-permute-start.4 = (f16[960,128]{1,0:T(8,128)(2,1)S(1)}, f16[960,128]{1,0:T(8,128)(2,1)S(1)}, u32[]{:S(2)}, u32[]{:S(2)}) collective-permute-start(f16[960,128]{1,0:T(8,128)(2,1)S(1)} %fusion.8), channel_id=1, source_target_pairs={{0,56},{8,0},{16,8},{24,16},{32,24},{40,32},{48,40},{56,48},{1,57}... | collective-permute-start | bytes 737288 | tf_op jit(solution)/shard_map/ppermute | solution.py:336
  68.7 6.3 %collective-permute-start.5 = (f16[960,128]{1,0:T(8,128)(2,1)S(1)}, f16[960,128]{1,0:T(8,128)(2,1)S(1)}, u32[]{:S(2)}, u32[]{:S(2)}) collective-permute-start(f16[960,128]{1,0:T(8,128)(2,1)S(1)} %fusion.11), channel_id=1, source_target_pairs={{0,8},{8,16},{16,24},{24,32},{32,40},{40,48},{48,56},{56,0},{1,9},... | collective-permute-start | bytes 737288 | tf_op jit(solution)/shard_map/ppermute | solution.py:336
  68.8 6.2 %collective-permute-start.6 = (f16[960,128]{1,0:T(8,128)(2,1)S(1)}, f16[960,128]{1,0:T(8,128)(2,1)S(1)}, u32[]{:S(2)}, u32[]{:S(2)}) collective-permute-start(f16[960,128]{1,0:T(8,128)(2,1)S(1)} %fusion.14), channel_id=1, source_target_pairs={{0,56},{8,0},{16,8},{24,16},{32,24},{40,32},{48,40},{56,48},{1,57}... | collective-permute-start | bytes 737288 | tf_op jit(solution)/shard_map/ppermute | solution.py:336
  75.9 11.4 %collective-permute-start.7 = (bf16[960,128]{1,0:T(8,128)(2,1)S(1)}, bf16[960,128]{1,0:T(8,128)(2,1)S(1)}, u32[]{:S(2)}, u32[]{:S(2)}) collective-permute-start(bf16[960,128]{1,0:T(8,128)(2,1)S(1)} %get-tuple-element.81.refs_0_), channel_id=1, source_target_pairs={{0,8},{8,16},{16,24},{24,32},{32,40},{40,48},{48,56},{56,0},{1,9},... | collective-permute-start | bytes 737288 | tf_op jit(solution)/shard_map/ppermute | solution.py:336
  78.1 9.2 %collective-permute-start.8 = (bf16[960,128]{1,0:T(8,128)(2,1)S(1)}, bf16[960,128]{1,0:T(8,128)(2,1)S(1)}, u32[]{:S(2)}, u32[]{:S(2)}) collective-permute-start(bf16[960,128]{1,0:T(8,128)(2,1)S(1)} %get-tuple-element.81.refs_0_), channel_id=1, source_target_pairs={{0,56},{8,0},{16,8},{24,16},{32,24},{40,32},{48,40},{56,48},{1,57}... | collective-permute-start | bytes 737288 | tf_op jit(solution)/shard_map/ppermute | solution.py:336
  78.9 11.1 %collective-permute-start.13 = (f16[960,128]{1,0:T(8,128)(2,1)S(1)}, f16[960,128]{1,0:T(8,128)(2,1)S(1)}, u32[]{:S(2)}, u32[]{:S(2)}) collective-permute-start(f16[960,128]{1,0:T(8,128)(2,1)S(1)} %get-tuple-element.103), channel_id=1, source_target_pairs={{0,64},{64,128},{128,192},{192,0},{1,65},{65,129},{129,193},{193,1... | collective-permute-start | bytes 737288 | tf_op jit(solution)/shard_map/ppermute | solution.py:336
  84.6 10.1 %collective-permute-start.12 = (f16[960,128]{1,0:T(8,128)(2,1)S(1)}, f16[960,128]{1,0:T(8,128)(2,1)S(1)}, u32[]{:S(2)}, u32[]{:S(2)}) collective-permute-start(f16[960,128]{1,0:T(8,128)(2,1)S(1)} %get-tuple-element.103), channel_id=1, source_target_pairs={{0,128},{64,192},{128,0},{192,64},{1,129},{65,193},{129,1},{193,65... | collective-permute-start | bytes 737288 | tf_op jit(solution)/shard_map/ppermute | solution.py:336
  85.3 9.4 %collective-permute-start.11 = (f16[960,128]{1,0:T(8,128)(2,1)S(1)}, f16[960,128]{1,0:T(8,128)(2,1)S(1)}, u32[]{:S(2)}, u32[]{:S(2)}) collective-permute-start(f16[960,128]{1,0:T(8,128)(2,1)S(1)} %get-tuple-element.103), channel_id=1, source_target_pairs={{0,192},{64,0},{128,64},{192,128},{1,193},{65,1},{129,65},{193,129... | collective-permute-start | bytes 737288 | tf_op jit(solution)/shard_map/ppermute | solution.py:336
  87.3 7.4 %collective-permute-start.9 = (bf16[960,128]{1,0:T(8,128)(2,1)S(1)}, bf16[960,128]{1,0:T(8,128)(2,1)S(1)}, u32[]{:S(2)}, u32[]{:S(2)}) collective-permute-start(bf16[960,128]{1,0:T(8,128)(2,1)S(1)} %collective-permute-done.7.refs_2_), channel_id=1, source_target_pairs={{0,8},{8,16},{16,24},{24,32},{32,40},{40,48},{48,56},{56,0},{1,9},... | collective-permute-start | bytes 737288 | tf_op jit(solution)/shard_map/ppermute | solution.py:336
  87.3 7.4 %collective-permute-start.10 = (bf16[960,128]{1,0:T(8,128)(2,1)S(1)}, bf16[960,128]{1,0:T(8,128)(2,1)S(1)}, u32[]{:S(2)}, u32[]{:S(2)}) collective-permute-start(bf16[960,128]{1,0:T(8,128)(2,1)S(1)} %collective-permute-done.8.refs_1_), channel_id=1, source_target_pairs={{0,56},{8,0},{16,8},{24,16},{32,24},{40,32},{48,40},{56,48},{1,57}... | collective-permute-start | bytes 737288 | tf_op jit(solution)/shard_map/ppermute | solution.py:336
  94.7 2.8 %copy-start.2 = (f16[960,128]{1,0:T(8,128)(2,1)}, f16[960,128]{1,0:T(8,128)(2,1)S(1)}, u32[]{:S(2)}) copy-start(f16[960,128]{1,0:T(8,128)(2,1)S(1)} %collective-permute-done.11) | copy-start | bytes 737284
  97.5 33.1 %all-to-all-start.2 = ((bf16[32,208,128]{2,1,0:T(8,128)(2,1)}), bf16[32,208,128]{2,1,0:T(8,128)(2,1)S(1)}, u32[]{:S(2)}, u32[]{:S(2)}) async-start(bf16[32,208,128]{2,1,0:T(8,128)(2,1)} %fetch.2), calls=%async_computation.2 | async-start | bytes 3407872 | tf_op jit(solution)/shard_map/all_to_all | solution.py:360
  107.1 8.6 %collective-permute-start.14 = (bf16[960,128]{1,0:T(8,128)(2,1)S(1)}, bf16[960,128]{1,0:T(8,128)(2,1)S(1)}, u32[]{:S(2)}, u32[]{:S(2)}) collective-permute-start(bf16[960,128]{1,0:T(8,128)(2,1)S(1)} %collective-permute-done.9.refs_4_), channel_id=1, source_target_pairs={{0,8},{8,16},{16,24},{24,32},{32,40},{40,48},{48,56},{56,0},{1,9},... | collective-permute-start | bytes 737288 | tf_op jit(solution)/shard_map/ppermute | solution.py:336
  108.1 7.6 %collective-permute-start.15 = (bf16[960,128]{1,0:T(8,128)(2,1)S(1)}, bf16[960,128]{1,0:T(8,128)(2,1)S(1)}, u32[]{:S(2)}, u32[]{:S(2)}) collective-permute-start(bf16[960,128]{1,0:T(8,128)(2,1)S(1)} %collective-permute-done.10.refs_3_), channel_id=1, source_target_pairs={{0,56},{8,0},{16,8},{24,16},{32,24},{40,32},{48,40},{56,48},{1,57}... | collective-permute-start | bytes 737288 | tf_op jit(solution)/shard_map/ppermute | solution.py:336
  115.7 7.6 %collective-permute-start.16 = (bf16[960,128]{1,0:T(8,128)(2,1)S(1)}, bf16[960,128]{1,0:T(8,128)(2,1)S(1)}, u32[]{:S(2)}, u32[]{:S(2)}) collective-permute-start(bf16[960,128]{1,0:T(8,128)(2,1)S(1)} %collective-permute-done.14.refs_1_), channel_id=1, source_target_pairs={{0,8},{8,16},{16,24},{24,32},{32,40},{40,48},{48,56},{56,0},{1,9},... | collective-permute-start | bytes 737288 | tf_op jit(solution)/shard_map/ppermute | solution.py:336
  130.6 23.0 %all-to-all-start.3 = ((bf16[32,128,128]{2,1,0:T(8,128)(2,1)}), bf16[32,128,128]{2,1,0:T(8,128)(2,1)S(1)}, u32[]{:S(2)}, u32[]{:S(2)}) async-start(bf16[32,128,128]{2,1,0:T(8,128)(2,1)} %fetch.3), calls=%async_computation.3 | async-start | bytes 2097152 | tf_op jit(solution)/shard_map/all_to_all | solution.py:360

commit v3 on v2

--- a/solution.py
+++ b/solution.py
@@ -13,7 +13,7 @@
 BF = jnp.bfloat16
 F32 = jnp.float32
 F16 = jnp.float16
-SLAB = ("y", "x", "c")
+SLAB = ("x", "c", "y")
 GROUP = 32
 NZ = 8
 NY = 4
@@ -46,6 +46,14 @@
         jnp.where(low, pltpu.roll(a, 64, axis), b),
         jnp.where(low, a, pltpu.roll(b, 64, axis)),
     )
+
+
+def centred(rows):
+    return (rows.astype(F32) - HALF).astype(BF)
+
+
+def one_hot(rows, ids):
+    return jnp.where(rows == ids, jnp.ones((), BF), jnp.zeros((), BF))
 
 
 def params(mib):
@@ -90,8 +98,8 @@
                     rest = jnp.where(sub == 4 * t + r, row, rest)
         for y in range(NY):
             for p in range(n):
-                o_ref[y, u, pl.ds(p * CAP, CAP), :] = blocks[p][0, u, :, pl.ds(y * LANES, LANES)]
-                o_ref[y, u, pl.ds((n + p) * CAP, CAP), :] = blocks[p][0, u, :, pl.ds(512 + y * LANES, LANES)]
+                o_ref[u, y, pl.ds(p * CAP, CAP), :] = blocks[p][0, u, :, pl.ds(y * LANES, LANES)]
+                o_ref[u, y, pl.ds((n + p) * CAP, CAP), :] = blocks[p][0, u, :, pl.ds(512 + y * LANES, LANES)]
             cols = pl.ds(1024 + (y // 2) * LANES, LANES)
             for t in range((n + 1) // 2):
                 a = blocks[2 * t][0, u, :, cols].astype(F32)
@@ -99,7 +107,7 @@
                     tile = pair(a, blocks[2 * t + 1][0, u, :, cols].astype(F32), y % 2 == 1)
                 else:
                     tile = jnp.where(low_lanes(a.shape), pltpu.roll(a, 64, 1) if y % 2 else a, rest)
-                o_ref[y, u, pl.ds((2 * n + t) * CAP, CAP), :] = tile.astype(BF)
+                o_ref[u, y, pl.ds((2 * n + t) * CAP, CAP), :] = tile.astype(BF)
 
 
 def pack(z, ks, grad_rows, ids=()):
@@ -114,9 +122,9 @@
             num_scalar_prefetch=1,
             grid=(XC // step,),
             in_specs=[block(k) for k in ks] + [whole for _ in ids],
-            out_specs=pl.BlockSpec((NY, step, rows, LANES), lambda i, s: (0, i, 0, 0)),
+            out_specs=pl.BlockSpec((step, NY, rows, LANES), lambda i, s: (i, 0, 0, 0)),
         ),
-        out_shape=pltpu.HBM((NY, XC, rows, LANES), BF),
+        out_shape=pltpu.HBM((XC, NY, rows, LANES), BF),
         compiler_params=params(14),
         cost_estimate=pl.CostEstimate(flops=0, bytes_accessed=700_000 * n, transcendentals=0),
         name="pack",
@@ -148,9 +156,9 @@
         read_ids(z_ref, got_ref, (2 * n + n // 2) * CAP, refs[1 + n :])
     else:
         got_ref, ids_ref, outs = refs[0], refs[1], refs[2:]
-    rows = lax.broadcasted_iota(jnp.int32, (ROWS, GROUP * CAP), 0)
+    rows = centred(lax.broadcasted_iota(jnp.int32, (ROWS, GROUP * CAP), 0))
     for p, k in enumerate(ks):
-        pick = jnp.where(rows == ids_ref[pl.ds(k, 1), :], 1.0, 0.0).astype(BF)
+        pick = one_hot(rows, centred(ids_ref[pl.ds(k, 1), :]))
         slots = jnp.concatenate(
             [
                 got_ref[:, pl.ds(at * CAP, CAP), :].reshape(GROUP * CAP, LANES)
@@ -215,12 +223,12 @@
 def fetch_kernel(ks, ids_ref, *refs):
     n = len(ks)
     tables, o_ref = refs[:n], refs[n]
-    rows = lax.broadcasted_iota(jnp.int32, (GROUP * CAP, ROWS), 1).astype(F32)
-    columns = jnp.transpose(ids_ref[...].astype(F32))
+    rows = centred(lax.broadcasted_iota(jnp.int32, (GROUP * CAP, ROWS), 1))
+    columns = jnp.transpose(ids_ref[...].astype(F32) - HALF).astype(BF)
     low = low_lanes((GROUP, CAP, LANES))
     even = None
     for p, k in enumerate(ks):
-        pick = jnp.where(rows == columns[:, k : k + 1], 1.0, 0.0).astype(BF)
+        pick = one_hot(rows, columns[:, k : k + 1])
         table = tables[p]
         last = table[pl.ds(2 * ROWS, HALF), :]
         moved = pltpu.roll(last.astype(F32), 64, 1).astype(BF)
@@ -252,40 +260,42 @@
     )(ids, *[tables[k] for k in ks])
 
 
-def unpack_kernel(chunks, step, z_ref, *refs):
-    o_ref = refs[-1]
-    for ks, g_ref in zip(chunks, refs):
-        n = len(ks)
-        for p, k in enumerate(ks):
-            z = (z_ref[0] + k) % NZ
-            for u in range(step):
-                for y in range(NY):
-                    o_ref[z, u, :, pl.ds(y * LANES, LANES)] = g_ref[y, u, pl.ds(p * CAP, CAP), :]
-                    o_ref[z, u, :, pl.ds(512 + y * LANES, LANES)] = g_ref[y, u, pl.ds((n + p) * CAP, CAP), :]
-                at = pl.ds((2 * n + p // 2) * CAP, CAP)
-                for t in range(2):
-                    a = g_ref[2 * t, u, at, :].astype(F32)
-                    b = g_ref[2 * t + 1, u, at, :].astype(F32)
-                    o_ref[z, u, :, pl.ds(1024 + t * LANES, LANES)] = pair(a, b, p % 2 == 1).astype(BF)
-
-
-def unpack(z, chunks, backs):
-    step = 2
-    out = pl.pallas_call(
-        functools.partial(unpack_kernel, chunks, step),
-        grid_spec=pltpu.PrefetchScalarGridSpec(
-            num_scalar_prefetch=1,
-            grid=(XC // step,),
-            in_specs=[
-                pl.BlockSpec((NY, step, chunk_rows(len(ks)), LANES), lambda i, s: (0, i, 0, 0)) for ks in chunks
-            ],
-            out_specs=pl.BlockSpec((NZ, step, CAP, 1280), lambda i, s: (0, i, 0, 0)),
-        ),
-        out_shape=pltpu.HBM((NZ, XC, CAP, 1280), BF),
-        compiler_params=params(12),
+def unpack_kernel(ks, z_ref, g_ref, *refs):
+    o_ref, block_ref, sems = refs[-3:]
+    n = len(ks)
+    copies = []
+    for p, k in enumerate(ks):
+        for u in range(XC):
+            rows = pl.ds(u * CAP, CAP)
+            get = lambda y, at: g_ref[u * NY + y, pl.ds(at * CAP, CAP), :]
+            for y in range(NY):
+                block_ref[p, rows, pl.ds(y * LANES, LANES)] = get(y, p)
+                block_ref[p, rows, pl.ds(512 + y * LANES, LANES)] = get(y, n + p)
+            for t in range(2):
+                a = get(2 * t, 2 * n + p // 2).astype(F32)
+                b = get(2 * t + 1, 2 * n + p // 2).astype(F32)
+                block_ref[p, rows, pl.ds(1024 + t * LANES, LANES)] = pair(a, b, p % 2 == 1).astype(BF)
+        copies.append(pltpu.make_async_copy(block_ref.at[p], o_ref.at[(z_ref[0] + k) % NZ], sems.at[p]))
+        copies[-1].start()
+    for copy in copies:
+        copy.wait()
+
+
+def unpack(z, ks, back, into=None):
+    n = len(ks)
+    hbm_spec = pl.BlockSpec(memory_space=pltpu.HBM)
+    return pl.pallas_call(
+        functools.partial(unpack_kernel, ks),
+        in_specs=[pl.BlockSpec(memory_space=pltpu.SMEM), pl.BlockSpec(memory_space=pltpu.VMEM)]
+        + ([] if into is None else [hbm_spec]),
+        out_specs=hbm_spec,
+        out_shape=pltpu.HBM((NZ, XC * CAP, 1280), BF),
+        input_output_aliases={} if into is None else {2: 0},
+        scratch_shapes=[pltpu.VMEM((n, XC * CAP, 1280), BF), pltpu.SemaphoreType.DMA((n,))],
+        compiler_params=params(8),
+        cost_estimate=pl.CostEstimate(flops=0, bytes_accessed=700_000 * n, transcendentals=0),
         name="unpack",
-    )(z, *[b.reshape(NY, XC, -1, LANES) for b in backs])
-    return out.reshape(NZ * XC * CAP, 1280)
+    )(z, back, *(() if into is None else (into,)))
 
 
 FULL_STEP = 48
@@ -390,10 +400,11 @@
     back = swap(found)
     tables[5], tables[3] = both_ways(tables[6], tables[2])
     tables[4] = along(tables[5], "z", NZ, 1)
-    back, found = lax.optimization_barrier((back, fetch(LATER, wanted, tables)))
+    back, found, *grads = lax.optimization_barrier((back, fetch(LATER, wanted, tables), *grads))
     backs = [back, swap(found)]
     outs = full_rows(y, [decoded(g) for g in grads], table_rows, first_moment, second_moment)
-    return (*outs, unpack(z, (FIRST, LATER), backs))
+    fetched = unpack(z, LATER, backs[1], unpack(z, FIRST, backs[0]))
+    return (*outs, fetched.reshape(NZ * XC * CAP, 1280))
 
 
 def solution(mesh):

time: 157 us -> 152 us (0.968)
  starting transfers between devices: 58.6 us -> 55.1 us
  other arithmetic: 5.02 us -> 3.15 us
  local copies, waits for them, and re-layouts: 0.01 us -> 1.68 us
    ppermute x17, starting transfers between devices: 30.6 us -> 25.8 us  [along(): lax.ppermute(value, axis, [(i, (i + step) % size) for i in range(size)])]
    ppermute x17, waiting for transfers between devices: 37.9 us -> 41.1 us  [along(): lax.ppermute(value, axis, [(i, (i + step) % size) for i in range(size)])]
    all_to_all x4, waiting for transfers between devices: 30.6 us -> 27.5 us  [swap(): return lax.all_to_all(x, SLAB, split_axis=0, concat_axis=0, tiled=True)]
    mul x5, other arithmetic: 2.29 us -> 0.4 us  [decoded(): return wide * jnp.abs(wide) * (1.0 / 65536.0)]
    unnamed x6 -> x14, local copies, waits for them, and re-layouts: 0.01 us -> 1.68 us
  transfers between devices with their start and end apart: 21 -> 21, of which waited for: 11 -> 13; matrix products, arithmetic and copies ran while one was open for 2% -> 1% of each run, Pallas kernels for 9% -> 9%
where the time goes in v3:
time: 152 us; the launch traced here: 151 us
  waiting for transfers between devices  68.6 us (45%)
  starting transfers between devices  55.1 us (36%)
  Pallas kernels  21.7 us (14%)
  other arithmetic  3.15 us (2%)
  local copies, waits for them, and re-layouts  1.68 us (1%)
    ppermute x17, waiting for transfers between devices, along(): lax.ppermute(value, axis, [(i, (i + step) % size) for i in range(size)])  41.1 us
    all_to_all x4, starting transfers between devices, swap(): return lax.all_to_all(x, SLAB, split_axis=0, concat_axis=0, tiled=True)  29.3 us
    all_to_all x4, waiting for transfers between devices, swap(): return lax.all_to_all(x, SLAB, split_axis=0, concat_axis=0, tiled=True)  27.5 us
    ppermute x17, starting transfers between devices, along(): lax.ppermute(value, axis, [(i, (i + step) % size) for i in range(size)])  25.8 us
    pallas_call x1, Pallas kernels, full_rows(): pl.pallas_call(full_kernel, grid_spec=pltpu.PrefetchScalarGridSpec(num_sc...  6.33 us
    pallas_call x2, Pallas kernels, pack(): pl.pallas_call(functools.partial(pack_kernel, n, step, bool(ids)), grid_s...  5.08 us
    pallas_call x2, Pallas kernels, fetch(): pl.pallas_call(functools.partial(fetch_kernel, ks), in_specs=[vmem] * (1...  3.74 us
  transfers between devices with their start and end apart: 21, of which 13 were waited for; matrix products, arithmetic and copies ran while one was open for 1% of the time, Pallas kernels for 9%

profile of v3, /device:TPU:1, one launch (start us, length us, event | category | flops | bytes accessed | tf_op | source)
XLA Modules:
  0.0 151.2 jit_solution(949315262770614079)
XLA Ops:
  0.6 2.5 %pack.2 = bf16[8,4,128,128]{3,2,1,0:T(8,128)(2,1)} custom-call(s32[1]{0:T(128)} %bitcast.1.z_ref, bf16[8,8,16,1280]{3,2,1,0:T(8,128)(2,1)} %bitcast.22, bf16[8,8,16,1280]{3,2,1,0:T(8,128)(2,1)} %bitcast.23, bf16[8,8,16,1280]{3,2,1,0:T(8,128)(2,1)} %bitcast.24, s32[8,128]{1,0:T(8,128)} %bitcast.36, s32[8,128]{1,0:T(8,128)} %bitcast.37), custom_call_target="tpu_custom_call" | custom-call | bytes 2100000 | tf_op jit(solution)/shard_map/pack/pallas_call | solution.py:119
  3.1 8.6 %all-to-all-start = ((bf16[32,128,128]{2,1,0:T(8,128)(2,1)}), bf16[32,128,128]{2,1,0:T(8,128)(2,1)S(1)}, u32[]{:S(2)}, u32[]{:S(2)}) async-start(bf16[32,128,128]{2,1,0:T(8,128)(2,1)} %bitcast.35), calls=%async_computation | async-start | bytes 2097152 | tf_op jit(solution)/shard_map/all_to_all | solution.py:370
  11.7 2.6 %pack.3 = bf16[8,4,208,128]{3,2,1,0:T(8,128)(2,1)} custom-call(s32[1]{0:T(128)} %bitcast.1.z_ref, bf16[8,8,16,1280]{3,2,1,0:T(8,128)(2,1)} %bitcast.25, bf16[8,8,16,1280]{3,2,1,0:T(8,128)(2,1)} %bitcast.26, bf16[8,8,16,1280]{3,2,1,0:T(8,128)(2,1)} %bitcast.27, bf16[8,8,16,1280]{3,2,1,0:T(8,128)(2,1)} %bitcast.28, bf16[8,8,16,1280]{3,2,1,0:T(8,128)(2,1)} %bitcast.29), custom_call_target="tpu_custom_call" | custom-call | bytes 3500000 | tf_op jit(solution)/shard_map/pack/pallas_call | solution.py:119
  14.3 13.7 %all-to-all-done.refs_0_ = bf16[32,128,128]{2,1,0:T(8,128)(2,1)S(1)} async-done(((bf16[32,128,128]{2,1,0:T(8,128)(2,1)}), bf16[32,128,128]{2,1,0:T(8,128)(2,1)S(1)}, u32[]{:S(2)}, u32[]{:S(2)}) %all-to-all-start) | async-done | bytes 1048608 | tf_op jit(solution)/shard_map/all_to_all | solution.py:370
  28.0 4.7 %all-to-all-start.1 = ((bf16[32,208,128]{2,1,0:T(8,128)(2,1)}), bf16[32,208,128]{2,1,0:T(8,128)(2,1)S(1)}, u32[]{:S(2)}, u32[]{:S(2)}) async-start(bf16[32,208,128]{2,1,0:T(8,128)(2,1)} %bitcast.34), calls=%async_computation.1 | async-start | bytes 3407872 | tf_op jit(solution)/shard_map/all_to_all | solution.py:370
  32.7 1.1 partial_sums.2
  34.0 1.7 %collective-permute-start = (f16[960,128]{1,0:T(8,128)(2,1)S(1)}, f16[960,128]{1,0:T(8,128)(2,1)S(1)}, u32[]{:S(2)}, u32[]{:S(2)}) collective-permute-start(f16[960,128]{1,0:T(8,128)(2,1)S(1)} %fusion), channel_id=1, source_target_pairs={{0,8},{8,16},{16,24},{24,32},{32,40},{40,48},{48,56},{56,0},{1,9},... | collective-permute-start | bytes 737288 | tf_op jit(solution)/shard_map/ppermute | solution.py:346
  36.0 9.8 %collective-permute-done = f16[960,128]{1,0:T(8,128)(2,1)S(1)} collective-permute-done((f16[960,128]{1,0:T(8,128)(2,1)S(1)}, f16[960,128]{1,0:T(8,128)(2,1)S(1)}, u32[]{:S(2)}, u32[]{:S(2)}) %collective-permute-start) | collective-permute-done | bytes 245792 | tf_op jit(solution)/shard_map/ppermute | solution.py:346
  45.8 0.3 fusion.3
  46.2 2.7 %collective-permute-start.2 = (f16[960,128]{1,0:T(8,128)(2,1)S(1)}, f16[960,128]{1,0:T(8,128)(2,1)S(1)}, u32[]{:S(2)}, u32[]{:S(2)}) collective-permute-start(f16[960,128]{1,0:T(8,128)(2,1)S(1)} %fusion.4), channel_id=1, source_target_pairs={{0,56},{8,0},{16,8},{24,16},{32,24},{40,32},{48,40},{56,48},{1,57}... | collective-permute-start | bytes 737288 | tf_op jit(solution)/shard_map/ppermute | solution.py:346
  48.8 5.2 %collective-permute-done.1 = f16[960,128]{1,0:T(8,128)(2,1)S(1)} collective-permute-done((f16[960,128]{1,0:T(8,128)(2,1)S(1)}, f16[960,128]{1,0:T(8,128)(2,1)S(1)}, u32[]{:S(2)}, u32[]{:S(2)}) %collective-permute-start.1) | collective-permute-done | bytes 245792 | tf_op jit(solution)/shard_map/ppermute | solution.py:346
  54.2 1.5 %all-to-all-done.1.refs_0_ = bf16[32,208,128]{2,1,0:T(8,128)(2,1)S(1)} async-done(((bf16[32,208,128]{2,1,0:T(8,128)(2,1)}), bf16[32,208,128]{2,1,0:T(8,128)(2,1)S(1)}, u32[]{:S(2)}, u32[]{:S(2)}) %all-to-all-start.1) | async-done | bytes 1703968 | tf_op jit(solution)/shard_map/all_to_all | solution.py:370
  55.7 1.2 partial_sums.3
  56.9 0.3 fusion.8
  57.2 0.3 fusion.7
  57.4 1.7 %collective-permute-start.3 = (f16[960,128]{1,0:T(8,128)(2,1)S(1)}, f16[960,128]{1,0:T(8,128)(2,1)S(1)}, u32[]{:S(2)}, u32[]{:S(2)}) collective-permute-start(f16[960,128]{1,0:T(8,128)(2,1)S(1)} %fusion.7), channel_id=1, source_target_pairs={{0,8},{8,16},{16,24},{24,32},{32,40},{40,48},{48,56},{56,0},{1,9},... | collective-permute-start | bytes 737288 | tf_op jit(solution)/shard_map/ppermute | solution.py:346
  59.2 4.0 %collective-permute-start.4 = (f16[960,128]{1,0:T(8,128)(2,1)S(1)}, f16[960,128]{1,0:T(8,128)(2,1)S(1)}, u32[]{:S(2)}, u32[]{:S(2)}) collective-permute-start(f16[960,128]{1,0:T(8,128)(2,1)S(1)} %fusion.8), channel_id=1, source_target_pairs={{0,56},{8,0},{16,8},{24,16},{32,24},{40,32},{48,40},{56,48},{1,57}... | collective-permute-start | bytes 737288 | tf_op jit(solution)/shard_map/ppermute | solution.py:346
  63.2 4.7 %collective-permute-done.3 = f16[960,128]{1,0:T(8,128)(2,1)S(1)} collective-permute-done((f16[960,128]{1,0:T(8,128)(2,1)S(1)}, f16[960,128]{1,0:T(8,128)(2,1)S(1)}, u32[]{:S(2)}, u32[]{:S(2)}) %collective-permute-start.3) | collective-permute-done | bytes 245792 | tf_op jit(solution)/shard_map/ppermute | solution.py:346
  67.8 0.3 fusion.14
  68.2 0.3 fusion.11
  68.6 2.7 %collective-permute-start.6 = (f16[960,128]{1,0:T(8,128)(2,1)S(1)}, f16[960,128]{1,0:T(8,128)(2,1)S(1)}, u32[]{:S(2)}, u32[]{:S(2)}) collective-permute-start(f16[960,128]{1,0:T(8,128)(2,1)S(1)} %fusion.14), channel_id=1, source_target_pairs={{0,56},{8,0},{16,8},{24,16},{32,24},{40,32},{48,40},{56,48},{1,57}... | collective-permute-start | bytes 737288 | tf_op jit(solution)/shard_map/ppermute | solution.py:346
  71.2 1.8 %quarters.1 = (f32[960,128]{1,0:T(8,128)S(1)}, f32[960,128]{1,0:T(8,128)S(1)}, f32[960,128]{1,0:T(8,128)S(1)}) custom-call(s32[1]{0:T(128)} %bitcast.y_ref, f32[384,1280]{1,0:T(8,128)} %refs_2_.1, f32[384,1280]{1,0:T(8,128)} %refs_2_.1, f32[384,1280]{1,0:T(8,128)} %refs_2_.1, f32[384,1280]{1,0:T(8,128)} %refs_5_.1, f32[384,1280]{1,0:T(8,128)} %refs_5_.1, ...), custom_call_target="tpu_custom_call" | custom-call | flops 1000000 | bytes 3000000 | tf_op jit(solution)/shard_map/quarters/pallas_call | solution.py:208
  73.1 1.7 %collective-permute-done.5 = f16[960,128]{1,0:T(8,128)(2,1)S(1)} collective-permute-done((f16[960,128]{1,0:T(8,128)(2,1)S(1)}, f16[960,128]{1,0:T(8,128)(2,1)S(1)}, u32[]{:S(2)}, u32[]{:S(2)}) %collective-permute-start.5) | collective-permute-done | bytes 245792 | tf_op jit(solution)/shard_map/ppermute | solution.py:346
  74.8 0.8 subtract_convert_fusion
  75.7 2.0 %collective-permute-start.7 = (bf16[960,128]{1,0:T(8,128)(2,1)S(1)}, bf16[960,128]{1,0:T(8,128)(2,1)S(1)}, u32[]{:S(2)}, u32[]{:S(2)}) collective-permute-start(bf16[960,128]{1,0:T(8,128)(2,1)S(1)} %get-tuple-element.86.refs_0_), channel_id=1, source_target_pairs={{0,8},{8,16},{16,24},{24,32},{32,40},{40,48},{48,56},{56,0},{1,9},... | collective-permute-start | bytes 737288 | tf_op jit(solution)/shard_map/ppermute | solution.py:346
  77.6 1.0 collective-permute-start.8
  78.7 2.1 %collective-permute-start.13 = (f16[960,128]{1,0:T(8,128)(2,1)S(1)}, f16[960,128]{1,0:T(8,128)(2,1)S(1)}, u32[]{:S(2)}, u32[]{:S(2)}) collective-permute-start(f16[960,128]{1,0:T(8,128)(2,1)S(1)} %get-tuple-element.101), channel_id=1, source_target_pairs={{0,64},{64,128},{128,192},{192,0},{1,65},{65,129},{129,193},{193,1... | collective-permute-start | bytes 737288 | tf_op jit(solution)/shard_map/ppermute | solution.py:346
  80.8 2.6 %collective-permute-start.12 = (f16[960,128]{1,0:T(8,128)(2,1)S(1)}, f16[960,128]{1,0:T(8,128)(2,1)S(1)}, u32[]{:S(2)}, u32[]{:S(2)}) collective-permute-start(f16[960,128]{1,0:T(8,128)(2,1)S(1)} %get-tuple-element.101), channel_id=1, source_target_pairs={{0,128},{64,192},{128,0},{192,64},{1,129},{65,193},{129,1},{193,65... | collective-permute-start | bytes 737288 | tf_op jit(solution)/shard_map/ppermute | solution.py:346
  83.4 0.8 collective-permute-start.11
  84.3 1.2 collective-permute-start.10
  85.4 0.3 collective-permute-start.9
  85.7 0.4 collective-permute-done.13
  86.1 5.3 %collective-permute-done.12 = f16[960,128]{1,0:T(8,128)(2,1)S(1)} collective-permute-done((f16[960,128]{1,0:T(8,128)(2,1)S(1)}, f16[960,128]{1,0:T(8,128)(2,1)S(1)}, u32[]{:S(2)}, u32[]{:S(2)}) %collective-permute-start.12) | collective-permute-done | bytes 245792 | tf_op jit(solution)/shard_map/ppermute | solution.py:346
  91.4 0.6 collective-permute-done.9.refs_4_
  92.0 2.7 %fetch.2 = bf16[32,208,128]{2,1,0:T(8,128)(2,1)} custom-call(s32[8,512]{1,0:T(8,128)S(1)} %get-tuple-element.57.ids_ref, bf16[960,128]{1,0:T(8,128)(2,1)S(1)} %get-tuple-element.86.refs_0_, bf16[960,128]{1,0:T(8,128)(2,1)S(1)} %collective-permute-done.8.refs_1_, bf16[960,128]{1,0:T(8,128)(2,1)S(1)} %collective-permute-done.7.refs_2_, ...), custom_call_target="tpu_custom_call" | custom-call | tf_op jit(solution)/shard_map/fetch/pallas_call | solution.py:253
  94.7 10.8 %all-to-all-start.2 = ((bf16[32,208,128]{2,1,0:T(8,128)(2,1)}), bf16[32,208,128]{2,1,0:T(8,128)(2,1)S(1)}, u32[]{:S(2)}, u32[]{:S(2)}) async-start(bf16[32,208,128]{2,1,0:T(8,128)(2,1)} %fetch.2), calls=%async_computation.2 | async-start | bytes 3407872 | tf_op jit(solution)/shard_map/all_to_all | solution.py:370
  105.6 2.7 %collective-permute-start.15 = (bf16[960,128]{1,0:T(8,128)(2,1)S(1)}, bf16[960,128]{1,0:T(8,128)(2,1)S(1)}, u32[]{:S(2)}, u32[]{:S(2)}) collective-permute-start(bf16[960,128]{1,0:T(8,128)(2,1)S(1)} %collective-permute-done.10.refs_3_), channel_id=1, source_target_pairs={{0,56},{8,0},{16,8},{24,16},{32,24},{40,32},{48,40},{56,48},{1,57}... | collective-permute-start | bytes 737288 | tf_op jit(solution)/shard_map/ppermute | solution.py:346
  108.3 5.9 %collective-permute-done.14.refs_1_ = bf16[960,128]{1,0:T(8,128)(2,1)S(1)} collective-permute-done((bf16[960,128]{1,0:T(8,128)(2,1)S(1)}, bf16[960,128]{1,0:T(8,128)(2,1)S(1)}, u32[]{:S(2)}, u32[]{:S(2)}) %collective-permute-start.14) | collective-permute-done | bytes 245792 | tf_op jit(solution)/shard_map/ppermute | solution.py:346
  114.1 7.6 %collective-permute-done.16.refs_2_ = bf16[960,128]{1,0:T(8,128)(2,1)S(1)} collective-permute-done((bf16[960,128]{1,0:T(8,128)(2,1)S(1)}, bf16[960,128]{1,0:T(8,128)(2,1)S(1)}, u32[]{:S(2)}, u32[]{:S(2)}) %collective-permute-start.16) | collective-permute-done | bytes 245792 | tf_op jit(solution)/shard_map/ppermute | solution.py:346
  121.7 1.0 fetch.3
  122.8 1.0 copy-done
  123.7 4.7 %all-to-all-done.2.g_ref = bf16[32,208,128]{2,1,0:T(8,128)(2,1)S(1)} async-done(((bf16[32,208,128]{2,1,0:T(8,128)(2,1)}), bf16[32,208,128]{2,1,0:T(8,128)(2,1)S(1)}, u32[]{:S(2)}, u32[]{:S(2)}) %all-to-all-start.2) | async-done | bytes 1703968 | tf_op jit(solution)/shard_map/all_to_all | solution.py:370
  128.4 5.2 %all-to-all-start.3 = ((bf16[32,128,128]{2,1,0:T(8,128)(2,1)}), bf16[32,128,128]{2,1,0:T(8,128)(2,1)S(1)}, u32[]{:S(2)}, u32[]{:S(2)}) async-start(bf16[32,128,128]{2,1,0:T(8,128)(2,1)} %copy-done), calls=%async_computation.3 | async-start | bytes 2097152 | tf_op jit(solution)/shard_map/all_to_all | solution.py:370
  133.7 1.3 unpack.2.refs_0_
  135.3 0.7 copy-done.2
  136.1 6.3 %full_rows.1 = (f32[2,192,1280]{2,1,0:T(8,128)}, f32[2,192,1280]{2,1,0:T(8,128)}, f32[2,192,1280]{2,1,0:T(8,128)}) custom-call(s32[1]{0:T(128)} %bitcast.y_ref, f32[5,192,128]{2,1,0:T(8,128)S(1)} %bitcast.18, f32[5,192,128]{2,1,0:T(8,128)S(1)} %bitcast.19, f32[5,192,128]{2,1,0:T(8,128)S(1)} %bitcast.20, f32[5,192,128]{2,1,0:T(8,128)S(1)} %bitcast.21, ...), custom_call_target="tpu_custom_call" | custom-call | flops 10000000 | bytes 14000000 | tf_op jit(solution)/shard_map/full_rows/pallas_call | solution.py:324
  142.4 7.6 %all-to-all-done.3.g_ref = bf16[32,128,128]{2,1,0:T(8,128)(2,1)S(1)} async-done(((bf16[32,128,128]{2,1,0:T(8,128)(2,1)}), bf16[32,128,128]{2,1,0:T(8,128)(2,1)S(1)}, u32[]{:S(2)}, u32[]{:S(2)}) %all-to-all-start.3) | async-done | bytes 1048608 | tf_op jit(solution)/shard_map/all_to_all | solution.py:370
  150.0 1.1 unpack.3
  (31 shorter events, 1.2 us)
Async XLA Ops:
  3.1 24.9 %all-to-all-start = ((bf16[32,128,128]{2,1,0:T(8,128)(2,1)}), bf16[32,128,128]{2,1,0:T(8,128)(2,1)S(1)}, u32[]{:S(2)}, u32[]{:S(2)}) async-start(bf16[32,128,128]{2,1,0:T(8,128)(2,1)} %bitcast.35), calls=%async_computation | async-start | bytes 2097152 | tf_op jit(solution)/shard_map/all_to_all | solution.py:370
  28.0 27.7 %all-to-all-start.1 = ((bf16[32,208,128]{2,1,0:T(8,128)(2,1)}), bf16[32,208,128]{2,1,0:T(8,128)(2,1)S(1)}, u32[]{:S(2)}, u32[]{:S(2)}) async-start(bf16[32,208,128]{2,1,0:T(8,128)(2,1)} %bitcast.34), calls=%async_computation.1 | async-start | bytes 3407872 | tf_op jit(solution)/shard_map/all_to_all | solution.py:370
  34.0 11.7 %collective-permute-start = (f16[960,128]{1,0:T(8,128)(2,1)S(1)}, f16[960,128]{1,0:T(8,128)(2,1)S(1)}, u32[]{:S(2)}, u32[]{:S(2)}) collective-permute-start(f16[960,128]{1,0:T(8,128)(2,1)S(1)} %fusion), channel_id=1, source_target_pairs={{0,8},{8,16},{16,24},{24,32},{32,40},{40,48},{48,56},{56,0},{1,9},... | collective-permute-start | bytes 737288 | tf_op jit(solution)/shard_map/ppermute | solution.py:346
  46.1 7.9 %collective-permute-start.1 = (f16[960,128]{1,0:T(8,128)(2,1)S(1)}, f16[960,128]{1,0:T(8,128)(2,1)S(1)}, u32[]{:S(2)}, u32[]{:S(2)}) collective-permute-start(f16[960,128]{1,0:T(8,128)(2,1)S(1)} %fusion.3), channel_id=1, source_target_pairs={{0,8},{8,16},{16,24},{24,32},{32,40},{40,48},{48,56},{56,0},{1,9},... | collective-permute-start | bytes 737288 | tf_op jit(solution)/shard_map/ppermute | solution.py:346
  46.2 7.8 %collective-permute-start.2 = (f16[960,128]{1,0:T(8,128)(2,1)S(1)}, f16[960,128]{1,0:T(8,128)(2,1)S(1)}, u32[]{:S(2)}, u32[]{:S(2)}) collective-permute-start(f16[960,128]{1,0:T(8,128)(2,1)S(1)} %fusion.4), channel_id=1, source_target_pairs={{0,56},{8,0},{16,8},{24,16},{32,24},{40,32},{48,40},{56,48},{1,57}... | collective-permute-start | bytes 737288 | tf_op jit(solution)/shard_map/ppermute | solution.py:346
  57.4 10.4 %collective-permute-start.3 = (f16[960,128]{1,0:T(8,128)(2,1)S(1)}, f16[960,128]{1,0:T(8,128)(2,1)S(1)}, u32[]{:S(2)}, u32[]{:S(2)}) collective-permute-start(f16[960,128]{1,0:T(8,128)(2,1)S(1)} %fusion.7), channel_id=1, source_target_pairs={{0,8},{8,16},{16,24},{24,32},{32,40},{40,48},{48,56},{56,0},{1,9},... | collective-permute-start | bytes 737288 | tf_op jit(solution)/shard_map/ppermute | solution.py:346
  59.2 8.7 %collective-permute-start.4 = (f16[960,128]{1,0:T(8,128)(2,1)S(1)}, f16[960,128]{1,0:T(8,128)(2,1)S(1)}, u32[]{:S(2)}, u32[]{:S(2)}) collective-permute-start(f16[960,128]{1,0:T(8,128)(2,1)S(1)} %fusion.8), channel_id=1, source_target_pairs={{0,56},{8,0},{16,8},{24,16},{32,24},{40,32},{48,40},{56,48},{1,57}... | collective-permute-start | bytes 737288 | tf_op jit(solution)/shard_map/ppermute | solution.py:346
  68.5 6.3 %collective-permute-start.5 = (f16[960,128]{1,0:T(8,128)(2,1)S(1)}, f16[960,128]{1,0:T(8,128)(2,1)S(1)}, u32[]{:S(2)}, u32[]{:S(2)}) collective-permute-start(f16[960,128]{1,0:T(8,128)(2,1)S(1)} %fusion.11), channel_id=1, source_target_pairs={{0,8},{8,16},{16,24},{24,32},{32,40},{40,48},{48,56},{56,0},{1,9},... | collective-permute-start | bytes 737288 | tf_op jit(solution)/shard_map/ppermute | solution.py:346
  68.6 6.2 %collective-permute-start.6 = (f16[960,128]{1,0:T(8,128)(2,1)S(1)}, f16[960,128]{1,0:T(8,128)(2,1)S(1)}, u32[]{:S(2)}, u32[]{:S(2)}) collective-permute-start(f16[960,128]{1,0:T(8,128)(2,1)S(1)} %fusion.14), channel_id=1, source_target_pairs={{0,56},{8,0},{16,8},{24,16},{32,24},{40,32},{48,40},{56,48},{1,57}... | collective-permute-start | bytes 737288 | tf_op jit(solution)/shard_map/ppermute | solution.py:346
  75.7 8.6 %collective-permute-start.7 = (bf16[960,128]{1,0:T(8,128)(2,1)S(1)}, bf16[960,128]{1,0:T(8,128)(2,1)S(1)}, u32[]{:S(2)}, u32[]{:S(2)}) collective-permute-start(bf16[960,128]{1,0:T(8,128)(2,1)S(1)} %get-tuple-element.86.refs_0_), channel_id=1, source_target_pairs={{0,8},{8,16},{16,24},{24,32},{32,40},{40,48},{48,56},{56,0},{1,9},... | collective-permute-start | bytes 737288 | tf_op jit(solution)/shard_map/ppermute | solution.py:346
  77.6 6.6 %collective-permute-start.8 = (bf16[960,128]{1,0:T(8,128)(2,1)S(1)}, bf16[960,128]{1,0:T(8,128)(2,1)S(1)}, u32[]{:S(2)}, u32[]{:S(2)}) collective-permute-start(bf16[960,128]{1,0:T(8,128)(2,1)S(1)} %get-tuple-element.86.refs_0_), channel_id=1, source_target_pairs={{0,56},{8,0},{16,8},{24,16},{32,24},{40,32},{48,40},{56,48},{1,57}... | collective-permute-start | bytes 737288 | tf_op jit(solution)/shard_map/ppermute | solution.py:346
  78.7 7.4 %collective-permute-start.13 = (f16[960,128]{1,0:T(8,128)(2,1)S(1)}, f16[960,128]{1,0:T(8,128)(2,1)S(1)}, u32[]{:S(2)}, u32[]{:S(2)}) collective-permute-start(f16[960,128]{1,0:T(8,128)(2,1)S(1)} %get-tuple-element.101), channel_id=1, source_target_pairs={{0,64},{64,128},{128,192},{192,0},{1,65},{65,129},{129,193},{193,1... | collective-permute-start | bytes 737288 | tf_op jit(solution)/shard_map/ppermute | solution.py:346
  80.8 10.7 %collective-permute-start.12 = (f16[960,128]{1,0:T(8,128)(2,1)S(1)}, f16[960,128]{1,0:T(8,128)(2,1)S(1)}, u32[]{:S(2)}, u32[]{:S(2)}) collective-permute-start(f16[960,128]{1,0:T(8,128)(2,1)S(1)} %get-tuple-element.101), channel_id=1, source_target_pairs={{0,128},{64,192},{128,0},{192,64},{1,129},{65,193},{129,1},{193,65... | collective-permute-start | bytes 737288 | tf_op jit(solution)/shard_map/ppermute | solution.py:346
  83.4 8.0 %collective-permute-start.11 = (f16[960,128]{1,0:T(8,128)(2,1)S(1)}, f16[960,128]{1,0:T(8,128)(2,1)S(1)}, u32[]{:S(2)}, u32[]{:S(2)}) collective-permute-start(f16[960,128]{1,0:T(8,128)(2,1)S(1)} %get-tuple-element.101), channel_id=1, source_target_pairs={{0,192},{64,0},{128,64},{192,128},{1,193},{65,1},{129,65},{193,129... | collective-permute-start | bytes 737288 | tf_op jit(solution)/shard_map/ppermute | solution.py:346
  84.3 7.2 %collective-permute-start.10 = (bf16[960,128]{1,0:T(8,128)(2,1)S(1)}, bf16[960,128]{1,0:T(8,128)(2,1)S(1)}, u32[]{:S(2)}, u32[]{:S(2)}) collective-permute-start(bf16[960,128]{1,0:T(8,128)(2,1)S(1)} %collective-permute-done.8.refs_1_), channel_id=1, source_target_pairs={{0,56},{8,0},{16,8},{24,16},{32,24},{40,32},{48,40},{56,48},{1,57}... | collective-permute-start | bytes 737288 | tf_op jit(solution)/shard_map/ppermute | solution.py:346
  85.4 6.6 %collective-permute-start.9 = (bf16[960,128]{1,0:T(8,128)(2,1)S(1)}, bf16[960,128]{1,0:T(8,128)(2,1)S(1)}, u32[]{:S(2)}, u32[]{:S(2)}) collective-permute-start(bf16[960,128]{1,0:T(8,128)(2,1)S(1)} %collective-permute-done.7.refs_2_), channel_id=1, source_target_pairs={{0,8},{8,16},{16,24},{24,32},{32,40},{40,48},{48,56},{56,0},{1,9},... | collective-permute-start | bytes 737288 | tf_op jit(solution)/shard_map/ppermute | solution.py:346
  86.1 8.6 %copy-start.1 = (f16[960,128]{1,0:T(8,128)(2,1)}, f16[960,128]{1,0:T(8,128)(2,1)S(1)}, u32[]{:S(2)}) copy-start(f16[960,128]{1,0:T(8,128)(2,1)S(1)} %collective-permute-done.13) | copy-start | bytes 737284
  91.4 3.3 %copy-start.3 = (f16[960,128]{1,0:T(8,128)(2,1)}, f16[960,128]{1,0:T(8,128)(2,1)S(1)}, u32[]{:S(2)}) copy-start(f16[960,128]{1,0:T(8,128)(2,1)S(1)} %collective-permute-done.12) | copy-start | bytes 737284
  91.4 3.3 %copy-start.5 = (f16[960,128]{1,0:T(8,128)(2,1)}, f16[960,128]{1,0:T(8,128)(2,1)S(1)}, u32[]{:S(2)}) copy-start(f16[960,128]{1,0:T(8,128)(2,1)S(1)} %collective-permute-done.11) | copy-start | bytes 737284
  94.7 33.7 %all-to-all-start.2 = ((bf16[32,208,128]{2,1,0:T(8,128)(2,1)}), bf16[32,208,128]{2,1,0:T(8,128)(2,1)S(1)}, u32[]{:S(2)}, u32[]{:S(2)}) async-start(bf16[32,208,128]{2,1,0:T(8,128)(2,1)} %fetch.2), calls=%async_computation.2 | async-start | bytes 3407872 | tf_op jit(solution)/shard_map/all_to_all | solution.py:370
  105.5 8.6 %collective-permute-start.14 = (bf16[960,128]{1,0:T(8,128)(2,1)S(1)}, bf16[960,128]{1,0:T(8,128)(2,1)S(1)}, u32[]{:S(2)}, u32[]{:S(2)}) collective-permute-start(bf16[960,128]{1,0:T(8,128)(2,1)S(1)} %collective-permute-done.9.refs_4_), channel_id=1, source_target_pairs={{0,8},{8,16},{16,24},{24,32},{32,40},{40,48},{48,56},{56,0},{1,9},... | collective-permute-start | bytes 737288 | tf_op jit(solution)/shard_map/ppermute | solution.py:346
  105.6 8.5 %collective-permute-start.15 = (bf16[960,128]{1,0:T(8,128)(2,1)S(1)}, bf16[960,128]{1,0:T(8,128)(2,1)S(1)}, u32[]{:S(2)}, u32[]{:S(2)}) collective-permute-start(bf16[960,128]{1,0:T(8,128)(2,1)S(1)} %collective-permute-done.10.refs_3_), channel_id=1, source_target_pairs={{0,56},{8,0},{16,8},{24,16},{32,24},{40,32},{48,40},{56,48},{1,57}... | collective-permute-start | bytes 737288 | tf_op jit(solution)/shard_map/ppermute | solution.py:346
  114.1 7.6 %collective-permute-start.16 = (bf16[960,128]{1,0:T(8,128)(2,1)S(1)}, bf16[960,128]{1,0:T(8,128)(2,1)S(1)}, u32[]{:S(2)}, u32[]{:S(2)}) collective-permute-start(bf16[960,128]{1,0:T(8,128)(2,1)S(1)} %collective-permute-done.14.refs_1_), channel_id=1, source_target_pairs={{0,8},{8,16},{16,24},{24,32},{32,40},{40,48},{48,56},{56,0},{1,9},... | collective-permute-start | bytes 737288 | tf_op jit(solution)/shard_map/ppermute | solution.py:346
  122.8 1.0 copy-start
  128.4 21.6 %all-to-all-start.3 = ((bf16[32,128,128]{2,1,0:T(8,128)(2,1)}), bf16[32,128,128]{2,1,0:T(8,128)(2,1)S(1)}, u32[]{:S(2)}, u32[]{:S(2)}) async-start(bf16[32,128,128]{2,1,0:T(8,128)(2,1)} %copy-done), calls=%async_computation.3 | async-start | bytes 2097152 | tf_op jit(solution)/shard_map/all_to_all | solution.py:370
  133.7 1.4 copy-start.6
  133.7 1.5 copy-start.4
  135.0 0.9 copy-start.2

commit v4 on v3

--- a/solution.py
+++ b/solution.py
@@ -149,7 +149,7 @@
                 ref[pl.ds(k, 1), pl.ds(q * LANES, LANES)] = diagonal(rolled, z_ref[0] + k).astype(jnp.int32)
 
 
-def sums_kernel(ks, first, z_ref, *refs):
+def sums_kernel(ks, first, wanted, z_ref, *refs):
     n = len(ks)
     if first:
         got_ref, outs, ids_ref = refs[0], refs[1 : 1 + n], refs[1 + n]
@@ -157,7 +157,8 @@
     else:
         got_ref, ids_ref, outs = refs[0], refs[1], refs[2:]
     rows = centred(lax.broadcasted_iota(jnp.int32, (ROWS, GROUP * CAP), 0))
-    for p, k in enumerate(ks):
+    for out_ref, k in zip(outs, wanted):
+        p = ks.index(k)
         pick = one_hot(rows, centred(ids_ref[pl.ds(k, 1), :]))
         slots = jnp.concatenate(
             [
@@ -167,26 +168,28 @@
             axis=1,
         )
         total = jnp.dot(pick, slots, preferred_element_type=F32)
-        outs[p][pl.ds(0, ROWS), :] = total[:, :128]
-        outs[p][pl.ds(ROWS, ROWS), :] = total[:, 128:256]
+        out_ref[pl.ds(0, ROWS), :] = total[:, :128]
+        out_ref[pl.ds(ROWS, ROWS), :] = total[:, 128:256]
         last = total[:, 256:]
-        outs[p][pl.ds(2 * ROWS, HALF), :] = pair(last[:HALF], last[HALF:], p % 2 == 1)
-
-
-def partial_sums(z, ks, got, ids=None):
+        out_ref[pl.ds(2 * ROWS, HALF), :] = pair(last[:HALF], last[HALF:], p % 2 == 1)
+
+
+def partial_sums(z, ks, got, ids=None, wanted=None):
     vmem = pl.BlockSpec(memory_space=pltpu.VMEM)
     first = ids is None
+    wanted = wanted or ks
     ids_shape = jax.ShapeDtypeStruct((NZ, GROUP * CAP), jnp.int32)
-    outs = [jax.ShapeDtypeStruct((QROWS, LANES), F32)] * len(ks) + [ids_shape] * (2 if first else 0)
+    outs = [jax.ShapeDtypeStruct((QROWS, LANES), F32)] * len(wanted) + [ids_shape] * (2 if first else 0)
     got = pl.pallas_call(
-        functools.partial(sums_kernel, ks, first),
+        functools.partial(sums_kernel, ks, first, wanted),
         in_specs=[pl.BlockSpec(memory_space=pltpu.SMEM)] + [vmem] * (1 if first else 2),
         out_specs=[vmem] * len(outs),
         out_shape=outs,
         compiler_params=params(12),
         name="partial_sums",
     )(z, got, *(() if first else (ids,)))
-    return dict(zip(ks, got)), tuple(got[len(ks) :])
+    sums = dict(zip(wanted, got))
+    return (sums, tuple(got[len(ks) :])) if first else sums
 
 
 def quarter_kernel(y_ref, *refs):
@@ -220,69 +223,108 @@
     )(y, *[hbm(t) for t in arrays for _ in range(3)])
 
 
-def fetch_kernel(ks, ids_ref, *refs):
+def back_rows(ks):
+    return chunk_rows(len(ks)) - (CAP if ks == FIRST else 0)
+
+
+def fetch_kernel(ks, some, ids_ref, *refs):
     n = len(ks)
-    tables, o_ref = refs[:n], refs[n]
+    tables, (out_ref, o_ref, sems) = refs[: len(some)], refs[-3:]
     rows = centred(lax.broadcasted_iota(jnp.int32, (GROUP * CAP, ROWS), 1))
     columns = jnp.transpose(ids_ref[...].astype(F32) - HALF).astype(BF)
     low = low_lanes((GROUP, CAP, LANES))
-    even = None
-    for p, k in enumerate(ks):
-        pick = one_hot(rows, columns[:, k : k + 1])
-        table = tables[p]
+    even = rest = None
+    copies = []
+
+    def leave(at, value):
+        piece = (slice(None), pl.ds(at * CAP, CAP))
+        o_ref[piece] = value
+        copies.append(pltpu.make_async_copy(o_ref.at[piece], out_ref.at[piece], sems.at[at]))
+        copies[-1].start()
+
+    def find(k, wide):
+        found = jnp.dot(one_hot(rows, columns[:, k : k + 1]), wide, preferred_element_type=F32)
+        return found.astype(BF).reshape(GROUP, CAP, wide.shape[1])
+
+    for table, k in zip(tables, some):
+        p = ks.index(k) if k in ks else -1
         last = table[pl.ds(2 * ROWS, HALF), :]
         moved = pltpu.roll(last.astype(F32), 64, 1).astype(BF)
-        halves = [moved, last] if p % 2 else [last, moved]
-        wide = jnp.concatenate(
-            [table[pl.ds(0, ROWS), :], table[pl.ds(ROWS, ROWS), :], jnp.concatenate(halves, axis=0)], axis=1
-        )
-        found = jnp.dot(pick, wide, preferred_element_type=F32)
-        found = found.astype(BF).reshape(GROUP, CAP, 3 * LANES)
-        o_ref[:, pl.ds(p * CAP, CAP), :] = found[:, :, :128]
-        o_ref[:, pl.ds((n + p) * CAP, CAP), :] = found[:, :, 128:256]
+        ends = jnp.concatenate([moved, last] if p % 2 else [last, moved], axis=0)
+        if p < 0:
+            rest = find(k, ends)
+            continue
+        found = find(k, jnp.concatenate([table[pl.ds(0, ROWS), :], table[pl.ds(ROWS, ROWS), :], ends], axis=1))
+        leave(p, found[:, :, :128])
+        leave(n + p, found[:, :, 128:256])
         if p % 2:
-            o_ref[:, pl.ds((2 * n + p // 2) * CAP, CAP), :] = jnp.where(low, even, found[:, :, 256:])
-        else:
+            leave(2 * n + p // 2, jnp.where(low, even, found[:, :, 256:]))
+        elif p < n - 1:
             even = found[:, :, 256:]
-            if p == n - 1:
-                o_ref[:, pl.ds((2 * n + p // 2) * CAP, CAP), :] = even
-
-
-def fetch(ks, ids, tables):
+        elif rest is not None:
+            leave(2 * n + p // 2, jnp.where(low, found[:, :, 256:], rest))
+    for copy in copies:
+        copy.wait()
+
+
+def fetch(ks, some, ids, tables, into=None):
     vmem = pl.BlockSpec(memory_space=pltpu.VMEM)
+    hbm_spec = pl.BlockSpec(memory_space=pltpu.HBM)
+    shape = (GROUP, back_rows(ks), LANES)
     return pl.pallas_call(
-        functools.partial(fetch_kernel, ks),
-        in_specs=[vmem] * (1 + len(ks)),
-        out_specs=vmem,
-        out_shape=jax.ShapeDtypeStruct((GROUP, chunk_rows(len(ks)), LANES), BF),
+        functools.partial(fetch_kernel, ks, some),
+        in_specs=[vmem] * (1 + len(some)) + ([] if into is None else [hbm_spec]),
+        out_specs=hbm_spec,
+        out_shape=pltpu.HBM(shape, BF),
+        input_output_aliases={} if into is None else {1 + len(some): 0},
+        scratch_shapes=[pltpu.VMEM(shape, BF), pltpu.SemaphoreType.DMA((shape[1] // CAP,))],
         compiler_params=params(12),
         name="fetch",
-    )(ids, *[tables[k] for k in ks])
+    )(ids, *[tables[k] for k in some], *(() if into is None else (into,)))
 
 
 def unpack_kernel(ks, z_ref, g_ref, *refs):
     o_ref, block_ref, sems = refs[-3:]
     n = len(ks)
     copies = []
+
+    def last_columns(slot, p, odd):
+        for u in range(XC):
+            get = lambda y: g_ref[u * NY + y, pl.ds((2 * n + p // 2) * CAP, CAP), :].astype(F32)
+            for t in range(2):
+                block_ref[slot, pl.ds(u * CAP, CAP), pl.ds(1024 + t * LANES, LANES)] = pair(
+                    get(2 * t), get(2 * t + 1), odd
+                ).astype(BF)
+
+    def leave(slot, k, cols):
+        piece = (slice(None), cols)
+        copies.append(
+            pltpu.make_async_copy(
+                block_ref.at[slot].at[piece], o_ref.at[(z_ref[0] + k) % NZ].at[piece], sems.at[slot]
+            )
+        )
+        copies[-1].start()
+
     for p, k in enumerate(ks):
         for u in range(XC):
             rows = pl.ds(u * CAP, CAP)
-            get = lambda y, at: g_ref[u * NY + y, pl.ds(at * CAP, CAP), :]
             for y in range(NY):
-                block_ref[p, rows, pl.ds(y * LANES, LANES)] = get(y, p)
-                block_ref[p, rows, pl.ds(512 + y * LANES, LANES)] = get(y, n + p)
-            for t in range(2):
-                a = get(2 * t, 2 * n + p // 2).astype(F32)
-                b = get(2 * t + 1, 2 * n + p // 2).astype(F32)
-                block_ref[p, rows, pl.ds(1024 + t * LANES, LANES)] = pair(a, b, p % 2 == 1).astype(BF)
-        copies.append(pltpu.make_async_copy(block_ref.at[p], o_ref.at[(z_ref[0] + k) % NZ], sems.at[p]))
-        copies[-1].start()
+                block_ref[p, rows, pl.ds(y * LANES, LANES)] = g_ref[u * NY + y, pl.ds(p * CAP, CAP), :]
+                block_ref[p, rows, pl.ds(512 + y * LANES, LANES)] = g_ref[u * NY + y, pl.ds((n + p) * CAP, CAP), :]
+        if ks == FIRST and p == n - 1:
+            leave(p, k, pl.ds(0, 1024))
+        else:
+            last_columns(p, p, p % 2 == 1)
+            leave(p, k, pl.ds(0, 1280))
+    if ks == LATER:
+        last_columns(n, n - 1, True)
+        leave(n, FIRST[-1], pl.ds(1024, 256))
     for copy in copies:
         copy.wait()
 
 
 def unpack(z, ks, back, into=None):
-    n = len(ks)
+    n = len(ks) + (ks == LATER)
     hbm_spec = pl.BlockSpec(memory_space=pltpu.HBM)
     return pl.pallas_call(
         functools.partial(unpack_kernel, ks),
@@ -362,7 +404,8 @@
 
 
 def send_sums(up, down):
-    up, down = both_ways(coded(up), coded(down))
+    up, down = along(coded(up), "z", NZ, 1), along(coded(down), "z", NZ, -1)
+    up, down = lax.optimization_barrier((up, down))
     return decoded(up), decoded(down)
 
 
@@ -371,7 +414,7 @@
 
 
 FAR, NEAR = (4, 3, 5), (2, 6, 1, 7, 0)
-FIRST, LATER = (0, 1, 7, 2, 6), (3, 5, 4)
+FIRST, LATER = (0, 1, 2, 6, 7), (3, 5, 4)
 
 
 def local(table_rows, first_moment, second_moment, grad_rows, row_ids, next_ids):
@@ -384,8 +427,9 @@
     up = decoded(along(coded(part[4]), "z", NZ, 1))
     up, down = send_sums(part[3] + up, part[5])
     near, up, down = lax.optimization_barrier((near, up, down))
-    part, _ = partial_sums(z, NEAR, near, ids)
+    part = partial_sums(z, NEAR, near, ids, (2, 6))
     up, down = send_sums(part[2] + up, part[6] + down)
+    part = partial_sums(z, NEAR, near, ids, (1, 7, 0))
     up, down = send_sums(part[1] + up, part[7] + down)
     shared = coded(part[0] + up + down)
     summed = decoded(shared)
@@ -393,14 +437,16 @@
     grads = [shared] + [along(shared, "y", NY, -d) for d in range(1, NY)]
     tables = {0: own}
     tables[7], tables[1] = both_ways(own, own)
+    found = fetch(FIRST, (0, 1, 7), wanted, tables)
     tables[6], tables[2], *grads[1:] = lax.optimization_barrier(
         (along(tables[7], "z", NZ, 1), along(tables[1], "z", NZ, -1), *grads[1:])
     )
-    found, tables[6], tables[2] = lax.optimization_barrier((fetch(FIRST, wanted, tables), tables[6], tables[2]))
+    found = fetch(FIRST, (2, 6), wanted, tables, found)
+    found, tables[6], tables[2] = lax.optimization_barrier((found, tables[6], tables[2]))
     back = swap(found)
     tables[5], tables[3] = both_ways(tables[6], tables[2])
     tables[4] = along(tables[5], "z", NZ, 1)
-    back, found, *grads = lax.optimization_barrier((back, fetch(LATER, wanted, tables), *grads))
+    back, found, *grads = lax.optimization_barrier((back, fetch(LATER, (7, *LATER), wanted, tables), *grads))
     backs = [back, swap(found)]
     outs = full_rows(y, [decoded(g) for g in grads], table_rows, first_moment, second_moment)
     fetched = unpack(z, LATER, backs[1], unpack(z, FIRST, backs[0]))

time: 152 us -> 149 us (0.980)
  waiting for transfers between devices: 68.6 us -> 62.3 us
  Pallas kernels: 21.7 us -> 24 us
  starting transfers between devices: 55.1 us -> 57.1 us
    ppermute x17, waiting for transfers between devices: 41.1 us -> 36.4 us  [along(): lax.ppermute(value, axis, [(i, (i + step) % size) for i in range(size)])]
    pallas_call x4 -> x6, Pallas kernels: 6.06 us -> 8.41 us  [the longest x3 5.91 us: fetch(): pl.pallas_call(functools.partial(fetch_kernel, ks, some), in_specs=[vmem]...]
    ppermute x17, starting transfers between devices: 25.8 us -> 27.4 us  [along(): lax.ppermute(value, axis, [(i, (i + step) % size) for i in range(size)])]
    all_to_all x4, waiting for transfers between devices: 27.5 us -> 26 us  [swap(): return lax.all_to_all(x, SLAB, split_axis=0, concat_axis=0, tiled=True)]
  transfers between devices with their start and end apart: 21 -> 21, of which waited for: 13 -> 12; matrix products, arithmetic and copies ran while one was open for 1% -> 1% of each run, Pallas kernels for 9% -> 12%
where the time goes in v4:
time: 149 us; the launch traced here: 148 us
  waiting for transfers between devices  62.3 us (42%)
  starting transfers between devices  57.1 us (38%)
  Pallas kernels  24 us (16%)
  other arithmetic  3.14 us (2%)
    ppermute x17, waiting for transfers between devices, along(): lax.ppermute(value, axis, [(i, (i + step) % size) for i in range(size)])  36.4 us
    all_to_all x4, starting transfers between devices, swap(): return lax.all_to_all(x, SLAB, split_axis=0, concat_axis=0, tiled=True)  29.6 us
    ppermute x17, starting transfers between devices, along(): lax.ppermute(value, axis, [(i, (i + step) % size) for i in range(size)])  27.4 us
    all_to_all x4, waiting for transfers between devices, swap(): return lax.all_to_all(x, SLAB, split_axis=0, concat_axis=0, tiled=True)  26 us
    pallas_call x1, Pallas kernels, full_rows(): pl.pallas_call(full_kernel, grid_spec=pltpu.PrefetchScalarGridSpec(num_sc...  6.33 us
    pallas_call x3, Pallas kernels, fetch(): pl.pallas_call(functools.partial(fetch_kernel, ks, some), in_specs=[vmem]...  5.91 us
    pallas_call x2, Pallas kernels, pack(): pl.pallas_call(functools.partial(pack_kernel, n, step, bool(ids)), grid_s...  5.08 us
  transfers between devices with their start and end apart: 21, of which 12 were waited for; matrix products, arithmetic and copies ran while one was open for 1% of the time, Pallas kernels for 12%

profile of v4, /device:TPU:1, one launch (start us, length us, event | category | flops | bytes accessed | tf_op | source)
XLA Modules:
  0.0 148.4 jit_solution(12884118888445157134)
XLA Ops:
  0.6 2.5 %pack.2 = bf16[8,4,128,128]{3,2,1,0:T(8,128)(2,1)} custom-call(s32[1]{0:T(128)} %bitcast.1.z_ref, bf16[8,8,16,1280]{3,2,1,0:T(8,128)(2,1)} %bitcast.22, bf16[8,8,16,1280]{3,2,1,0:T(8,128)(2,1)} %bitcast.23, bf16[8,8,16,1280]{3,2,1,0:T(8,128)(2,1)} %bitcast.24, s32[8,128]{1,0:T(8,128)} %bitcast.36, s32[8,128]{1,0:T(8,128)} %bitcast.37), custom_call_target="tpu_custom_call" | custom-call | bytes 2100000 | tf_op jit(solution)/shard_map/pack/pallas_call | solution.py:119
  3.1 8.6 %all-to-all-start = ((bf16[32,128,128]{2,1,0:T(8,128)(2,1)}), bf16[32,128,128]{2,1,0:T(8,128)(2,1)S(1)}, u32[]{:S(2)}, u32[]{:S(2)}) async-start(bf16[32,128,128]{2,1,0:T(8,128)(2,1)} %bitcast.35), calls=%async_computation | async-start | bytes 2097152 | tf_op jit(solution)/shard_map/all_to_all | solution.py:413
  11.7 2.6 %pack.3 = bf16[8,4,208,128]{3,2,1,0:T(8,128)(2,1)} custom-call(s32[1]{0:T(128)} %bitcast.1.z_ref, bf16[8,8,16,1280]{3,2,1,0:T(8,128)(2,1)} %bitcast.25, bf16[8,8,16,1280]{3,2,1,0:T(8,128)(2,1)} %bitcast.26, bf16[8,8,16,1280]{3,2,1,0:T(8,128)(2,1)} %bitcast.27, bf16[8,8,16,1280]{3,2,1,0:T(8,128)(2,1)} %bitcast.28, bf16[8,8,16,1280]{3,2,1,0:T(8,128)(2,1)} %bitcast.29), custom_call_target="tpu_custom_call" | custom-call | bytes 3500000 | tf_op jit(solution)/shard_map/pack/pallas_call | solution.py:119
  14.3 13.7 %all-to-all-done.refs_0_ = bf16[32,128,128]{2,1,0:T(8,128)(2,1)S(1)} async-done(((bf16[32,128,128]{2,1,0:T(8,128)(2,1)}), bf16[32,128,128]{2,1,0:T(8,128)(2,1)S(1)}, u32[]{:S(2)}, u32[]{:S(2)}) %all-to-all-start) | async-done | bytes 1048608 | tf_op jit(solution)/shard_map/all_to_all | solution.py:413
  28.0 4.7 %all-to-all-start.1 = ((bf16[32,208,128]{2,1,0:T(8,128)(2,1)}), bf16[32,208,128]{2,1,0:T(8,128)(2,1)S(1)}, u32[]{:S(2)}, u32[]{:S(2)}) async-start(bf16[32,208,128]{2,1,0:T(8,128)(2,1)} %bitcast.34), calls=%async_computation.1 | async-start | bytes 3407872 | tf_op jit(solution)/shard_map/all_to_all | solution.py:413
  32.7 1.1 partial_sums.3
  33.8 0.2 fusion
  34.0 1.7 %collective-permute-start = (f16[960,128]{1,0:T(8,128)(2,1)S(1)}, f16[960,128]{1,0:T(8,128)(2,1)S(1)}, u32[]{:S(2)}, u32[]{:S(2)}) collective-permute-start(f16[960,128]{1,0:T(8,128)(2,1)S(1)} %fusion), channel_id=1, source_target_pairs={{0,8},{8,16},{16,24},{24,32},{32,40},{40,48},{48,56},{56,0},{1,9},... | collective-permute-start | bytes 737288 | tf_op jit(solution)/shard_map/ppermute | solution.py:388
  36.0 4.0 %collective-permute-start.2 = (f16[960,128]{1,0:T(8,128)(2,1)S(1)}, f16[960,128]{1,0:T(8,128)(2,1)S(1)}, u32[]{:S(2)}, u32[]{:S(2)}) collective-permute-start(f16[960,128]{1,0:T(8,128)(2,1)S(1)} %fusion.4), channel_id=1, source_target_pairs={{0,56},{8,0},{16,8},{24,16},{32,24},{40,32},{48,40},{56,48},{1,57}... | collective-permute-start | bytes 737288 | tf_op jit(solution)/shard_map/ppermute | solution.py:388
  40.0 5.7 %collective-permute-done = f16[960,128]{1,0:T(8,128)(2,1)S(1)} collective-permute-done((f16[960,128]{1,0:T(8,128)(2,1)S(1)}, f16[960,128]{1,0:T(8,128)(2,1)S(1)}, u32[]{:S(2)}, u32[]{:S(2)}) %collective-permute-start) | collective-permute-done | bytes 245792 | tf_op jit(solution)/shard_map/ppermute | solution.py:388
  45.8 0.3 fusion.3
  46.2 7.8 %collective-permute-done.1 = f16[960,128]{1,0:T(8,128)(2,1)S(1)} collective-permute-done((f16[960,128]{1,0:T(8,128)(2,1)S(1)}, f16[960,128]{1,0:T(8,128)(2,1)S(1)}, u32[]{:S(2)}, u32[]{:S(2)}) %collective-permute-start.1) | collective-permute-done | bytes 245792 | tf_op jit(solution)/shard_map/ppermute | solution.py:388
  54.1 1.5 %all-to-all-done.1.refs_0_ = bf16[32,208,128]{2,1,0:T(8,128)(2,1)S(1)} async-done(((bf16[32,208,128]{2,1,0:T(8,128)(2,1)}), bf16[32,208,128]{2,1,0:T(8,128)(2,1)S(1)}, u32[]{:S(2)}, u32[]{:S(2)}) %all-to-all-start.1) | async-done | bytes 1703968 | tf_op jit(solution)/shard_map/all_to_all | solution.py:413
  55.7 0.6 partial_sums.5
  56.3 0.3 fusion.7
  56.5 1.7 %collective-permute-start.3 = (f16[960,128]{1,0:T(8,128)(2,1)S(1)}, f16[960,128]{1,0:T(8,128)(2,1)S(1)}, u32[]{:S(2)}, u32[]{:S(2)}) collective-permute-start(f16[960,128]{1,0:T(8,128)(2,1)S(1)} %fusion.7), channel_id=1, source_target_pairs={{0,8},{8,16},{16,24},{24,32},{32,40},{40,48},{48,56},{56,0},{1,9},... | collective-permute-start | bytes 737288 | tf_op jit(solution)/shard_map/ppermute | solution.py:388
  58.2 0.3 fusion.8
  58.5 4.0 %collective-permute-start.4 = (f16[960,128]{1,0:T(8,128)(2,1)S(1)}, f16[960,128]{1,0:T(8,128)(2,1)S(1)}, u32[]{:S(2)}, u32[]{:S(2)}) collective-permute-start(f16[960,128]{1,0:T(8,128)(2,1)S(1)} %fusion.8), channel_id=1, source_target_pairs={{0,56},{8,0},{16,8},{24,16},{32,24},{40,32},{48,40},{56,48},{1,57}... | collective-permute-start | bytes 737288 | tf_op jit(solution)/shard_map/ppermute | solution.py:388
  62.5 0.8 partial_sums.4
  63.4 3.6 %collective-permute-done.3 = f16[960,128]{1,0:T(8,128)(2,1)S(1)} collective-permute-done((f16[960,128]{1,0:T(8,128)(2,1)S(1)}, f16[960,128]{1,0:T(8,128)(2,1)S(1)}, u32[]{:S(2)}, u32[]{:S(2)}) %collective-permute-start.3) | collective-permute-done | bytes 245792 | tf_op jit(solution)/shard_map/ppermute | solution.py:388
  66.9 0.3 fusion.11
  67.3 0.3 fusion.14
  67.6 2.8 %collective-permute-start.6 = (f16[960,128]{1,0:T(8,128)(2,1)S(1)}, f16[960,128]{1,0:T(8,128)(2,1)S(1)}, u32[]{:S(2)}, u32[]{:S(2)}) collective-permute-start(f16[960,128]{1,0:T(8,128)(2,1)S(1)} %fusion.14), channel_id=1, source_target_pairs={{0,56},{8,0},{16,8},{24,16},{32,24},{40,32},{48,40},{56,48},{1,57}... | collective-permute-start | bytes 737288 | tf_op jit(solution)/shard_map/ppermute | solution.py:388
  70.5 1.8 %quarters.1 = (f32[960,128]{1,0:T(8,128)S(1)}, f32[960,128]{1,0:T(8,128)S(1)}, f32[960,128]{1,0:T(8,128)S(1)}) custom-call(s32[1]{0:T(128)} %bitcast.y_ref, f32[384,1280]{1,0:T(8,128)} %refs_2_.1, f32[384,1280]{1,0:T(8,128)} %refs_2_.1, f32[384,1280]{1,0:T(8,128)} %refs_2_.1, f32[384,1280]{1,0:T(8,128)} %refs_5_.1, f32[384,1280]{1,0:T(8,128)} %refs_5_.1, ...), custom_call_target="tpu_custom_call" | custom-call | flops 1000000 | bytes 3000000 | tf_op jit(solution)/shard_map/quarters/pallas_call | solution.py:211
  72.3 1.3 collective-permute-done.5
  73.6 0.8 subtract_convert_fusion
  74.5 2.5 %collective-permute-start.7 = (bf16[960,128]{1,0:T(8,128)(2,1)S(1)}, bf16[960,128]{1,0:T(8,128)(2,1)S(1)}, u32[]{:S(2)}, u32[]{:S(2)}) collective-permute-start(bf16[960,128]{1,0:T(8,128)(2,1)S(1)} %get-tuple-element.74.refs_0_), channel_id=1, source_target_pairs={{0,8},{8,16},{16,24},{24,32},{32,40},{40,48},{48,56},{56,0},{1,9},... | collective-permute-start | bytes 737288 | tf_op jit(solution)/shard_map/ppermute | solution.py:388
  77.0 0.9 collective-permute-start.8
  77.9 1.8 %collective-permute-start.13 = (f16[960,128]{1,0:T(8,128)(2,1)S(1)}, f16[960,128]{1,0:T(8,128)(2,1)S(1)}, u32[]{:S(2)}, u32[]{:S(2)}) collective-permute-start(f16[960,128]{1,0:T(8,128)(2,1)S(1)} %get-tuple-element.89), channel_id=1, source_target_pairs={{0,64},{64,128},{128,192},{192,0},{1,65},{65,129},{129,193},{193,1... | collective-permute-start | bytes 737288 | tf_op jit(solution)/shard_map/ppermute | solution.py:388
  79.7 2.6 %collective-permute-start.12 = (f16[960,128]{1,0:T(8,128)(2,1)S(1)}, f16[960,128]{1,0:T(8,128)(2,1)S(1)}, u32[]{:S(2)}, u32[]{:S(2)}) collective-permute-start(f16[960,128]{1,0:T(8,128)(2,1)S(1)} %get-tuple-element.89), channel_id=1, source_target_pairs={{0,128},{64,192},{128,0},{192,64},{1,129},{65,193},{129,1},{193,65... | collective-permute-start | bytes 737288 | tf_op jit(solution)/shard_map/ppermute | solution.py:388
  82.4 0.8 collective-permute-start.11
  83.2 1.4 collective-permute-start.10
  84.7 2.0 %fetch.3.refs_2_ = bf16[32,192,128]{2,1,0:T(8,128)(2,1)} custom-call(s32[8,512]{1,0:T(8,128)S(1)} %get-tuple-element.51.ids_ref, bf16[960,128]{1,0:T(8,128)(2,1)S(1)} %get-tuple-element.74.refs_0_, bf16[960,128]{1,0:T(8,128)(2,1)S(1)} %collective-permute-done.8.refs_1_, bf16[960,128]{1,0:T(8,128)(2,1)S(1)} %collective-permute-done.7.refs_2_.refs_0_), custom_call_target="tpu_custom_call" | custom-call | tf_op jit(solution)/shard_map/fetch/pallas_call | solution.py:274
  86.7 3.6 %collective-permute-done.12 = f16[960,128]{1,0:T(8,128)(2,1)S(1)} collective-permute-done((f16[960,128]{1,0:T(8,128)(2,1)S(1)}, f16[960,128]{1,0:T(8,128)(2,1)S(1)}, u32[]{:S(2)}, u32[]{:S(2)}) %collective-permute-start.12) | collective-permute-done | bytes 245792 | tf_op jit(solution)/shard_map/ppermute | solution.py:388
  90.4 0.8 collective-permute-done.9.refs_1_
  91.1 1.8 %fetch.4 = bf16[32,192,128]{2,1,0:T(8,128)(2,1)} custom-call(s32[8,512]{1,0:T(8,128)S(1)} %get-tuple-element.51.ids_ref, bf16[960,128]{1,0:T(8,128)(2,1)S(1)} %collective-permute-done.10.refs_0_, bf16[960,128]{1,0:T(8,128)(2,1)S(1)} %collective-permute-done.9.refs_1_, bf16[32,192,128]{2,1,0:T(8,128)(2,1)} %fetch.3.refs_2_), custom_call_target="tpu_custom_call", output_to_operand_aliasing={{}: (3, {})} | custom-call | tf_op jit(solution)/shard_map/fetch/pallas_call | solution.py:274
  92.9 10.6 %all-to-all-start.2 = ((bf16[32,192,128]{2,1,0:T(8,128)(2,1)}), bf16[32,192,128]{2,1,0:T(8,128)(2,1)S(1)}, u32[]{:S(2)}, u32[]{:S(2)}) async-start(bf16[32,192,128]{2,1,0:T(8,128)(2,1)} %fetch.4), calls=%async_computation.2 | async-start | bytes 3145728 | tf_op jit(solution)/shard_map/all_to_all | solution.py:413
  103.7 2.7 %collective-permute-start.15 = (bf16[960,128]{1,0:T(8,128)(2,1)S(1)}, bf16[960,128]{1,0:T(8,128)(2,1)S(1)}, u32[]{:S(2)}, u32[]{:S(2)}) collective-permute-start(bf16[960,128]{1,0:T(8,128)(2,1)S(1)} %collective-permute-done.10.refs_0_), channel_id=1, source_target_pairs={{0,56},{8,0},{16,8},{24,16},{32,24},{40,32},{48,40},{56,48},{1,57}... | collective-permute-start | bytes 737288 | tf_op jit(solution)/shard_map/ppermute | solution.py:388
  106.3 5.9 %collective-permute-done.14.refs_2_ = bf16[960,128]{1,0:T(8,128)(2,1)S(1)} collective-permute-done((bf16[960,128]{1,0:T(8,128)(2,1)S(1)}, bf16[960,128]{1,0:T(8,128)(2,1)S(1)}, u32[]{:S(2)}, u32[]{:S(2)}) %collective-permute-start.14) | collective-permute-done | bytes 245792 | tf_op jit(solution)/shard_map/ppermute | solution.py:388
  112.2 7.6 %collective-permute-done.16.refs_3_ = bf16[960,128]{1,0:T(8,128)(2,1)S(1)} collective-permute-done((bf16[960,128]{1,0:T(8,128)(2,1)S(1)}, bf16[960,128]{1,0:T(8,128)(2,1)S(1)}, u32[]{:S(2)}, u32[]{:S(2)}) %collective-permute-start.16) | collective-permute-done | bytes 245792 | tf_op jit(solution)/shard_map/ppermute | solution.py:388
  119.8 2.1 %fetch.5 = bf16[32,128,128]{2,1,0:T(8,128)(2,1)} custom-call(s32[8,512]{1,0:T(8,128)S(1)} %get-tuple-element.51.ids_ref, bf16[960,128]{1,0:T(8,128)(2,1)S(1)} %collective-permute-done.7.refs_2_.refs_0_, bf16[960,128]{1,0:T(8,128)(2,1)S(1)} %collective-permute-done.15.refs_1_, bf16[960,128]{1,0:T(8,128)(2,1)S(1)} %collective-permute-done.14.refs_2_, ...), custom_call_target="tpu_custom_call" | custom-call | tf_op jit(solution)/shard_map/fetch/pallas_call | solution.py:274
  121.9 3.1 %all-to-all-done.2.g_ref = bf16[32,192,128]{2,1,0:T(8,128)(2,1)S(1)} async-done(((bf16[32,192,128]{2,1,0:T(8,128)(2,1)}), bf16[32,192,128]{2,1,0:T(8,128)(2,1)S(1)}, u32[]{:S(2)}, u32[]{:S(2)}) %all-to-all-start.2) | async-done | bytes 1572896 | tf_op jit(solution)/shard_map/all_to_all | solution.py:413
  125.1 5.7 %all-to-all-start.3 = ((bf16[32,128,128]{2,1,0:T(8,128)(2,1)}), bf16[32,128,128]{2,1,0:T(8,128)(2,1)S(1)}, u32[]{:S(2)}, u32[]{:S(2)}) async-start(bf16[32,128,128]{2,1,0:T(8,128)(2,1)} %fetch.5), calls=%async_computation.3 | async-start | bytes 2097152 | tf_op jit(solution)/shard_map/all_to_all | solution.py:413
  130.8 1.3 unpack.2.refs_0_
  132.4 0.7 copy-done.1
  133.1 6.3 %full_rows.1 = (f32[2,192,1280]{2,1,0:T(8,128)}, f32[2,192,1280]{2,1,0:T(8,128)}, f32[2,192,1280]{2,1,0:T(8,128)}) custom-call(s32[1]{0:T(128)} %bitcast.y_ref, f32[5,192,128]{2,1,0:T(8,128)S(1)} %bitcast.18, f32[5,192,128]{2,1,0:T(8,128)S(1)} %bitcast.19, f32[5,192,128]{2,1,0:T(8,128)S(1)} %bitcast.20, f32[5,192,128]{2,1,0:T(8,128)S(1)} %bitcast.21, ...), custom_call_target="tpu_custom_call" | custom-call | flops 10000000 | bytes 14000000 | tf_op jit(solution)/shard_map/full_rows/pallas_call | solution.py:366
  139.5 7.7 %all-to-all-done.3.g_ref = bf16[32,128,128]{2,1,0:T(8,128)(2,1)S(1)} async-done(((bf16[32,128,128]{2,1,0:T(8,128)(2,1)}), bf16[32,128,128]{2,1,0:T(8,128)(2,1)S(1)}, u32[]{:S(2)}, u32[]{:S(2)}) %all-to-all-start.3) | async-done | bytes 1048608 | tf_op jit(solution)/shard_map/all_to_all | solution.py:413
  147.1 1.1 unpack.3
  (31 shorter events, 1.0 us)
Async XLA Ops:
  3.1 24.9 %all-to-all-start = ((bf16[32,128,128]{2,1,0:T(8,128)(2,1)}), bf16[32,128,128]{2,1,0:T(8,128)(2,1)S(1)}, u32[]{:S(2)}, u32[]{:S(2)}) async-start(bf16[32,128,128]{2,1,0:T(8,128)(2,1)} %bitcast.35), calls=%async_computation | async-start | bytes 2097152 | tf_op jit(solution)/shard_map/all_to_all | solution.py:413
  28.0 27.7 %all-to-all-start.1 = ((bf16[32,208,128]{2,1,0:T(8,128)(2,1)}), bf16[32,208,128]{2,1,0:T(8,128)(2,1)S(1)}, u32[]{:S(2)}, u32[]{:S(2)}) async-start(bf16[32,208,128]{2,1,0:T(8,128)(2,1)} %bitcast.34), calls=%async_computation.1 | async-start | bytes 3407872 | tf_op jit(solution)/shard_map/all_to_all | solution.py:413
  34.0 11.7 %collective-permute-start = (f16[960,128]{1,0:T(8,128)(2,1)S(1)}, f16[960,128]{1,0:T(8,128)(2,1)S(1)}, u32[]{:S(2)}, u32[]{:S(2)}) collective-permute-start(f16[960,128]{1,0:T(8,128)(2,1)S(1)} %fusion), channel_id=1, source_target_pairs={{0,8},{8,16},{16,24},{24,32},{32,40},{40,48},{48,56},{56,0},{1,9},... | collective-permute-start | bytes 737288 | tf_op jit(solution)/shard_map/ppermute | solution.py:388
  36.0 10.2 %collective-permute-start.2 = (f16[960,128]{1,0:T(8,128)(2,1)S(1)}, f16[960,128]{1,0:T(8,128)(2,1)S(1)}, u32[]{:S(2)}, u32[]{:S(2)}) collective-permute-start(f16[960,128]{1,0:T(8,128)(2,1)S(1)} %fusion.4), channel_id=1, source_target_pairs={{0,56},{8,0},{16,8},{24,16},{32,24},{40,32},{48,40},{56,48},{1,57}... | collective-permute-start | bytes 737288 | tf_op jit(solution)/shard_map/ppermute | solution.py:388
  46.1 7.9 %collective-permute-start.1 = (f16[960,128]{1,0:T(8,128)(2,1)S(1)}, f16[960,128]{1,0:T(8,128)(2,1)S(1)}, u32[]{:S(2)}, u32[]{:S(2)}) collective-permute-start(f16[960,128]{1,0:T(8,128)(2,1)S(1)} %fusion.3), channel_id=1, source_target_pairs={{0,8},{8,16},{16,24},{24,32},{32,40},{40,48},{48,56},{56,0},{1,9},... | collective-permute-start | bytes 737288 | tf_op jit(solution)/shard_map/ppermute | solution.py:388
  56.5 10.4 %collective-permute-start.3 = (f16[960,128]{1,0:T(8,128)(2,1)S(1)}, f16[960,128]{1,0:T(8,128)(2,1)S(1)}, u32[]{:S(2)}, u32[]{:S(2)}) collective-permute-start(f16[960,128]{1,0:T(8,128)(2,1)S(1)} %fusion.7), channel_id=1, source_target_pairs={{0,8},{8,16},{16,24},{24,32},{32,40},{40,48},{48,56},{56,0},{1,9},... | collective-permute-start | bytes 737288 | tf_op jit(solution)/shard_map/ppermute | solution.py:388
  58.5 8.4 %collective-permute-start.4 = (f16[960,128]{1,0:T(8,128)(2,1)S(1)}, f16[960,128]{1,0:T(8,128)(2,1)S(1)}, u32[]{:S(2)}, u32[]{:S(2)}) collective-permute-start(f16[960,128]{1,0:T(8,128)(2,1)S(1)} %fusion.8), channel_id=1, source_target_pairs={{0,56},{8,0},{16,8},{24,16},{32,24},{40,32},{48,40},{56,48},{1,57}... | collective-permute-start | bytes 737288 | tf_op jit(solution)/shard_map/ppermute | solution.py:388
  67.2 6.4 %collective-permute-start.5 = (f16[960,128]{1,0:T(8,128)(2,1)S(1)}, f16[960,128]{1,0:T(8,128)(2,1)S(1)}, u32[]{:S(2)}, u32[]{:S(2)}) collective-permute-start(f16[960,128]{1,0:T(8,128)(2,1)S(1)} %fusion.11), channel_id=1, source_target_pairs={{0,8},{8,16},{16,24},{24,32},{32,40},{40,48},{48,56},{56,0},{1,9},... | collective-permute-start | bytes 737288 | tf_op jit(solution)/shard_map/ppermute | solution.py:388
  67.6 6.0 %collective-permute-start.6 = (f16[960,128]{1,0:T(8,128)(2,1)S(1)}, f16[960,128]{1,0:T(8,128)(2,1)S(1)}, u32[]{:S(2)}, u32[]{:S(2)}) collective-permute-start(f16[960,128]{1,0:T(8,128)(2,1)S(1)} %fusion.14), channel_id=1, source_target_pairs={{0,56},{8,0},{16,8},{24,16},{32,24},{40,32},{48,40},{56,48},{1,57}... | collective-permute-start | bytes 737288 | tf_op jit(solution)/shard_map/ppermute | solution.py:388
  74.5 8.7 %collective-permute-start.7 = (bf16[960,128]{1,0:T(8,128)(2,1)S(1)}, bf16[960,128]{1,0:T(8,128)(2,1)S(1)}, u32[]{:S(2)}, u32[]{:S(2)}) collective-permute-start(bf16[960,128]{1,0:T(8,128)(2,1)S(1)} %get-tuple-element.74.refs_0_), channel_id=1, source_target_pairs={{0,8},{8,16},{16,24},{24,32},{32,40},{40,48},{48,56},{56,0},{1,9},... | collective-permute-start | bytes 737288 | tf_op jit(solution)/shard_map/ppermute | solution.py:388
  77.0 6.2 %collective-permute-start.8 = (bf16[960,128]{1,0:T(8,128)(2,1)S(1)}, bf16[960,128]{1,0:T(8,128)(2,1)S(1)}, u32[]{:S(2)}, u32[]{:S(2)}) collective-permute-start(bf16[960,128]{1,0:T(8,128)(2,1)S(1)} %get-tuple-element.74.refs_0_), channel_id=1, source_target_pairs={{0,56},{8,0},{16,8},{24,16},{32,24},{40,32},{48,40},{56,48},{1,57}... | collective-permute-start | bytes 737288 | tf_op jit(solution)/shard_map/ppermute | solution.py:388
  77.9 8.8 %collective-permute-start.13 = (f16[960,128]{1,0:T(8,128)(2,1)S(1)}, f16[960,128]{1,0:T(8,128)(2,1)S(1)}, u32[]{:S(2)}, u32[]{:S(2)}) collective-permute-start(f16[960,128]{1,0:T(8,128)(2,1)S(1)} %get-tuple-element.89), channel_id=1, source_target_pairs={{0,64},{64,128},{128,192},{192,0},{1,65},{65,129},{129,193},{193,1... | collective-permute-start | bytes 737288 | tf_op jit(solution)/shard_map/ppermute | solution.py:388
  79.7 10.6 %collective-permute-start.12 = (f16[960,128]{1,0:T(8,128)(2,1)S(1)}, f16[960,128]{1,0:T(8,128)(2,1)S(1)}, u32[]{:S(2)}, u32[]{:S(2)}) collective-permute-start(f16[960,128]{1,0:T(8,128)(2,1)S(1)} %get-tuple-element.89), channel_id=1, source_target_pairs={{0,128},{64,192},{128,0},{192,64},{1,129},{65,193},{129,1},{193,65... | collective-permute-start | bytes 737288 | tf_op jit(solution)/shard_map/ppermute | solution.py:388
  82.4 8.0 %collective-permute-start.11 = (f16[960,128]{1,0:T(8,128)(2,1)S(1)}, f16[960,128]{1,0:T(8,128)(2,1)S(1)}, u32[]{:S(2)}, u32[]{:S(2)}) collective-permute-start(f16[960,128]{1,0:T(8,128)(2,1)S(1)} %get-tuple-element.89), channel_id=1, source_target_pairs={{0,192},{64,0},{128,64},{192,128},{1,193},{65,1},{129,65},{193,129... | collective-permute-start | bytes 737288 | tf_op jit(solution)/shard_map/ppermute | solution.py:388
  83.2 7.1 %collective-permute-start.10 = (bf16[960,128]{1,0:T(8,128)(2,1)S(1)}, bf16[960,128]{1,0:T(8,128)(2,1)S(1)}, u32[]{:S(2)}, u32[]{:S(2)}) collective-permute-start(bf16[960,128]{1,0:T(8,128)(2,1)S(1)} %collective-permute-done.8.refs_1_), channel_id=1, source_target_pairs={{0,56},{8,0},{16,8},{24,16},{32,24},{40,32},{48,40},{56,48},{1,57}... | collective-permute-start | bytes 737288 | tf_op jit(solution)/shard_map/ppermute | solution.py:388
  84.6 6.6 %collective-permute-start.9 = (bf16[960,128]{1,0:T(8,128)(2,1)S(1)}, bf16[960,128]{1,0:T(8,128)(2,1)S(1)}, u32[]{:S(2)}, u32[]{:S(2)}) collective-permute-start(bf16[960,128]{1,0:T(8,128)(2,1)S(1)} %collective-permute-done.7.refs_2_.refs_0_), channel_id=1, source_target_pairs={{0,8},{8,16},{16,24},{24,32},{32,40},{40,48},{48,56},{56,0},{1,9},... | collective-permute-start | bytes 737288 | tf_op jit(solution)/shard_map/ppermute | solution.py:388
  86.7 6.2 %copy-start = (f16[960,128]{1,0:T(8,128)(2,1)}, f16[960,128]{1,0:T(8,128)(2,1)S(1)}, u32[]{:S(2)}) copy-start(f16[960,128]{1,0:T(8,128)(2,1)S(1)} %collective-permute-done.13) | copy-start | bytes 737284
  90.3 2.6 %copy-start.2 = (f16[960,128]{1,0:T(8,128)(2,1)}, f16[960,128]{1,0:T(8,128)(2,1)S(1)}, u32[]{:S(2)}) copy-start(f16[960,128]{1,0:T(8,128)(2,1)S(1)} %collective-permute-done.12) | copy-start | bytes 737284
  90.3 0.8 copy-start.4
  92.9 32.1 %all-to-all-start.2 = ((bf16[32,192,128]{2,1,0:T(8,128)(2,1)}), bf16[32,192,128]{2,1,0:T(8,128)(2,1)S(1)}, u32[]{:S(2)}, u32[]{:S(2)}) async-start(bf16[32,192,128]{2,1,0:T(8,128)(2,1)} %fetch.4), calls=%async_computation.2 | async-start | bytes 3145728 | tf_op jit(solution)/shard_map/all_to_all | solution.py:413
  103.6 8.6 %collective-permute-start.14 = (bf16[960,128]{1,0:T(8,128)(2,1)S(1)}, bf16[960,128]{1,0:T(8,128)(2,1)S(1)}, u32[]{:S(2)}, u32[]{:S(2)}) collective-permute-start(bf16[960,128]{1,0:T(8,128)(2,1)S(1)} %collective-permute-done.9.refs_1_), channel_id=1, source_target_pairs={{0,8},{8,16},{16,24},{24,32},{32,40},{40,48},{48,56},{56,0},{1,9},... | collective-permute-start | bytes 737288 | tf_op jit(solution)/shard_map/ppermute | solution.py:388
  103.7 8.5 %collective-permute-start.15 = (bf16[960,128]{1,0:T(8,128)(2,1)S(1)}, bf16[960,128]{1,0:T(8,128)(2,1)S(1)}, u32[]{:S(2)}, u32[]{:S(2)}) collective-permute-start(bf16[960,128]{1,0:T(8,128)(2,1)S(1)} %collective-permute-done.10.refs_0_), channel_id=1, source_target_pairs={{0,56},{8,0},{16,8},{24,16},{32,24},{40,32},{48,40},{56,48},{1,57}... | collective-permute-start | bytes 737288 | tf_op jit(solution)/shard_map/ppermute | solution.py:388
  112.2 7.6 %collective-permute-start.16 = (bf16[960,128]{1,0:T(8,128)(2,1)S(1)}, bf16[960,128]{1,0:T(8,128)(2,1)S(1)}, u32[]{:S(2)}, u32[]{:S(2)}) collective-permute-start(bf16[960,128]{1,0:T(8,128)(2,1)S(1)} %collective-permute-done.14.refs_2_), channel_id=1, source_target_pairs={{0,8},{8,16},{16,24},{24,32},{32,40},{40,48},{48,56},{56,0},{1,9},... | collective-permute-start | bytes 737288 | tf_op jit(solution)/shard_map/ppermute | solution.py:388
  125.1 22.1 %all-to-all-start.3 = ((bf16[32,128,128]{2,1,0:T(8,128)(2,1)}), bf16[32,128,128]{2,1,0:T(8,128)(2,1)S(1)}, u32[]{:S(2)}, u32[]{:S(2)}) async-start(bf16[32,128,128]{2,1,0:T(8,128)(2,1)} %fetch.5), calls=%async_computation.3 | async-start | bytes 2097152 | tf_op jit(solution)/shard_map/all_to_all | solution.py:413
  130.8 1.4 copy-start.5
  130.8 1.5 %copy-start.3 = (f16[960,128]{1,0:T(8,128)(2,1)S(1)}, f16[960,128]{1,0:T(8,128)(2,1)}, u32[]{:S(2)}) copy-start(f16[960,128]{1,0:T(8,128)(2,1)} %copy-done.2) | copy-start | bytes 737284
  132.1 0.9 copy-start.1

commit v5 on v4

--- a/solution.py
+++ b/solution.py
@@ -132,6 +132,83 @@
     return out.reshape(GROUP, rows, LANES)
 
 
+def pack_far_kernel(z_ref, row_ref, next_ref, g_ref, out_ref, ids_ref, block_ref, o_ref, in_sems, sems):
+    n = len(FAR)
+    loads = [pltpu.make_async_copy(r, ids_ref.at[t], in_sems.at[n + t]) for t, r in enumerate((row_ref, next_ref))]
+    for p, k in enumerate(FAR):
+        loads.append(pltpu.make_async_copy(g_ref.at[(z_ref[0] + k) % NZ], block_ref.at[p], in_sems.at[p]))
+    for load in loads:
+        load.start()
+    copies = []
+
+    def leave(at):
+        piece = (slice(None), slice(None), pl.ds(at * CAP, CAP))
+        copies.append(pltpu.make_async_copy(o_ref.at[piece], out_ref.at[piece], sems.at[at]))
+        copies[-1].start()
+
+    sub = lax.broadcasted_iota(jnp.int32, (CAP, LANES), 0)
+    rests = [jnp.zeros((CAP, LANES), F32)] * XC
+    for t in range(2):
+        loads[t].wait()
+        ids = row_roll(ids_ref[t].astype(F32))
+        for u in range(XC):
+            mine = diagonal(ids, u)
+            upper = jnp.floor(mine * (1.0 / 16.0))
+            lower = mine - 16.0 * upper
+            for r, row in enumerate((pltpu.roll(upper, 64, 1), upper, pltpu.roll(lower, 64, 1), lower)):
+                rests[u] = jnp.where(sub == 4 * t + r, row, rests[u])
+    low = low_lanes((CAP, LANES))
+    for p in range(n):
+        loads[2 + p].wait()
+        for u in range(XC):
+            rows = pl.ds(u * CAP, CAP)
+            for y in range(NY):
+                o_ref[u, y, pl.ds(p * CAP, CAP), :] = block_ref[p, rows, pl.ds(y * LANES, LANES)]
+                o_ref[u, y, pl.ds((n + p) * CAP, CAP), :] = block_ref[p, rows, pl.ds(512 + y * LANES, LANES)]
+                if p % 2 == 0 and p < n - 1:
+                    continue
+                cols = pl.ds(1024 + (y // 2) * LANES, LANES)
+                b = block_ref[p, rows, cols].astype(F32)
+                if p % 2:
+                    tile = pair(block_ref[p - 1, rows, cols].astype(F32), b, y % 2 == 1)
+                else:
+                    tile = jnp.where(low, pltpu.roll(b, 64, 1) if y % 2 else b, rests[u])
+                o_ref[u, y, pl.ds((2 * n + p // 2) * CAP, CAP), :] = tile.astype(BF)
+        leave(p)
+        leave(n + p)
+        if p % 2 or p == n - 1:
+            leave(2 * n + p // 2)
+    for copy in copies:
+        copy.wait()
+
+
+def pack_far(z, grad_rows, row_ids, next_ids):
+    n = len(FAR)
+    hbm_spec = pl.BlockSpec(memory_space=pltpu.HBM)
+    shape = (XC, NY, chunk_rows(n), LANES)
+    out = pl.pallas_call(
+        pack_far_kernel,
+        in_specs=[pl.BlockSpec(memory_space=pltpu.SMEM)] + [hbm_spec] * 3,
+        out_specs=hbm_spec,
+        out_shape=pltpu.HBM(shape, BF),
+        scratch_shapes=[
+            pltpu.VMEM((2, 8, LANES), jnp.int32),
+            pltpu.VMEM((n, XC * CAP, 1280), BF),
+            pltpu.VMEM(shape, BF),
+            pltpu.SemaphoreType.DMA((n + 2,)),
+            pltpu.SemaphoreType.DMA((shape[2] // CAP,)),
+        ],
+        compiler_params=params(8),
+        name="pack_far",
+    )(
+        z,
+        hbm(row_ids.reshape(8, LANES)),
+        hbm(next_ids.reshape(8, LANES)),
+        hbm(grad_rows.reshape(NZ, XC * CAP, 1280)),
+    )
+    return out.reshape(GROUP, shape[2], LANES)
+
+
 def read_ids(z_ref, got_ref, at, outs):
     sub = tile_iota(0)
     low = low_lanes((8, LANES))
@@ -420,7 +497,7 @@
 def local(table_rows, first_moment, second_moment, grad_rows, row_ids, next_ids):
     z = lax.axis_index("z").astype(jnp.int32)[None]
     y = lax.axis_index("y").astype(jnp.int32)[None]
-    far = swap(pack(z, FAR, grad_rows, (row_ids, next_ids)))
+    far = swap(pack_far(z, grad_rows, row_ids, next_ids))
     near = swap(pack(z, NEAR, grad_rows))
     mine = quarters(y, table_rows, first_moment, second_moment)
     part, (ids, wanted) = partial_sums(z, FAR, far)

time: 149 us -> 149 us (level)
    pallas_call x2 -> x1, Pallas kernels: 5.08 us -> 2.62 us  [pack(): pl.pallas_call(functools.partial(pack_kernel, n, step, bool(ids)), grid_s...]
    pallas_call x0 -> x1, Pallas kernels: none -> 2.28 us  [pack_far(): pl.pallas_call(pack_far_kernel, in_specs=[pl.BlockSpec(memory_space=pltpu...]
  transfers between devices with their start and end apart: 21 -> 21, of which waited for: 12 -> 13; matrix products, arithmetic and copies ran while one was open for 1% -> 1% of each run, Pallas kernels for 12% -> 12%
where the time goes in v5:
time: 149 us; the launch traced here: 148 us
  waiting for transfers between devices  63.2 us (42%)
  starting transfers between devices  56.9 us (38%)
  Pallas kernels  23.9 us (16%)
  other arithmetic  3.15 us (2%)
    ppermute x17, waiting for transfers between devices, along(): lax.ppermute(value, axis, [(i, (i + step) % size) for i in range(size)])  36.5 us
    all_to_all x4, starting transfers between devices, swap(): return lax.all_to_all(x, SLAB, split_axis=0, concat_axis=0, tiled=True)  29.7 us
    ppermute x17, starting transfers between devices, along(): lax.ppermute(value, axis, [(i, (i + step) % size) for i in range(size)])  27.3 us
    all_to_all x4, waiting for transfers between devices, swap(): return lax.all_to_all(x, SLAB, split_axis=0, concat_axis=0, tiled=True)  26.7 us
    pallas_call x1, Pallas kernels, full_rows(): pl.pallas_call(full_kernel, grid_spec=pltpu.PrefetchScalarGridSpec(num_sc...  6.33 us
    pallas_call x3, Pallas kernels, fetch(): pl.pallas_call(functools.partial(fetch_kernel, ks, some), in_specs=[vmem]...  5.94 us
  transfers between devices with their start and end apart: 21, of which 13 were waited for; matrix products, arithmetic and copies ran while one was open for 1% of the time, Pallas kernels for 12%

profile of v5, /device:TPU:1, one launch (start us, length us, event | category | flops | bytes accessed | tf_op | source)
XLA Modules:
  0.0 148.2 jit_solution(9857769746588902893)
XLA Ops:
  0.6 2.3 %pack_far.1 = bf16[8,4,128,128]{3,2,1,0:T(8,128)(2,1)} custom-call(s32[1]{0:T(128)} %bitcast.1.z_ref, s32[8,128]{1,0:T(8,128)} %bitcast.35, s32[8,128]{1,0:T(8,128)} %bitcast.36, bf16[8,128,1280]{2,1,0:T(8,128)(2,1)} %bitcast.23), custom_call_target="tpu_custom_call" | custom-call | tf_op jit(solution)/shard_map/pack_far/pallas_call | solution.py:189
  2.9 8.6 %all-to-all-start = ((bf16[32,128,128]{2,1,0:T(8,128)(2,1)}), bf16[32,128,128]{2,1,0:T(8,128)(2,1)S(1)}, u32[]{:S(2)}, u32[]{:S(2)}) async-start(bf16[32,128,128]{2,1,0:T(8,128)(2,1)} %bitcast.34), calls=%async_computation | async-start | bytes 2097152 | tf_op jit(solution)/shard_map/all_to_all | solution.py:490
  11.5 2.6 %pack.1 = bf16[8,4,208,128]{3,2,1,0:T(8,128)(2,1)} custom-call(s32[1]{0:T(128)} %bitcast.1.z_ref, bf16[8,8,16,1280]{3,2,1,0:T(8,128)(2,1)} %bitcast.24, bf16[8,8,16,1280]{3,2,1,0:T(8,128)(2,1)} %bitcast.25, bf16[8,8,16,1280]{3,2,1,0:T(8,128)(2,1)} %bitcast.26, bf16[8,8,16,1280]{3,2,1,0:T(8,128)(2,1)} %bitcast.27, bf16[8,8,16,1280]{3,2,1,0:T(8,128)(2,1)} %bitcast.28), custom_call_target="tpu_custom_call" | custom-call | bytes 3500000 | tf_op jit(solution)/shard_map/pack/pallas_call | solution.py:119
  14.2 13.7 %all-to-all-done.refs_0_ = bf16[32,128,128]{2,1,0:T(8,128)(2,1)S(1)} async-done(((bf16[32,128,128]{2,1,0:T(8,128)(2,1)}), bf16[32,128,128]{2,1,0:T(8,128)(2,1)S(1)}, u32[]{:S(2)}, u32[]{:S(2)}) %all-to-all-start) | async-done | bytes 1048608 | tf_op jit(solution)/shard_map/all_to_all | solution.py:490
  27.9 4.7 %all-to-all-start.1 = ((bf16[32,208,128]{2,1,0:T(8,128)(2,1)}), bf16[32,208,128]{2,1,0:T(8,128)(2,1)S(1)}, u32[]{:S(2)}, u32[]{:S(2)}) async-start(bf16[32,208,128]{2,1,0:T(8,128)(2,1)} %bitcast.33), calls=%async_computation.1 | async-start | bytes 3407872 | tf_op jit(solution)/shard_map/all_to_all | solution.py:490
  32.6 1.1 partial_sums.3
  33.6 0.2 fusion
  33.9 1.7 %collective-permute-start = (f16[960,128]{1,0:T(8,128)(2,1)S(1)}, f16[960,128]{1,0:T(8,128)(2,1)S(1)}, u32[]{:S(2)}, u32[]{:S(2)}) collective-permute-start(f16[960,128]{1,0:T(8,128)(2,1)S(1)} %fusion), channel_id=1, source_target_pairs={{0,8},{8,16},{16,24},{24,32},{32,40},{40,48},{48,56},{56,0},{1,9},... | collective-permute-start | bytes 737288 | tf_op jit(solution)/shard_map/ppermute | solution.py:465
  35.8 4.1 %collective-permute-start.2 = (f16[960,128]{1,0:T(8,128)(2,1)S(1)}, f16[960,128]{1,0:T(8,128)(2,1)S(1)}, u32[]{:S(2)}, u32[]{:S(2)}) collective-permute-start(f16[960,128]{1,0:T(8,128)(2,1)S(1)} %fusion.4), channel_id=1, source_target_pairs={{0,56},{8,0},{16,8},{24,16},{32,24},{40,32},{48,40},{56,48},{1,57}... | collective-permute-start | bytes 737288 | tf_op jit(solution)/shard_map/ppermute | solution.py:465
  39.9 5.7 %collective-permute-done = f16[960,128]{1,0:T(8,128)(2,1)S(1)} collective-permute-done((f16[960,128]{1,0:T(8,128)(2,1)S(1)}, f16[960,128]{1,0:T(8,128)(2,1)S(1)}, u32[]{:S(2)}, u32[]{:S(2)}) %collective-permute-start) | collective-permute-done | bytes 245792 | tf_op jit(solution)/shard_map/ppermute | solution.py:465
  45.6 0.3 fusion.3
  46.0 7.8 %collective-permute-done.1 = f16[960,128]{1,0:T(8,128)(2,1)S(1)} collective-permute-done((f16[960,128]{1,0:T(8,128)(2,1)S(1)}, f16[960,128]{1,0:T(8,128)(2,1)S(1)}, u32[]{:S(2)}, u32[]{:S(2)}) %collective-permute-start.1) | collective-permute-done | bytes 245792 | tf_op jit(solution)/shard_map/ppermute | solution.py:465
  54.0 1.5 %all-to-all-done.1.refs_0_ = bf16[32,208,128]{2,1,0:T(8,128)(2,1)S(1)} async-done(((bf16[32,208,128]{2,1,0:T(8,128)(2,1)}), bf16[32,208,128]{2,1,0:T(8,128)(2,1)S(1)}, u32[]{:S(2)}, u32[]{:S(2)}) %all-to-all-start.1) | async-done | bytes 1703968 | tf_op jit(solution)/shard_map/all_to_all | solution.py:490
  55.5 0.6 partial_sums.5
  56.1 0.3 fusion.7
  56.4 1.7 %collective-permute-start.3 = (f16[960,128]{1,0:T(8,128)(2,1)S(1)}, f16[960,128]{1,0:T(8,128)(2,1)S(1)}, u32[]{:S(2)}, u32[]{:S(2)}) collective-permute-start(f16[960,128]{1,0:T(8,128)(2,1)S(1)} %fusion.7), channel_id=1, source_target_pairs={{0,8},{8,16},{16,24},{24,32},{32,40},{40,48},{48,56},{56,0},{1,9},... | collective-permute-start | bytes 737288 | tf_op jit(solution)/shard_map/ppermute | solution.py:465
  58.1 0.3 fusion.8
  58.3 4.0 %collective-permute-start.4 = (f16[960,128]{1,0:T(8,128)(2,1)S(1)}, f16[960,128]{1,0:T(8,128)(2,1)S(1)}, u32[]{:S(2)}, u32[]{:S(2)}) collective-permute-start(f16[960,128]{1,0:T(8,128)(2,1)S(1)} %fusion.8), channel_id=1, source_target_pairs={{0,56},{8,0},{16,8},{24,16},{32,24},{40,32},{48,40},{56,48},{1,57}... | collective-permute-start | bytes 737288 | tf_op jit(solution)/shard_map/ppermute | solution.py:465
  62.4 0.8 partial_sums.4
  63.2 3.6 %collective-permute-done.3 = f16[960,128]{1,0:T(8,128)(2,1)S(1)} collective-permute-done((f16[960,128]{1,0:T(8,128)(2,1)S(1)}, f16[960,128]{1,0:T(8,128)(2,1)S(1)}, u32[]{:S(2)}, u32[]{:S(2)}) %collective-permute-start.3) | collective-permute-done | bytes 245792 | tf_op jit(solution)/shard_map/ppermute | solution.py:465
  66.8 0.3 fusion.11
  67.2 0.3 fusion.14
  67.5 3.0 %collective-permute-start.6 = (f16[960,128]{1,0:T(8,128)(2,1)S(1)}, f16[960,128]{1,0:T(8,128)(2,1)S(1)}, u32[]{:S(2)}, u32[]{:S(2)}) collective-permute-start(f16[960,128]{1,0:T(8,128)(2,1)S(1)} %fusion.14), channel_id=1, source_target_pairs={{0,56},{8,0},{16,8},{24,16},{32,24},{40,32},{48,40},{56,48},{1,57}... | collective-permute-start | bytes 737288 | tf_op jit(solution)/shard_map/ppermute | solution.py:465
  70.5 1.8 %quarters.1 = (f32[960,128]{1,0:T(8,128)S(1)}, f32[960,128]{1,0:T(8,128)S(1)}, f32[960,128]{1,0:T(8,128)S(1)}) custom-call(s32[1]{0:T(128)} %bitcast.y_ref, f32[384,1280]{1,0:T(8,128)} %refs_2_.1, f32[384,1280]{1,0:T(8,128)} %refs_2_.1, f32[384,1280]{1,0:T(8,128)} %refs_2_.1, f32[384,1280]{1,0:T(8,128)} %refs_5_.1, f32[384,1280]{1,0:T(8,128)} %refs_5_.1, ...), custom_call_target="tpu_custom_call" | custom-call | flops 1000000 | bytes 3000000 | tf_op jit(solution)/shard_map/quarters/pallas_call | solution.py:288
  72.3 1.2 collective-permute-done.5
  73.5 0.3 collective-permute-done.6
  73.8 0.8 subtract_convert_fusion
  74.7 2.2 %collective-permute-start.7 = (bf16[960,128]{1,0:T(8,128)(2,1)S(1)}, bf16[960,128]{1,0:T(8,128)(2,1)S(1)}, u32[]{:S(2)}, u32[]{:S(2)}) collective-permute-start(bf16[960,128]{1,0:T(8,128)(2,1)S(1)} %get-tuple-element.74.refs_0_), channel_id=1, source_target_pairs={{0,8},{8,16},{16,24},{24,32},{32,40},{40,48},{48,56},{56,0},{1,9},... | collective-permute-start | bytes 737288 | tf_op jit(solution)/shard_map/ppermute | solution.py:465
  76.8 0.9 collective-permute-start.8
  77.7 1.8 %collective-permute-start.13 = (f16[960,128]{1,0:T(8,128)(2,1)S(1)}, f16[960,128]{1,0:T(8,128)(2,1)S(1)}, u32[]{:S(2)}, u32[]{:S(2)}) collective-permute-start(f16[960,128]{1,0:T(8,128)(2,1)S(1)} %get-tuple-element.89), channel_id=1, source_target_pairs={{0,64},{64,128},{128,192},{192,0},{1,65},{65,129},{129,193},{193,1... | collective-permute-start | bytes 737288 | tf_op jit(solution)/shard_map/ppermute | solution.py:465
  79.6 2.7 %collective-permute-start.12 = (f16[960,128]{1,0:T(8,128)(2,1)S(1)}, f16[960,128]{1,0:T(8,128)(2,1)S(1)}, u32[]{:S(2)}, u32[]{:S(2)}) collective-permute-start(f16[960,128]{1,0:T(8,128)(2,1)S(1)} %get-tuple-element.89), channel_id=1, source_target_pairs={{0,128},{64,192},{128,0},{192,64},{1,129},{65,193},{129,1},{193,65... | collective-permute-start | bytes 737288 | tf_op jit(solution)/shard_map/ppermute | solution.py:465
  82.2 0.8 collective-permute-start.11
  83.1 1.4 collective-permute-start.10
  84.5 2.0 %fetch.3.refs_2_ = bf16[32,192,128]{2,1,0:T(8,128)(2,1)} custom-call(s32[8,512]{1,0:T(8,128)S(1)} %get-tuple-element.51.ids_ref, bf16[960,128]{1,0:T(8,128)(2,1)S(1)} %get-tuple-element.74.refs_0_, bf16[960,128]{1,0:T(8,128)(2,1)S(1)} %collective-permute-done.8.refs_1_, bf16[960,128]{1,0:T(8,128)(2,1)S(1)} %collective-permute-done.7.refs_2_.refs_0_), custom_call_target="tpu_custom_call" | custom-call | tf_op jit(solution)/shard_map/fetch/pallas_call | solution.py:351
  86.6 3.6 %collective-permute-done.12 = f16[960,128]{1,0:T(8,128)(2,1)S(1)} collective-permute-done((f16[960,128]{1,0:T(8,128)(2,1)S(1)}, f16[960,128]{1,0:T(8,128)(2,1)S(1)}, u32[]{:S(2)}, u32[]{:S(2)}) %collective-permute-start.12) | collective-permute-done | bytes 245792 | tf_op jit(solution)/shard_map/ppermute | solution.py:465
  90.2 0.8 collective-permute-done.9.refs_1_
  91.0 1.8 %fetch.4 = bf16[32,192,128]{2,1,0:T(8,128)(2,1)} custom-call(s32[8,512]{1,0:T(8,128)S(1)} %get-tuple-element.51.ids_ref, bf16[960,128]{1,0:T(8,128)(2,1)S(1)} %collective-permute-done.10.refs_0_, bf16[960,128]{1,0:T(8,128)(2,1)S(1)} %collective-permute-done.9.refs_1_, bf16[32,192,128]{2,1,0:T(8,128)(2,1)} %fetch.3.refs_2_), custom_call_target="tpu_custom_call", output_to_operand_aliasing={{}: (3, {})} | custom-call | tf_op jit(solution)/shard_map/fetch/pallas_call | solution.py:351
  92.8 10.6 %all-to-all-start.2 = ((bf16[32,192,128]{2,1,0:T(8,128)(2,1)}), bf16[32,192,128]{2,1,0:T(8,128)(2,1)S(1)}, u32[]{:S(2)}, u32[]{:S(2)}) async-start(bf16[32,192,128]{2,1,0:T(8,128)(2,1)} %fetch.4), calls=%async_computation.2 | async-start | bytes 3145728 | tf_op jit(solution)/shard_map/all_to_all | solution.py:490
  103.5 2.7 %collective-permute-start.15 = (bf16[960,128]{1,0:T(8,128)(2,1)S(1)}, bf16[960,128]{1,0:T(8,128)(2,1)S(1)}, u32[]{:S(2)}, u32[]{:S(2)}) collective-permute-start(bf16[960,128]{1,0:T(8,128)(2,1)S(1)} %collective-permute-done.10.refs_0_), channel_id=1, source_target_pairs={{0,56},{8,0},{16,8},{24,16},{32,24},{40,32},{48,40},{56,48},{1,57}... | collective-permute-start | bytes 737288 | tf_op jit(solution)/shard_map/ppermute | solution.py:465
  106.2 5.9 %collective-permute-done.14.refs_2_ = bf16[960,128]{1,0:T(8,128)(2,1)S(1)} collective-permute-done((bf16[960,128]{1,0:T(8,128)(2,1)S(1)}, bf16[960,128]{1,0:T(8,128)(2,1)S(1)}, u32[]{:S(2)}, u32[]{:S(2)}) %collective-permute-start.14) | collective-permute-done | bytes 245792 | tf_op jit(solution)/shard_map/ppermute | solution.py:465
  112.0 7.6 %collective-permute-done.16.refs_3_ = bf16[960,128]{1,0:T(8,128)(2,1)S(1)} collective-permute-done((bf16[960,128]{1,0:T(8,128)(2,1)S(1)}, bf16[960,128]{1,0:T(8,128)(2,1)S(1)}, u32[]{:S(2)}, u32[]{:S(2)}) %collective-permute-start.16) | collective-permute-done | bytes 245792 | tf_op jit(solution)/shard_map/ppermute | solution.py:465
  119.6 2.1 %fetch.5 = bf16[32,128,128]{2,1,0:T(8,128)(2,1)} custom-call(s32[8,512]{1,0:T(8,128)S(1)} %get-tuple-element.51.ids_ref, bf16[960,128]{1,0:T(8,128)(2,1)S(1)} %collective-permute-done.7.refs_2_.refs_0_, bf16[960,128]{1,0:T(8,128)(2,1)S(1)} %collective-permute-done.15.refs_1_, bf16[960,128]{1,0:T(8,128)(2,1)S(1)} %collective-permute-done.14.refs_2_, ...), custom_call_target="tpu_custom_call" | custom-call | tf_op jit(solution)/shard_map/fetch/pallas_call | solution.py:351
  121.8 3.1 %all-to-all-done.2.g_ref = bf16[32,192,128]{2,1,0:T(8,128)(2,1)S(1)} async-done(((bf16[32,192,128]{2,1,0:T(8,128)(2,1)}), bf16[32,192,128]{2,1,0:T(8,128)(2,1)S(1)}, u32[]{:S(2)}, u32[]{:S(2)}) %all-to-all-start.2) | async-done | bytes 1572896 | tf_op jit(solution)/shard_map/all_to_all | solution.py:490
  124.9 5.8 %all-to-all-start.3 = ((bf16[32,128,128]{2,1,0:T(8,128)(2,1)}), bf16[32,128,128]{2,1,0:T(8,128)(2,1)S(1)}, u32[]{:S(2)}, u32[]{:S(2)}) async-start(bf16[32,128,128]{2,1,0:T(8,128)(2,1)} %fetch.5), calls=%async_computation.3 | async-start | bytes 2097152 | tf_op jit(solution)/shard_map/all_to_all | solution.py:490
  130.7 1.3 unpack.2.refs_0_
  132.3 6.3 %full_rows.1 = (f32[2,192,1280]{2,1,0:T(8,128)}, f32[2,192,1280]{2,1,0:T(8,128)}, f32[2,192,1280]{2,1,0:T(8,128)}) custom-call(s32[1]{0:T(128)} %bitcast.y_ref, f32[5,192,128]{2,1,0:T(8,128)S(1)} %bitcast.19, f32[5,192,128]{2,1,0:T(8,128)S(1)} %bitcast.20, f32[5,192,128]{2,1,0:T(8,128)S(1)} %bitcast.21, f32[5,192,128]{2,1,0:T(8,128)S(1)} %bitcast.22, ...), custom_call_target="tpu_custom_call" | custom-call | flops 10000000 | bytes 14000000 | tf_op jit(solution)/shard_map/full_rows/pallas_call | solution.py:443
  138.6 8.4 %all-to-all-done.3.g_ref = bf16[32,128,128]{2,1,0:T(8,128)(2,1)S(1)} async-done(((bf16[32,128,128]{2,1,0:T(8,128)(2,1)}), bf16[32,128,128]{2,1,0:T(8,128)(2,1)S(1)}, u32[]{:S(2)}, u32[]{:S(2)}) %all-to-all-start.3) | async-done | bytes 1048608 | tf_op jit(solution)/shard_map/all_to_all | solution.py:490
  147.0 1.1 unpack.3
  (23 shorter events, 1.0 us)
Async XLA Ops:
  2.9 24.9 %all-to-all-start = ((bf16[32,128,128]{2,1,0:T(8,128)(2,1)}), bf16[32,128,128]{2,1,0:T(8,128)(2,1)S(1)}, u32[]{:S(2)}, u32[]{:S(2)}) async-start(bf16[32,128,128]{2,1,0:T(8,128)(2,1)} %bitcast.34), calls=%async_computation | async-start | bytes 2097152 | tf_op jit(solution)/shard_map/all_to_all | solution.py:490
  27.9 27.6 %all-to-all-start.1 = ((bf16[32,208,128]{2,1,0:T(8,128)(2,1)}), bf16[32,208,128]{2,1,0:T(8,128)(2,1)S(1)}, u32[]{:S(2)}, u32[]{:S(2)}) async-start(bf16[32,208,128]{2,1,0:T(8,128)(2,1)} %bitcast.33), calls=%async_computation.1 | async-start | bytes 3407872 | tf_op jit(solution)/shard_map/all_to_all | solution.py:490
  33.9 11.7 %collective-permute-start = (f16[960,128]{1,0:T(8,128)(2,1)S(1)}, f16[960,128]{1,0:T(8,128)(2,1)S(1)}, u32[]{:S(2)}, u32[]{:S(2)}) collective-permute-start(f16[960,128]{1,0:T(8,128)(2,1)S(1)} %fusion), channel_id=1, source_target_pairs={{0,8},{8,16},{16,24},{24,32},{32,40},{40,48},{48,56},{56,0},{1,9},... | collective-permute-start | bytes 737288 | tf_op jit(solution)/shard_map/ppermute | solution.py:465
  35.8 10.2 %collective-permute-start.2 = (f16[960,128]{1,0:T(8,128)(2,1)S(1)}, f16[960,128]{1,0:T(8,128)(2,1)S(1)}, u32[]{:S(2)}, u32[]{:S(2)}) collective-permute-start(f16[960,128]{1,0:T(8,128)(2,1)S(1)} %fusion.4), channel_id=1, source_target_pairs={{0,56},{8,0},{16,8},{24,16},{32,24},{40,32},{48,40},{56,48},{1,57}... | collective-permute-start | bytes 737288 | tf_op jit(solution)/shard_map/ppermute | solution.py:465
  45.9 7.9 %collective-permute-start.1 = (f16[960,128]{1,0:T(8,128)(2,1)S(1)}, f16[960,128]{1,0:T(8,128)(2,1)S(1)}, u32[]{:S(2)}, u32[]{:S(2)}) collective-permute-start(f16[960,128]{1,0:T(8,128)(2,1)S(1)} %fusion.3), channel_id=1, source_target_pairs={{0,8},{8,16},{16,24},{24,32},{32,40},{40,48},{48,56},{56,0},{1,9},... | collective-permute-start | bytes 737288 | tf_op jit(solution)/shard_map/ppermute | solution.py:465
  56.4 10.4 %collective-permute-start.3 = (f16[960,128]{1,0:T(8,128)(2,1)S(1)}, f16[960,128]{1,0:T(8,128)(2,1)S(1)}, u32[]{:S(2)}, u32[]{:S(2)}) collective-permute-start(f16[960,128]{1,0:T(8,128)(2,1)S(1)} %fusion.7), channel_id=1, source_target_pairs={{0,8},{8,16},{16,24},{24,32},{32,40},{40,48},{48,56},{56,0},{1,9},... | collective-permute-start | bytes 737288 | tf_op jit(solution)/shard_map/ppermute | solution.py:465
  58.3 8.4 %collective-permute-start.4 = (f16[960,128]{1,0:T(8,128)(2,1)S(1)}, f16[960,128]{1,0:T(8,128)(2,1)S(1)}, u32[]{:S(2)}, u32[]{:S(2)}) collective-permute-start(f16[960,128]{1,0:T(8,128)(2,1)S(1)} %fusion.8), channel_id=1, source_target_pairs={{0,56},{8,0},{16,8},{24,16},{32,24},{40,32},{48,40},{56,48},{1,57}... | collective-permute-start | bytes 737288 | tf_op jit(solution)/shard_map/ppermute | solution.py:465
  67.1 6.4 %collective-permute-start.5 = (f16[960,128]{1,0:T(8,128)(2,1)S(1)}, f16[960,128]{1,0:T(8,128)(2,1)S(1)}, u32[]{:S(2)}, u32[]{:S(2)}) collective-permute-start(f16[960,128]{1,0:T(8,128)(2,1)S(1)} %fusion.11), channel_id=1, source_target_pairs={{0,8},{8,16},{16,24},{24,32},{32,40},{40,48},{48,56},{56,0},{1,9},... | collective-permute-start | bytes 737288 | tf_op jit(solution)/shard_map/ppermute | solution.py:465
  67.5 6.3 %collective-permute-start.6 = (f16[960,128]{1,0:T(8,128)(2,1)S(1)}, f16[960,128]{1,0:T(8,128)(2,1)S(1)}, u32[]{:S(2)}, u32[]{:S(2)}) collective-permute-start(f16[960,128]{1,0:T(8,128)(2,1)S(1)} %fusion.14), channel_id=1, source_target_pairs={{0,56},{8,0},{16,8},{24,16},{32,24},{40,32},{48,40},{56,48},{1,57}... | collective-permute-start | bytes 737288 | tf_op jit(solution)/shard_map/ppermute | solution.py:465
  74.7 8.4 %collective-permute-start.7 = (bf16[960,128]{1,0:T(8,128)(2,1)S(1)}, bf16[960,128]{1,0:T(8,128)(2,1)S(1)}, u32[]{:S(2)}, u32[]{:S(2)}) collective-permute-start(bf16[960,128]{1,0:T(8,128)(2,1)S(1)} %get-tuple-element.74.refs_0_), channel_id=1, source_target_pairs={{0,8},{8,16},{16,24},{24,32},{32,40},{40,48},{48,56},{56,0},{1,9},... | collective-permute-start | bytes 737288 | tf_op jit(solution)/shard_map/ppermute | solution.py:465
  76.8 6.2 %collective-permute-start.8 = (bf16[960,128]{1,0:T(8,128)(2,1)S(1)}, bf16[960,128]{1,0:T(8,128)(2,1)S(1)}, u32[]{:S(2)}, u32[]{:S(2)}) collective-permute-start(bf16[960,128]{1,0:T(8,128)(2,1)S(1)} %get-tuple-element.74.refs_0_), channel_id=1, source_target_pairs={{0,56},{8,0},{16,8},{24,16},{32,24},{40,32},{48,40},{56,48},{1,57}... | collective-permute-start | bytes 737288 | tf_op jit(solution)/shard_map/ppermute | solution.py:465
  77.7 8.8 %collective-permute-start.13 = (f16[960,128]{1,0:T(8,128)(2,1)S(1)}, f16[960,128]{1,0:T(8,128)(2,1)S(1)}, u32[]{:S(2)}, u32[]{:S(2)}) collective-permute-start(f16[960,128]{1,0:T(8,128)(2,1)S(1)} %get-tuple-element.89), channel_id=1, source_target_pairs={{0,64},{64,128},{128,192},{192,0},{1,65},{65,129},{129,193},{193,1... | collective-permute-start | bytes 737288 | tf_op jit(solution)/shard_map/ppermute | solution.py:465
  79.6 10.7 %collective-permute-start.12 = (f16[960,128]{1,0:T(8,128)(2,1)S(1)}, f16[960,128]{1,0:T(8,128)(2,1)S(1)}, u32[]{:S(2)}, u32[]{:S(2)}) collective-permute-start(f16[960,128]{1,0:T(8,128)(2,1)S(1)} %get-tuple-element.89), channel_id=1, source_target_pairs={{0,128},{64,192},{128,0},{192,64},{1,129},{65,193},{129,1},{193,65... | collective-permute-start | bytes 737288 | tf_op jit(solution)/shard_map/ppermute | solution.py:465
  82.2 8.0 %collective-permute-start.11 = (f16[960,128]{1,0:T(8,128)(2,1)S(1)}, f16[960,128]{1,0:T(8,128)(2,1)S(1)}, u32[]{:S(2)}, u32[]{:S(2)}) collective-permute-start(f16[960,128]{1,0:T(8,128)(2,1)S(1)} %get-tuple-element.89), channel_id=1, source_target_pairs={{0,192},{64,0},{128,64},{192,128},{1,193},{65,1},{129,65},{193,129... | collective-permute-start | bytes 737288 | tf_op jit(solution)/shard_map/ppermute | solution.py:465
  83.1 7.2 %collective-permute-start.10 = (bf16[960,128]{1,0:T(8,128)(2,1)S(1)}, bf16[960,128]{1,0:T(8,128)(2,1)S(1)}, u32[]{:S(2)}, u32[]{:S(2)}) collective-permute-start(bf16[960,128]{1,0:T(8,128)(2,1)S(1)} %collective-permute-done.8.refs_1_), channel_id=1, source_target_pairs={{0,56},{8,0},{16,8},{24,16},{32,24},{40,32},{48,40},{56,48},{1,57}... | collective-permute-start | bytes 737288 | tf_op jit(solution)/shard_map/ppermute | solution.py:465
  84.5 6.6 %collective-permute-start.9 = (bf16[960,128]{1,0:T(8,128)(2,1)S(1)}, bf16[960,128]{1,0:T(8,128)(2,1)S(1)}, u32[]{:S(2)}, u32[]{:S(2)}) collective-permute-start(bf16[960,128]{1,0:T(8,128)(2,1)S(1)} %collective-permute-done.7.refs_2_.refs_0_), channel_id=1, source_target_pairs={{0,8},{8,16},{16,24},{24,32},{32,40},{40,48},{48,56},{56,0},{1,9},... | collective-permute-start | bytes 737288 | tf_op jit(solution)/shard_map/ppermute | solution.py:465
  90.2 2.6 %copy-start = (f16[960,128]{1,0:T(8,128)(2,1)}, f16[960,128]{1,0:T(8,128)(2,1)S(1)}, u32[]{:S(2)}) copy-start(f16[960,128]{1,0:T(8,128)(2,1)S(1)} %collective-permute-done.11) | copy-start | bytes 737284
  92.8 32.1 %all-to-all-start.2 = ((bf16[32,192,128]{2,1,0:T(8,128)(2,1)}), bf16[32,192,128]{2,1,0:T(8,128)(2,1)S(1)}, u32[]{:S(2)}, u32[]{:S(2)}) async-start(bf16[32,192,128]{2,1,0:T(8,128)(2,1)} %fetch.4), calls=%async_computation.2 | async-start | bytes 3145728 | tf_op jit(solution)/shard_map/all_to_all | solution.py:490
  103.4 8.6 %collective-permute-start.14 = (bf16[960,128]{1,0:T(8,128)(2,1)S(1)}, bf16[960,128]{1,0:T(8,128)(2,1)S(1)}, u32[]{:S(2)}, u32[]{:S(2)}) collective-permute-start(bf16[960,128]{1,0:T(8,128)(2,1)S(1)} %collective-permute-done.9.refs_1_), channel_id=1, source_target_pairs={{0,8},{8,16},{16,24},{24,32},{32,40},{40,48},{48,56},{56,0},{1,9},... | collective-permute-start | bytes 737288 | tf_op jit(solution)/shard_map/ppermute | solution.py:465
  103.5 8.5 %collective-permute-start.15 = (bf16[960,128]{1,0:T(8,128)(2,1)S(1)}, bf16[960,128]{1,0:T(8,128)(2,1)S(1)}, u32[]{:S(2)}, u32[]{:S(2)}) collective-permute-start(bf16[960,128]{1,0:T(8,128)(2,1)S(1)} %collective-permute-done.10.refs_0_), channel_id=1, source_target_pairs={{0,56},{8,0},{16,8},{24,16},{32,24},{40,32},{48,40},{56,48},{1,57}... | collective-permute-start | bytes 737288 | tf_op jit(solution)/shard_map/ppermute | solution.py:465
  112.0 7.6 %collective-permute-start.16 = (bf16[960,128]{1,0:T(8,128)(2,1)S(1)}, bf16[960,128]{1,0:T(8,128)(2,1)S(1)}, u32[]{:S(2)}, u32[]{:S(2)}) collective-permute-start(bf16[960,128]{1,0:T(8,128)(2,1)S(1)} %collective-permute-done.14.refs_2_), channel_id=1, source_target_pairs={{0,8},{8,16},{16,24},{24,32},{32,40},{40,48},{48,56},{56,0},{1,9},... | collective-permute-start | bytes 737288 | tf_op jit(solution)/shard_map/ppermute | solution.py:465
  124.9 22.1 %all-to-all-start.3 = ((bf16[32,128,128]{2,1,0:T(8,128)(2,1)}), bf16[32,128,128]{2,1,0:T(8,128)(2,1)S(1)}, u32[]{:S(2)}, u32[]{:S(2)}) async-start(bf16[32,128,128]{2,1,0:T(8,128)(2,1)} %fetch.5), calls=%async_computation.3 | async-start | bytes 2097152 | tf_op jit(solution)/shard_map/all_to_all | solution.py:490
  130.7 1.4 copy-start.1

commit v6 on v4

--- a/solution.py
+++ b/solution.py
@@ -436,7 +436,7 @@
     own = adamw(*mine, summed)[0].astype(BF)
     grads = [shared] + [along(shared, "y", NY, -d) for d in range(1, NY)]
     tables = {0: own}
-    tables[7], tables[1] = both_ways(own, own)
+    tables[7], tables[1] = along(own, "z", NZ, 1), along(own, "z", NZ, -1)
     found = fetch(FIRST, (0, 1, 7), wanted, tables)
     tables[6], tables[2], *grads[1:] = lax.optimization_barrier(
         (along(tables[7], "z", NZ, 1), along(tables[1], "z", NZ, -1), *grads[1:])

time: 149 us -> 149 us (level)
    ppermute x17, starting transfers between devices: 27.4 us -> 29.5 us  [along(): lax.ppermute(value, axis, [(i, (i + step) % size) for i in range(size)])]
where the time goes in v6:
time: 149 us; the launch traced here: 148 us
  waiting for transfers between devices  61.4 us (41%)
  starting transfers between devices  57.9 us (39%)
  Pallas kernels  24 us (16%)
  other arithmetic  3.14 us (2%)
    ppermute x17, waiting for transfers between devices, along(): lax.ppermute(value, axis, [(i, (i + step) % size) for i in range(size)])  35.4 us
    ppermute x17, starting transfers between devices, along(): lax.ppermute(value, axis, [(i, (i + step) % size) for i in range(size)])  29.5 us
    all_to_all x4, starting transfers between devices, swap(): return lax.all_to_all(x, SLAB, split_axis=0, concat_axis=0, tiled=True)  28.3 us
    all_to_all x4, waiting for transfers between devices, swap(): return lax.all_to_all(x, SLAB, split_axis=0, concat_axis=0, tiled=True)  26 us
    pallas_call x1, Pallas kernels, full_rows(): pl.pallas_call(full_kernel, grid_spec=pltpu.PrefetchScalarGridSpec(num_sc...  6.33 us
    pallas_call x3, Pallas kernels, fetch(): pl.pallas_call(functools.partial(fetch_kernel, ks, some), in_specs=[vmem]...  5.91 us
    pallas_call x2, Pallas kernels, pack(): pl.pallas_call(functools.partial(pack_kernel, n, step, bool(ids)), grid_s...  5.08 us
  transfers between devices with their start and end apart: 21, of which 12 were waited for; matrix products, arithmetic and copies ran while one was open for 1% of the time, Pallas kernels for 12%

profile of v6, /device:TPU:1, one launch (start us, length us, event | category | flops | bytes accessed | tf_op | source)
XLA Modules:
  0.0 148.3 jit_solution(3660764810804281770)
XLA Ops:
  0.6 2.5 %pack.2 = bf16[8,4,128,128]{3,2,1,0:T(8,128)(2,1)} custom-call(s32[1]{0:T(128)} %bitcast.1.z_ref, bf16[8,8,16,1280]{3,2,1,0:T(8,128)(2,1)} %bitcast.22, bf16[8,8,16,1280]{3,2,1,0:T(8,128)(2,1)} %bitcast.23, bf16[8,8,16,1280]{3,2,1,0:T(8,128)(2,1)} %bitcast.24, s32[8,128]{1,0:T(8,128)} %bitcast.36, s32[8,128]{1,0:T(8,128)} %bitcast.37), custom_call_target="tpu_custom_call" | custom-call | bytes 2100000 | tf_op jit(solution)/shard_map/pack/pallas_call | solution.py:119
  3.1 8.6 %all-to-all-start = ((bf16[32,128,128]{2,1,0:T(8,128)(2,1)}), bf16[32,128,128]{2,1,0:T(8,128)(2,1)S(1)}, u32[]{:S(2)}, u32[]{:S(2)}) async-start(bf16[32,128,128]{2,1,0:T(8,128)(2,1)} %bitcast.35), calls=%async_computation | async-start | bytes 2097152 | tf_op jit(solution)/shard_map/all_to_all | solution.py:413
  11.7 2.6 %pack.3 = bf16[8,4,208,128]{3,2,1,0:T(8,128)(2,1)} custom-call(s32[1]{0:T(128)} %bitcast.1.z_ref, bf16[8,8,16,1280]{3,2,1,0:T(8,128)(2,1)} %bitcast.25, bf16[8,8,16,1280]{3,2,1,0:T(8,128)(2,1)} %bitcast.26, bf16[8,8,16,1280]{3,2,1,0:T(8,128)(2,1)} %bitcast.27, bf16[8,8,16,1280]{3,2,1,0:T(8,128)(2,1)} %bitcast.28, bf16[8,8,16,1280]{3,2,1,0:T(8,128)(2,1)} %bitcast.29), custom_call_target="tpu_custom_call" | custom-call | bytes 3500000 | tf_op jit(solution)/shard_map/pack/pallas_call | solution.py:119
  14.3 13.7 %all-to-all-done.refs_0_ = bf16[32,128,128]{2,1,0:T(8,128)(2,1)S(1)} async-done(((bf16[32,128,128]{2,1,0:T(8,128)(2,1)}), bf16[32,128,128]{2,1,0:T(8,128)(2,1)S(1)}, u32[]{:S(2)}, u32[]{:S(2)}) %all-to-all-start) | async-done | bytes 1048608 | tf_op jit(solution)/shard_map/all_to_all | solution.py:413
  28.0 4.7 %all-to-all-start.1 = ((bf16[32,208,128]{2,1,0:T(8,128)(2,1)}), bf16[32,208,128]{2,1,0:T(8,128)(2,1)S(1)}, u32[]{:S(2)}, u32[]{:S(2)}) async-start(bf16[32,208,128]{2,1,0:T(8,128)(2,1)} %bitcast.34), calls=%async_computation.1 | async-start | bytes 3407872 | tf_op jit(solution)/shard_map/all_to_all | solution.py:413
  32.7 1.1 partial_sums.3
  33.8 0.2 fusion
  34.0 1.7 %collective-permute-start = (f16[960,128]{1,0:T(8,128)(2,1)S(1)}, f16[960,128]{1,0:T(8,128)(2,1)S(1)}, u32[]{:S(2)}, u32[]{:S(2)}) collective-permute-start(f16[960,128]{1,0:T(8,128)(2,1)S(1)} %fusion), channel_id=1, source_target_pairs={{0,8},{8,16},{16,24},{24,32},{32,40},{40,48},{48,56},{56,0},{1,9},... | collective-permute-start | bytes 737288 | tf_op jit(solution)/shard_map/ppermute | solution.py:388
  36.0 4.0 %collective-permute-start.2 = (f16[960,128]{1,0:T(8,128)(2,1)S(1)}, f16[960,128]{1,0:T(8,128)(2,1)S(1)}, u32[]{:S(2)}, u32[]{:S(2)}) collective-permute-start(f16[960,128]{1,0:T(8,128)(2,1)S(1)} %fusion.4), channel_id=1, source_target_pairs={{0,56},{8,0},{16,8},{24,16},{32,24},{40,32},{48,40},{56,48},{1,57}... | collective-permute-start | bytes 737288 | tf_op jit(solution)/shard_map/ppermute | solution.py:388
  40.0 5.7 %collective-permute-done = f16[960,128]{1,0:T(8,128)(2,1)S(1)} collective-permute-done((f16[960,128]{1,0:T(8,128)(2,1)S(1)}, f16[960,128]{1,0:T(8,128)(2,1)S(1)}, u32[]{:S(2)}, u32[]{:S(2)}) %collective-permute-start) | collective-permute-done | bytes 245792 | tf_op jit(solution)/shard_map/ppermute | solution.py:388
  45.8 0.3 fusion.3
  46.2 7.8 %collective-permute-done.1 = f16[960,128]{1,0:T(8,128)(2,1)S(1)} collective-permute-done((f16[960,128]{1,0:T(8,128)(2,1)S(1)}, f16[960,128]{1,0:T(8,128)(2,1)S(1)}, u32[]{:S(2)}, u32[]{:S(2)}) %collective-permute-start.1) | collective-permute-done | bytes 245792 | tf_op jit(solution)/shard_map/ppermute | solution.py:388
  54.1 1.5 %all-to-all-done.1.refs_0_ = bf16[32,208,128]{2,1,0:T(8,128)(2,1)S(1)} async-done(((bf16[32,208,128]{2,1,0:T(8,128)(2,1)}), bf16[32,208,128]{2,1,0:T(8,128)(2,1)S(1)}, u32[]{:S(2)}, u32[]{:S(2)}) %all-to-all-start.1) | async-done | bytes 1703968 | tf_op jit(solution)/shard_map/all_to_all | solution.py:413
  55.7 0.6 partial_sums.5
  56.3 0.3 fusion.7
  56.5 1.7 %collective-permute-start.3 = (f16[960,128]{1,0:T(8,128)(2,1)S(1)}, f16[960,128]{1,0:T(8,128)(2,1)S(1)}, u32[]{:S(2)}, u32[]{:S(2)}) collective-permute-start(f16[960,128]{1,0:T(8,128)(2,1)S(1)} %fusion.7), channel_id=1, source_target_pairs={{0,8},{8,16},{16,24},{24,32},{32,40},{40,48},{48,56},{56,0},{1,9},... | collective-permute-start | bytes 737288 | tf_op jit(solution)/shard_map/ppermute | solution.py:388
  58.2 0.3 fusion.8
  58.5 4.0 %collective-permute-start.4 = (f16[960,128]{1,0:T(8,128)(2,1)S(1)}, f16[960,128]{1,0:T(8,128)(2,1)S(1)}, u32[]{:S(2)}, u32[]{:S(2)}) collective-permute-start(f16[960,128]{1,0:T(8,128)(2,1)S(1)} %fusion.8), channel_id=1, source_target_pairs={{0,56},{8,0},{16,8},{24,16},{32,24},{40,32},{48,40},{56,48},{1,57}... | collective-permute-start | bytes 737288 | tf_op jit(solution)/shard_map/ppermute | solution.py:388
  62.5 0.8 partial_sums.4
  63.4 3.6 %collective-permute-done.3 = f16[960,128]{1,0:T(8,128)(2,1)S(1)} collective-permute-done((f16[960,128]{1,0:T(8,128)(2,1)S(1)}, f16[960,128]{1,0:T(8,128)(2,1)S(1)}, u32[]{:S(2)}, u32[]{:S(2)}) %collective-permute-start.3) | collective-permute-done | bytes 245792 | tf_op jit(solution)/shard_map/ppermute | solution.py:388
  66.9 0.3 fusion.11
  67.3 0.3 fusion.14
  67.6 2.8 %collective-permute-start.6 = (f16[960,128]{1,0:T(8,128)(2,1)S(1)}, f16[960,128]{1,0:T(8,128)(2,1)S(1)}, u32[]{:S(2)}, u32[]{:S(2)}) collective-permute-start(f16[960,128]{1,0:T(8,128)(2,1)S(1)} %fusion.14), channel_id=1, source_target_pairs={{0,56},{8,0},{16,8},{24,16},{32,24},{40,32},{48,40},{56,48},{1,57}... | collective-permute-start | bytes 737288 | tf_op jit(solution)/shard_map/ppermute | solution.py:388
  70.5 1.8 %quarters.1 = (f32[960,128]{1,0:T(8,128)S(1)}, f32[960,128]{1,0:T(8,128)S(1)}, f32[960,128]{1,0:T(8,128)S(1)}) custom-call(s32[1]{0:T(128)} %bitcast.y_ref, f32[384,1280]{1,0:T(8,128)} %refs_2_.1, f32[384,1280]{1,0:T(8,128)} %refs_2_.1, f32[384,1280]{1,0:T(8,128)} %refs_2_.1, f32[384,1280]{1,0:T(8,128)} %refs_5_.1, f32[384,1280]{1,0:T(8,128)} %refs_5_.1, ...), custom_call_target="tpu_custom_call" | custom-call | flops 1000000 | bytes 3000000 | tf_op jit(solution)/shard_map/quarters/pallas_call | solution.py:211
  72.3 1.3 collective-permute-done.5
  73.6 0.8 subtract_convert_fusion
  74.5 3.3 %collective-permute-start.9 = (bf16[960,128]{1,0:T(8,128)(2,1)S(1)}, bf16[960,128]{1,0:T(8,128)(2,1)S(1)}, u32[]{:S(2)}, u32[]{:S(2)}) collective-permute-start(bf16[960,128]{1,0:T(8,128)(2,1)S(1)} %get-tuple-element.90.refs_0_), channel_id=1, source_target_pairs={{0,56},{8,0},{16,8},{24,16},{32,24},{40,32},{48,40},{56,48},{1,57}... | collective-permute-start | bytes 737288 | tf_op jit(solution)/shard_map/ppermute | solution.py:388
  77.8 1.8 %collective-permute-start.13 = (f16[960,128]{1,0:T(8,128)(2,1)S(1)}, f16[960,128]{1,0:T(8,128)(2,1)S(1)}, u32[]{:S(2)}, u32[]{:S(2)}) collective-permute-start(f16[960,128]{1,0:T(8,128)(2,1)S(1)} %get-tuple-element.81), channel_id=1, source_target_pairs={{0,64},{64,128},{128,192},{192,0},{1,65},{65,129},{129,193},{193,1... | collective-permute-start | bytes 737288 | tf_op jit(solution)/shard_map/ppermute | solution.py:388
  79.6 2.6 %collective-permute-start.12 = (f16[960,128]{1,0:T(8,128)(2,1)S(1)}, f16[960,128]{1,0:T(8,128)(2,1)S(1)}, u32[]{:S(2)}, u32[]{:S(2)}) collective-permute-start(f16[960,128]{1,0:T(8,128)(2,1)S(1)} %get-tuple-element.81), channel_id=1, source_target_pairs={{0,128},{64,192},{128,0},{192,64},{1,129},{65,193},{129,1},{193,65... | collective-permute-start | bytes 737288 | tf_op jit(solution)/shard_map/ppermute | solution.py:388
  82.3 0.8 collective-permute-start.11
  83.1 2.7 %collective-permute-start.10 = (bf16[960,128]{1,0:T(8,128)(2,1)S(1)}, bf16[960,128]{1,0:T(8,128)(2,1)S(1)}, u32[]{:S(2)}, u32[]{:S(2)}) collective-permute-start(bf16[960,128]{1,0:T(8,128)(2,1)S(1)} %collective-permute-done.9.refs_1_), channel_id=1, source_target_pairs={{0,56},{8,0},{16,8},{24,16},{32,24},{40,32},{48,40},{56,48},{1,57}... | collective-permute-start | bytes 737288 | tf_op jit(solution)/shard_map/ppermute | solution.py:388
  85.8 2.0 %fetch.3.refs_2_ = bf16[32,192,128]{2,1,0:T(8,128)(2,1)} custom-call(s32[8,512]{1,0:T(8,128)S(1)} %get-tuple-element.47.ids_ref, bf16[960,128]{1,0:T(8,128)(2,1)S(1)} %get-tuple-element.90.refs_0_, bf16[960,128]{1,0:T(8,128)(2,1)S(1)} %collective-permute-done.9.refs_1_, bf16[960,128]{1,0:T(8,128)(2,1)S(1)} %collective-permute-done.7.refs_2_.refs_0_), custom_call_target="tpu_custom_call" | custom-call | tf_op jit(solution)/shard_map/fetch/pallas_call | solution.py:274
  87.9 2.4 %collective-permute-done.12 = f16[960,128]{1,0:T(8,128)(2,1)S(1)} collective-permute-done((f16[960,128]{1,0:T(8,128)(2,1)S(1)}, f16[960,128]{1,0:T(8,128)(2,1)S(1)}, u32[]{:S(2)}, u32[]{:S(2)}) %collective-permute-start.12) | collective-permute-done | bytes 245792 | tf_op jit(solution)/shard_map/ppermute | solution.py:388
  90.3 2.1 %collective-permute-done.8.refs_1_ = bf16[960,128]{1,0:T(8,128)(2,1)S(1)} collective-permute-done((bf16[960,128]{1,0:T(8,128)(2,1)S(1)}, bf16[960,128]{1,0:T(8,128)(2,1)S(1)}, u32[]{:S(2)}, u32[]{:S(2)}) %collective-permute-start.8) | collective-permute-done | bytes 245792 | tf_op jit(solution)/shard_map/ppermute | solution.py:388
  92.4 1.8 %fetch.4 = bf16[32,192,128]{2,1,0:T(8,128)(2,1)} custom-call(s32[8,512]{1,0:T(8,128)S(1)} %get-tuple-element.47.ids_ref, bf16[960,128]{1,0:T(8,128)(2,1)S(1)} %collective-permute-done.10.refs_0_, bf16[960,128]{1,0:T(8,128)(2,1)S(1)} %collective-permute-done.8.refs_1_, bf16[32,192,128]{2,1,0:T(8,128)(2,1)} %fetch.3.refs_2_), custom_call_target="tpu_custom_call", output_to_operand_aliasing={{}: (3, {})} | custom-call | tf_op jit(solution)/shard_map/fetch/pallas_call | solution.py:274
  94.2 9.3 %all-to-all-start.2 = ((bf16[32,192,128]{2,1,0:T(8,128)(2,1)}), bf16[32,192,128]{2,1,0:T(8,128)(2,1)S(1)}, u32[]{:S(2)}, u32[]{:S(2)}) async-start(bf16[32,192,128]{2,1,0:T(8,128)(2,1)} %fetch.4), calls=%async_computation.2 | async-start | bytes 3145728 | tf_op jit(solution)/shard_map/all_to_all | solution.py:413
  103.6 2.7 %collective-permute-start.15 = (bf16[960,128]{1,0:T(8,128)(2,1)S(1)}, bf16[960,128]{1,0:T(8,128)(2,1)S(1)}, u32[]{:S(2)}, u32[]{:S(2)}) collective-permute-start(bf16[960,128]{1,0:T(8,128)(2,1)S(1)} %collective-permute-done.10.refs_0_), channel_id=1, source_target_pairs={{0,56},{8,0},{16,8},{24,16},{32,24},{40,32},{48,40},{56,48},{1,57}... | collective-permute-start | bytes 737288 | tf_op jit(solution)/shard_map/ppermute | solution.py:388
  106.2 5.9 %collective-permute-done.14.refs_2_ = bf16[960,128]{1,0:T(8,128)(2,1)S(1)} collective-permute-done((bf16[960,128]{1,0:T(8,128)(2,1)S(1)}, bf16[960,128]{1,0:T(8,128)(2,1)S(1)}, u32[]{:S(2)}, u32[]{:S(2)}) %collective-permute-start.14) | collective-permute-done | bytes 245792 | tf_op jit(solution)/shard_map/ppermute | solution.py:388
  112.1 1.0 collective-permute-start.16
  113.1 6.6 %collective-permute-done.16.refs_3_ = bf16[960,128]{1,0:T(8,128)(2,1)S(1)} collective-permute-done((bf16[960,128]{1,0:T(8,128)(2,1)S(1)}, bf16[960,128]{1,0:T(8,128)(2,1)S(1)}, u32[]{:S(2)}, u32[]{:S(2)}) %collective-permute-start.16) | collective-permute-done | bytes 245792 | tf_op jit(solution)/shard_map/ppermute | solution.py:388
  119.7 2.1 %fetch.5 = bf16[32,128,128]{2,1,0:T(8,128)(2,1)} custom-call(s32[8,512]{1,0:T(8,128)S(1)} %get-tuple-element.47.ids_ref, bf16[960,128]{1,0:T(8,128)(2,1)S(1)} %collective-permute-done.7.refs_2_.refs_0_, bf16[960,128]{1,0:T(8,128)(2,1)S(1)} %collective-permute-done.15.refs_1_, bf16[960,128]{1,0:T(8,128)(2,1)S(1)} %collective-permute-done.14.refs_2_, ...), custom_call_target="tpu_custom_call" | custom-call | tf_op jit(solution)/shard_map/fetch/pallas_call | solution.py:274
  121.8 3.1 %all-to-all-done.2.g_ref = bf16[32,192,128]{2,1,0:T(8,128)(2,1)S(1)} async-done(((bf16[32,192,128]{2,1,0:T(8,128)(2,1)}), bf16[32,192,128]{2,1,0:T(8,128)(2,1)S(1)}, u32[]{:S(2)}, u32[]{:S(2)}) %all-to-all-start.2) | async-done | bytes 1572896 | tf_op jit(solution)/shard_map/all_to_all | solution.py:413
  125.0 5.7 %all-to-all-start.3 = ((bf16[32,128,128]{2,1,0:T(8,128)(2,1)}), bf16[32,128,128]{2,1,0:T(8,128)(2,1)S(1)}, u32[]{:S(2)}, u32[]{:S(2)}) async-start(bf16[32,128,128]{2,1,0:T(8,128)(2,1)} %fetch.5), calls=%async_computation.3 | async-start | bytes 2097152 | tf_op jit(solution)/shard_map/all_to_all | solution.py:413
  130.7 1.3 unpack.2.refs_0_
  132.3 0.7 copy-done.1
  133.1 6.3 %full_rows.1 = (f32[2,192,1280]{2,1,0:T(8,128)}, f32[2,192,1280]{2,1,0:T(8,128)}, f32[2,192,1280]{2,1,0:T(8,128)}) custom-call(s32[1]{0:T(128)} %bitcast.y_ref, f32[5,192,128]{2,1,0:T(8,128)S(1)} %bitcast.18, f32[5,192,128]{2,1,0:T(8,128)S(1)} %bitcast.19, f32[5,192,128]{2,1,0:T(8,128)S(1)} %bitcast.20, f32[5,192,128]{2,1,0:T(8,128)S(1)} %bitcast.21, ...), custom_call_target="tpu_custom_call" | custom-call | flops 10000000 | bytes 14000000 | tf_op jit(solution)/shard_map/full_rows/pallas_call | solution.py:366
  139.4 7.7 %all-to-all-done.3.g_ref = bf16[32,128,128]{2,1,0:T(8,128)(2,1)S(1)} async-done(((bf16[32,128,128]{2,1,0:T(8,128)(2,1)}), bf16[32,128,128]{2,1,0:T(8,128)(2,1)S(1)}, u32[]{:S(2)}, u32[]{:S(2)}) %all-to-all-start.3) | async-done | bytes 1048608 | tf_op jit(solution)/shard_map/all_to_all | solution.py:413
  147.0 1.1 unpack.3
  (31 shorter events, 0.9 us)
Async XLA Ops:
  3.1 24.9 %all-to-all-start = ((bf16[32,128,128]{2,1,0:T(8,128)(2,1)}), bf16[32,128,128]{2,1,0:T(8,128)(2,1)S(1)}, u32[]{:S(2)}, u32[]{:S(2)}) async-start(bf16[32,128,128]{2,1,0:T(8,128)(2,1)} %bitcast.35), calls=%async_computation | async-start | bytes 2097152 | tf_op jit(solution)/shard_map/all_to_all | solution.py:413
  28.0 27.7 %all-to-all-start.1 = ((bf16[32,208,128]{2,1,0:T(8,128)(2,1)}), bf16[32,208,128]{2,1,0:T(8,128)(2,1)S(1)}, u32[]{:S(2)}, u32[]{:S(2)}) async-start(bf16[32,208,128]{2,1,0:T(8,128)(2,1)} %bitcast.34), calls=%async_computation.1 | async-start | bytes 3407872 | tf_op jit(solution)/shard_map/all_to_all | solution.py:413
  34.0 11.7 %collective-permute-start = (f16[960,128]{1,0:T(8,128)(2,1)S(1)}, f16[960,128]{1,0:T(8,128)(2,1)S(1)}, u32[]{:S(2)}, u32[]{:S(2)}) collective-permute-start(f16[960,128]{1,0:T(8,128)(2,1)S(1)} %fusion), channel_id=1, source_target_pairs={{0,8},{8,16},{16,24},{24,32},{32,40},{40,48},{48,56},{56,0},{1,9},... | collective-permute-start | bytes 737288 | tf_op jit(solution)/shard_map/ppermute | solution.py:388
  36.0 10.2 %collective-permute-start.2 = (f16[960,128]{1,0:T(8,128)(2,1)S(1)}, f16[960,128]{1,0:T(8,128)(2,1)S(1)}, u32[]{:S(2)}, u32[]{:S(2)}) collective-permute-start(f16[960,128]{1,0:T(8,128)(2,1)S(1)} %fusion.4), channel_id=1, source_target_pairs={{0,56},{8,0},{16,8},{24,16},{32,24},{40,32},{48,40},{56,48},{1,57}... | collective-permute-start | bytes 737288 | tf_op jit(solution)/shard_map/ppermute | solution.py:388
  46.1 7.9 %collective-permute-start.1 = (f16[960,128]{1,0:T(8,128)(2,1)S(1)}, f16[960,128]{1,0:T(8,128)(2,1)S(1)}, u32[]{:S(2)}, u32[]{:S(2)}) collective-permute-start(f16[960,128]{1,0:T(8,128)(2,1)S(1)} %fusion.3), channel_id=1, source_target_pairs={{0,8},{8,16},{16,24},{24,32},{32,40},{40,48},{48,56},{56,0},{1,9},... | collective-permute-start | bytes 737288 | tf_op jit(solution)/shard_map/ppermute | solution.py:388
  56.5 10.4 %collective-permute-start.3 = (f16[960,128]{1,0:T(8,128)(2,1)S(1)}, f16[960,128]{1,0:T(8,128)(2,1)S(1)}, u32[]{:S(2)}, u32[]{:S(2)}) collective-permute-start(f16[960,128]{1,0:T(8,128)(2,1)S(1)} %fusion.7), channel_id=1, source_target_pairs={{0,8},{8,16},{16,24},{24,32},{32,40},{40,48},{48,56},{56,0},{1,9},... | collective-permute-start | bytes 737288 | tf_op jit(solution)/shard_map/ppermute | solution.py:388
  58.5 8.4 %collective-permute-start.4 = (f16[960,128]{1,0:T(8,128)(2,1)S(1)}, f16[960,128]{1,0:T(8,128)(2,1)S(1)}, u32[]{:S(2)}, u32[]{:S(2)}) collective-permute-start(f16[960,128]{1,0:T(8,128)(2,1)S(1)} %fusion.8), channel_id=1, source_target_pairs={{0,56},{8,0},{16,8},{24,16},{32,24},{40,32},{48,40},{56,48},{1,57}... | collective-permute-start | bytes 737288 | tf_op jit(solution)/shard_map/ppermute | solution.py:388
  67.2 6.4 %collective-permute-start.5 = (f16[960,128]{1,0:T(8,128)(2,1)S(1)}, f16[960,128]{1,0:T(8,128)(2,1)S(1)}, u32[]{:S(2)}, u32[]{:S(2)}) collective-permute-start(f16[960,128]{1,0:T(8,128)(2,1)S(1)} %fusion.11), channel_id=1, source_target_pairs={{0,8},{8,16},{16,24},{24,32},{32,40},{40,48},{48,56},{56,0},{1,9},... | collective-permute-start | bytes 737288 | tf_op jit(solution)/shard_map/ppermute | solution.py:388
  67.6 6.0 %collective-permute-start.6 = (f16[960,128]{1,0:T(8,128)(2,1)S(1)}, f16[960,128]{1,0:T(8,128)(2,1)S(1)}, u32[]{:S(2)}, u32[]{:S(2)}) collective-permute-start(f16[960,128]{1,0:T(8,128)(2,1)S(1)} %fusion.14), channel_id=1, source_target_pairs={{0,56},{8,0},{16,8},{24,16},{32,24},{40,32},{48,40},{56,48},{1,57}... | collective-permute-start | bytes 737288 | tf_op jit(solution)/shard_map/ppermute | solution.py:388
  74.5 8.7 %collective-permute-start.9 = (bf16[960,128]{1,0:T(8,128)(2,1)S(1)}, bf16[960,128]{1,0:T(8,128)(2,1)S(1)}, u32[]{:S(2)}, u32[]{:S(2)}) collective-permute-start(bf16[960,128]{1,0:T(8,128)(2,1)S(1)} %get-tuple-element.90.refs_0_), channel_id=1, source_target_pairs={{0,56},{8,0},{16,8},{24,16},{32,24},{40,32},{48,40},{56,48},{1,57}... | collective-permute-start | bytes 737288 | tf_op jit(solution)/shard_map/ppermute | solution.py:388
  77.8 8.0 %collective-permute-start.7 = (bf16[960,128]{1,0:T(8,128)(2,1)S(1)}, bf16[960,128]{1,0:T(8,128)(2,1)S(1)}, u32[]{:S(2)}, u32[]{:S(2)}) collective-permute-start(bf16[960,128]{1,0:T(8,128)(2,1)S(1)} %get-tuple-element.90.refs_0_), channel_id=1, source_target_pairs={{0,8},{8,16},{16,24},{24,32},{32,40},{40,48},{48,56},{56,0},{1,9},... | collective-permute-start | bytes 737288 | tf_op jit(solution)/shard_map/ppermute | solution.py:388
  77.8 10.0 %collective-permute-start.13 = (f16[960,128]{1,0:T(8,128)(2,1)S(1)}, f16[960,128]{1,0:T(8,128)(2,1)S(1)}, u32[]{:S(2)}, u32[]{:S(2)}) collective-permute-start(f16[960,128]{1,0:T(8,128)(2,1)S(1)} %get-tuple-element.81), channel_id=1, source_target_pairs={{0,64},{64,128},{128,192},{192,0},{1,65},{65,129},{129,193},{193,1... | collective-permute-start | bytes 737288 | tf_op jit(solution)/shard_map/ppermute | solution.py:388
  79.6 10.6 %collective-permute-start.12 = (f16[960,128]{1,0:T(8,128)(2,1)S(1)}, f16[960,128]{1,0:T(8,128)(2,1)S(1)}, u32[]{:S(2)}, u32[]{:S(2)}) collective-permute-start(f16[960,128]{1,0:T(8,128)(2,1)S(1)} %get-tuple-element.81), channel_id=1, source_target_pairs={{0,128},{64,192},{128,0},{192,64},{1,129},{65,193},{129,1},{193,65... | collective-permute-start | bytes 737288 | tf_op jit(solution)/shard_map/ppermute | solution.py:388
  82.3 8.0 %collective-permute-start.11 = (f16[960,128]{1,0:T(8,128)(2,1)S(1)}, f16[960,128]{1,0:T(8,128)(2,1)S(1)}, u32[]{:S(2)}, u32[]{:S(2)}) collective-permute-start(f16[960,128]{1,0:T(8,128)(2,1)S(1)} %get-tuple-element.81), channel_id=1, source_target_pairs={{0,192},{64,0},{128,64},{192,128},{1,193},{65,1},{129,65},{193,129... | collective-permute-start | bytes 737288 | tf_op jit(solution)/shard_map/ppermute | solution.py:388
  83.1 7.1 %collective-permute-start.10 = (bf16[960,128]{1,0:T(8,128)(2,1)S(1)}, bf16[960,128]{1,0:T(8,128)(2,1)S(1)}, u32[]{:S(2)}, u32[]{:S(2)}) collective-permute-start(bf16[960,128]{1,0:T(8,128)(2,1)S(1)} %collective-permute-done.9.refs_1_), channel_id=1, source_target_pairs={{0,56},{8,0},{16,8},{24,16},{32,24},{40,32},{48,40},{56,48},{1,57}... | collective-permute-start | bytes 737288 | tf_op jit(solution)/shard_map/ppermute | solution.py:388
  85.8 6.6 %collective-permute-start.8 = (bf16[960,128]{1,0:T(8,128)(2,1)S(1)}, bf16[960,128]{1,0:T(8,128)(2,1)S(1)}, u32[]{:S(2)}, u32[]{:S(2)}) collective-permute-start(bf16[960,128]{1,0:T(8,128)(2,1)S(1)} %collective-permute-done.7.refs_2_.refs_0_), channel_id=1, source_target_pairs={{0,8},{8,16},{16,24},{24,32},{32,40},{40,48},{48,56},{56,0},{1,9},... | collective-permute-start | bytes 737288 | tf_op jit(solution)/shard_map/ppermute | solution.py:388
  87.8 6.3 %copy-start = (f16[960,128]{1,0:T(8,128)(2,1)}, f16[960,128]{1,0:T(8,128)(2,1)S(1)}, u32[]{:S(2)}) copy-start(f16[960,128]{1,0:T(8,128)(2,1)S(1)} %collective-permute-done.13) | copy-start | bytes 737284
  90.3 3.9 %copy-start.2 = (f16[960,128]{1,0:T(8,128)(2,1)}, f16[960,128]{1,0:T(8,128)(2,1)S(1)}, u32[]{:S(2)}) copy-start(f16[960,128]{1,0:T(8,128)(2,1)S(1)} %collective-permute-done.12) | copy-start | bytes 737284
  90.3 2.1 %copy-start.4 = (f16[960,128]{1,0:T(8,128)(2,1)}, f16[960,128]{1,0:T(8,128)(2,1)S(1)}, u32[]{:S(2)}) copy-start(f16[960,128]{1,0:T(8,128)(2,1)S(1)} %collective-permute-done.11) | copy-start | bytes 737284
  94.2 30.8 %all-to-all-start.2 = ((bf16[32,192,128]{2,1,0:T(8,128)(2,1)}), bf16[32,192,128]{2,1,0:T(8,128)(2,1)S(1)}, u32[]{:S(2)}, u32[]{:S(2)}) async-start(bf16[32,192,128]{2,1,0:T(8,128)(2,1)} %fetch.4), calls=%async_computation.2 | async-start | bytes 3145728 | tf_op jit(solution)/shard_map/all_to_all | solution.py:413
  103.5 8.6 %collective-permute-start.14 = (bf16[960,128]{1,0:T(8,128)(2,1)S(1)}, bf16[960,128]{1,0:T(8,128)(2,1)S(1)}, u32[]{:S(2)}, u32[]{:S(2)}) collective-permute-start(bf16[960,128]{1,0:T(8,128)(2,1)S(1)} %collective-permute-done.8.refs_1_), channel_id=1, source_target_pairs={{0,8},{8,16},{16,24},{24,32},{32,40},{40,48},{48,56},{56,0},{1,9},... | collective-permute-start | bytes 737288 | tf_op jit(solution)/shard_map/ppermute | solution.py:388
  103.6 8.5 %collective-permute-start.15 = (bf16[960,128]{1,0:T(8,128)(2,1)S(1)}, bf16[960,128]{1,0:T(8,128)(2,1)S(1)}, u32[]{:S(2)}, u32[]{:S(2)}) collective-permute-start(bf16[960,128]{1,0:T(8,128)(2,1)S(1)} %collective-permute-done.10.refs_0_), channel_id=1, source_target_pairs={{0,56},{8,0},{16,8},{24,16},{32,24},{40,32},{48,40},{56,48},{1,57}... | collective-permute-start | bytes 737288 | tf_op jit(solution)/shard_map/ppermute | solution.py:388
  112.1 7.6 %collective-permute-start.16 = (bf16[960,128]{1,0:T(8,128)(2,1)S(1)}, bf16[960,128]{1,0:T(8,128)(2,1)S(1)}, u32[]{:S(2)}, u32[]{:S(2)}) collective-permute-start(bf16[960,128]{1,0:T(8,128)(2,1)S(1)} %collective-permute-done.14.refs_2_), channel_id=1, source_target_pairs={{0,8},{8,16},{16,24},{24,32},{32,40},{40,48},{48,56},{56,0},{1,9},... | collective-permute-start | bytes 737288 | tf_op jit(solution)/shard_map/ppermute | solution.py:388
  125.0 22.1 %all-to-all-start.3 = ((bf16[32,128,128]{2,1,0:T(8,128)(2,1)}), bf16[32,128,128]{2,1,0:T(8,128)(2,1)S(1)}, u32[]{:S(2)}, u32[]{:S(2)}) async-start(bf16[32,128,128]{2,1,0:T(8,128)(2,1)} %fetch.5), calls=%async_computation.3 | async-start | bytes 2097152 | tf_op jit(solution)/shard_map/all_to_all | solution.py:413
  130.7 1.4 copy-start.5
  130.7 1.5 %copy-start.3 = (f16[960,128]{1,0:T(8,128)(2,1)S(1)}, f16[960,128]{1,0:T(8,128)(2,1)}, u32[]{:S(2)}) copy-start(f16[960,128]{1,0:T(8,128)(2,1)} %copy-done.2) | copy-start | bytes 737284
  132.0 0.9 copy-start.1
